TPU v7x, 32 devices: a whole 2x2x4 slice. The times are simulated.
32 devices in a mesh: section: 4 (over z), dp: 8 (over y, x, core).
Axes of the slice: x: 2, y: 2, z: 4, core: 2. Of those that a mesh axis runs over, the one named last changes fastest.
Arguments:
- tokens: float32 [16384, 768], P('dp'), may hold values from -6 to 6
- absorbed: int32 [16384], P('dp'), may hold values from 0 to 1, as said below
- timesteps: int32 [16], replicated, may hold values from 62 to 999
- mask_embedding: float32 [768], replicated, may hold values from -6 to 6
- time_table: float32 [1000, 768], replicated, may hold values from -6 to 6
- attn_gain: float32 [4, 768], P('section'), may hold values from 0.5 to 1.5
- attn_shift: float32 [4, 768], P('section'), may hold values from -1.75 to 1.75
- joint_weight: float32 [4, 768, 1152], P('section'), may hold values from -0.21875 to 0.21875
- pair_bias: float32 [4, 768], P('section'), may hold values from -1.75 to 1.75
- out_weight: float32 [4, 384, 768], P('section'), may hold values from -4 to 4
- out_bias: float32 [4, 768], P('section'), may hold values from -1.75 to 1.75
- ffn_gain: float32 [4, 768], P('section'), may hold values from 0.5 to 1.5
- ffn_shift: float32 [4, 768], P('section'), may hold values from -1.75 to 1.75
- up_weight: float32 [4, 768, 1536], P('section'), may hold values from -0.21875 to 0.21875
- up_bias: float32 [4, 1536], P('section'), may hold values from -1.75 to 1.75
- down_weight: float32 [4, 1536, 768], P('section'), may hold values from -0.15625 to 0.15625
- down_bias: float32 [4, 768], P('section'), may hold values from -1.75 to 1.75
- cotangent: float32 [16384, 768], P('dp'), may hold values from -8 to 8
Outputs:
- output: float32 [16384, 768], P('dp', 'section')
- input_grad: float32 [16384, 768], P('dp', 'section')
- mask_embedding_grad: float32 [768], P('section')
- time_table_grad: float32 [1000, 768], P(None, 'section')
- attn_gain_grad: float32 [4, 768], P('section', 'dp')
- attn_shift_grad: float32 [4, 768], P('section', 'dp')
- joint_weight_grad: float32 [4, 768, 1152], P('section', 'dp')
- pair_bias_grad: float32 [4, 768], P('section', 'dp')
- out_weight_grad: float32 [4, 384, 768], P('section', None, 'dp')
- out_bias_grad: float32 [4, 768], P('section', 'dp')
- ffn_gain_grad: float32 [4, 768], P('section', 'dp')
- ffn_shift_grad: float32 [4, 768], P('section', 'dp')
- up_weight_grad: float32 [4, 768, 1536], P('section', None, 'dp')
- up_bias_grad: float32 [4, 1536], P('section', 'dp')
- down_weight_grad: float32 [4, 1536, 768], P('section', None, 'dp')
- down_bias_grad: float32 [4, 768], P('section', 'dp')
Inputs may be any that keep to these rules, and one draw needn't show every extreme that they name: A token of a sequence with timestep t is absorbed independently with probability (t + 1) / 1000, except in one sequence of every draw, which has no absorbed token.
All inputs are finite; a program needn't handle non-finite values.
Results may differ from a plain program's by a relative error of at most 0.0003.
Values sent between devices are 32-bit elements; how exact they have to be, the bound alone decides.
No kernel may reach another device: no remote copies, remote signals or barrier semaphores. Data moves between devices by JAX's collectives and lax.ppermute only.
A program may use at most 384 MiB of HBM per device.

v0:
```python
from functools import reduce
import math

import jax
import jax.numpy as jnp
from jax import lax
from jax.sharding import PartitionSpec as P

HS = 64
LEN = 1024


PRECISE = lax.Precision.HIGHEST


def from_partner(block, axis, bit):
    count = lax.axis_size(axis)
    route = []
    for low in range(count):
        high = low | 1 << bit
        if high != low and high < count:
            route += [(low, high), (high, low)]
    return lax.ppermute(block, axis, route)


def from_behind(value, axis, steps):
    count = lax.axis_size(axis)
    leading, last = (max(0, -steps), min(count, count - steps))
    return lax.ppermute(value, axis, [(source, source + steps) for source in range(leading, last)])


def shifted(array, axis, by):
    size = lax.axis_size(axis)
    return lax.ppermute(array, axis, [(i, (i + by) % size) for i in range(size)])


def normalize(matrix):
    center = matrix - jnp.mean(matrix, axis=-1, keepdims=True)
    return center * lax.rsqrt(jnp.mean(center * center, axis=-1, keepdims=True) + 1e-05)


def smooth_gate(values):
    return jax.nn.gelu(values, approximate=False)


def attend(queries, key_rows, values):
    length, feature_width = queries.shape
    head_count = feature_width // HS
    block_rows = min(512, length)
    block_count = length // block_rows
    score_scale = 1.0 / math.sqrt(HS)
    key_heads = key_rows.reshape(length, head_count, HS)
    value_heads = values.reshape(length, head_count, HS)

    def one_block(query_block):
        scores = jnp.einsum("qhd,khd->hqk", query_block, key_heads, precision=PRECISE) * score_scale
        row_max = jnp.max(scores, axis=-1, keepdims=True)
        weights = jnp.exp(scores - row_max)
        row_total = jnp.sum(weights, axis=-1)
        attended = jnp.einsum("hqk,khd->qhd", weights, value_heads, precision=PRECISE)
        attended = attended / jnp.transpose(row_total)[:, :, None]
        return (attended.reshape(block_rows, feature_width), row_max[:, :, 0] + jnp.log(row_total))

    attended, log_totals = lax.map(
        one_block, queries.reshape(block_count, block_rows, head_count, HS)
    )
    return (attended.reshape(length, feature_width), log_totals)


def attend_back(queries, key_rows, values, attended, log_totals, grad_attended):
    length, feature_width = queries.shape
    head_count = feature_width // HS
    block_rows = min(512, length)
    block_count = length // block_rows
    score_scale = 1.0 / math.sqrt(HS)
    key_heads = key_rows.reshape(length, head_count, HS)
    value_heads = values.reshape(length, head_count, HS)
    diagonal = jnp.sum((grad_attended * attended).reshape(length, head_count, HS), axis=-1)

    def one_block(carried, block_item):
        delta_keys, delta_values = carried
        query_block, grad_block, total_block, diag_block = block_item
        scores = jnp.einsum("qhd,khd->hqk", query_block, key_heads, precision=PRECISE) * score_scale
        probs = jnp.exp(scores - total_block[:, :, None])
        delta_values = delta_values + jnp.einsum(
            "hqk,qhd->khd", probs, grad_block, precision=PRECISE
        )
        delta_probs = jnp.einsum("qhd,khd->hqk", grad_block, value_heads, precision=PRECISE)
        delta_scores = probs * (delta_probs - jnp.transpose(diag_block)[:, :, None]) * score_scale
        delta_query = jnp.einsum("hqk,khd->qhd", delta_scores, key_heads, precision=PRECISE)
        delta_keys = delta_keys + jnp.einsum(
            "hqk,qhd->khd", delta_scores, query_block, precision=PRECISE
        )
        return ((delta_keys, delta_values), delta_query.reshape(block_rows, feature_width))

    zero_state = jnp.zeros((length, head_count, HS), jnp.float32)
    block_items = (
        queries.reshape(block_count, block_rows, head_count, HS),
        grad_attended.reshape(block_count, block_rows, head_count, HS),
        log_totals,
        diagonal.reshape(block_count, block_rows, head_count),
    )
    (delta_keys, delta_values), delta_queries = lax.scan(
        one_block, (zero_state, zero_state), block_items
    )
    return (
        delta_queries.reshape(length, feature_width),
        delta_keys.reshape(length, feature_width),
        delta_values.reshape(length, feature_width),
    )


def attention_half(inputs, params):
    norm_gain, norm_shift, joint_matrix, pair_offset, out_matrix, out_offset = params
    inner_width = out_matrix.shape[0]
    normed = normalize(inputs) * norm_gain + norm_shift
    projected = jnp.dot(normed, joint_matrix, precision=PRECISE)
    queries = projected[:, :inner_width] + pair_offset[:inner_width]
    key_rows = projected[:, inner_width : 2 * inner_width]
    values = projected[:, 2 * inner_width :] + pair_offset[inner_width:]
    attended, log_totals = attend(queries, key_rows, values)
    partial_value = jnp.dot(attended, out_matrix, precision=PRECISE) + out_offset
    return (partial_value, (queries, key_rows, values, attended, log_totals))


def attention_back(inputs, kept_state, grad_rows, params):
    norm_gain, norm_shift, joint_matrix, pair_offset, out_matrix, out_offset = params
    queries, key_rows, values, attended, log_totals = kept_state
    delta_out_offset = jnp.sum(grad_rows, axis=0)
    delta_out_matrix = jnp.einsum("lw,ld->wd", attended, grad_rows, precision=PRECISE)
    delta_attended = jnp.einsum("ld,wd->lw", grad_rows, out_matrix, precision=PRECISE)
    delta_queries, delta_keys, delta_values = attend_back(
        queries, key_rows, values, attended, log_totals, delta_attended
    )
    delta_projected = jnp.concatenate([delta_queries, delta_keys, delta_values], axis=1)
    delta_pair = jnp.concatenate([jnp.sum(delta_queries, axis=0), jnp.sum(delta_values, axis=0)])
    unit_rows, norm_pull = jax.vjp(normalize, inputs)
    normed = unit_rows * norm_gain + norm_shift
    delta_joint = jnp.einsum("ld,lp->dp", normed, delta_projected, precision=PRECISE)
    delta_normed = jnp.einsum("lp,dp->ld", delta_projected, joint_matrix, precision=PRECISE)
    delta_gain = jnp.sum(delta_normed * unit_rows, axis=0)
    delta_shift = jnp.sum(delta_normed, axis=0)
    delta_inputs = norm_pull(delta_normed * norm_gain)[0]
    return (
        delta_inputs,
        (delta_gain, delta_shift, delta_joint, delta_pair, delta_out_matrix, delta_out_offset),
    )


def feed_half(inputs, params):
    norm_gain, norm_shift, up_matrix, up_offset, down_matrix, down_offset = params
    normed = normalize(inputs) * norm_gain + norm_shift
    before = jnp.dot(normed, up_matrix, precision=PRECISE) + up_offset
    partial_value = jnp.dot(smooth_gate(before), down_matrix, precision=PRECISE) + down_offset
    return (partial_value, before)


def feed_back(inputs, before, grad_rows, params):
    norm_gain, norm_shift, up_matrix, up_offset, down_matrix, down_offset = params
    delta_down_offset = jnp.sum(grad_rows, axis=0)
    activated, gate_pull = jax.vjp(smooth_gate, before)
    delta_down_matrix = jnp.einsum("lf,ld->fd", activated, grad_rows, precision=PRECISE)
    delta_before = gate_pull(jnp.einsum("ld,fd->lf", grad_rows, down_matrix, precision=PRECISE))[0]
    delta_up_offset = jnp.sum(delta_before, axis=0)
    unit_rows, norm_pull = jax.vjp(normalize, inputs)
    normed = unit_rows * norm_gain + norm_shift
    delta_up_matrix = jnp.einsum("ld,lf->df", normed, delta_before, precision=PRECISE)
    delta_normed = jnp.einsum("lf,df->ld", delta_before, up_matrix, precision=PRECISE)
    delta_gain = jnp.sum(delta_normed * unit_rows, axis=0)
    delta_shift = jnp.sum(delta_normed, axis=0)
    delta_inputs = norm_pull(delta_normed * norm_gain)[0]
    return (
        delta_inputs,
        (
            delta_gain,
            delta_shift,
            delta_up_matrix,
            delta_up_offset,
            delta_down_matrix,
            delta_down_offset,
        ),
    )


def run_attention(operand):
    return attention_half(operand[0], operand[1])


def blank_attention(operand):
    inputs, params = operand
    inner_width = params[4].shape[0]
    length = inputs.shape[0]
    block_rows = min(512, length)
    plane = jnp.zeros((length, inner_width), jnp.float32)
    totals = jnp.zeros((length // block_rows, inner_width // HS, block_rows), jnp.float32)
    return (jnp.zeros_like(inputs), (plane, plane, plane, plane, totals))


def run_feed(operand):
    return feed_half(operand[0], operand[1])


def blank_feed(operand):
    inputs, params = operand
    return (jnp.zeros_like(inputs), jnp.zeros((inputs.shape[0], params[2].shape[1]), jnp.float32))


def run_feed_back(operand):
    return feed_back(operand[0], operand[1], operand[2], operand[3])


def blank_feed_back(operand):
    return (jnp.zeros_like(operand[0]), jax.tree.map(jnp.zeros_like, operand[3]))


def run_attention_back(operand):
    return attention_back(operand[0], operand[1], operand[2], operand[3])


def blank_attention_back(operand):
    return (jnp.zeros_like(operand[0]), jax.tree.map(jnp.zeros_like, operand[3]))


def add_trees(first_tree, second_tree):
    return jax.tree.map(jnp.add, first_tree, second_tree)


def columns(matrix, column_block, quarter):
    return lax.dynamic_slice_in_dim(matrix, column_block * quarter, quarter, matrix.ndim - 1)


def body(
    tokens,
    absorbed,
    timesteps,
    mask_embedding,
    time_table,
    attn_gain,
    attn_shift,
    joint_weight,
    pair_bias,
    out_weight,
    out_bias,
    ffn_gain,
    ffn_shift,
    up_weight,
    up_bias,
    down_weight,
    down_bias,
    cotangent,
):
    section_index = lax.axis_index("section")
    section_count = lax.axis_size("section")
    layer_index = section_index // 2
    first_layer = layer_index == 0
    feature_width = tokens.shape[1]
    seq_count = tokens.shape[0] // LEN
    attn_params = (
        attn_gain[0],
        attn_shift[0],
        joint_weight[0],
        pair_bias[0],
        out_weight[0],
        out_bias[0],
    )
    feed_params = (
        ffn_gain[0],
        ffn_shift[0],
        up_weight[0],
        up_bias[0],
        down_weight[0],
        down_bias[0],
    )
    step_range = jnp.arange(time_table.shape[0], dtype=jnp.int32)
    own_steps = lax.dynamic_slice_in_dim(timesteps, lax.axis_index("dp") * seq_count, seq_count)
    own_picks = (own_steps[:, None] == step_range[None, :]).astype(jnp.float32)
    step_rows = jnp.dot(own_picks, time_table, precision=PRECISE)
    masked = absorbed.reshape(seq_count, LEN).astype(jnp.float32)
    row_weight = LEN / jnp.maximum(jnp.sum(masked, axis=1), 1.0)
    token_blocks = tokens.reshape(seq_count, LEN, feature_width)
    cot_blocks = cotangent.reshape(seq_count, LEN, feature_width)
    arriving = jnp.zeros((LEN, feature_width), jnp.float32)
    kept_steps = []
    leaving_steps = []
    for forward_step in range(seq_count + 1):
        batch_index = forward_step - layer_index
        is_valid = (batch_index >= 0) & (batch_index < seq_count)
        batch_safe = jnp.clip(batch_index, 0, seq_count - 1)
        mask_rows = lax.dynamic_index_in_dim(masked, batch_safe, 0, keepdims=False)
        absorbed_row = mask_embedding + lax.dynamic_index_in_dim(
            step_rows, batch_safe, 0, keepdims=False
        )
        clean_rows = lax.dynamic_index_in_dim(token_blocks, batch_safe, 0, keepdims=False)
        start_rows = jnp.where(mask_rows[:, None] > 0.5, absorbed_row[None, :], clean_rows)
        layer_input = jnp.where(first_layer, start_rows, arriving)
        attn_part, attn_kept = lax.cond(
            is_valid, run_attention, blank_attention, (layer_input, attn_params)
        )
        middle = layer_input + (attn_part + from_partner(attn_part, "section", 0))
        feed_part, before = lax.cond(is_valid, run_feed, blank_feed, (middle, feed_params))
        leaving = middle + (feed_part + from_partner(feed_part, "section", 0))
        kept_steps.append((layer_input, attn_kept, middle, before))
        leaving_steps.append(leaving)
        if forward_step < seq_count:
            arriving = from_behind(leaving, "section", 2)
    incoming = jnp.zeros((LEN, feature_width), jnp.float32)
    collected = []
    input_steps = []
    for backward_step in range(seq_count + 1):
        forward_step = seq_count - backward_step
        batch_index = forward_step - layer_index
        is_valid = (batch_index >= 0) & (batch_index < seq_count)
        batch_safe = jnp.clip(batch_index, 0, seq_count - 1)
        mask_rows = lax.dynamic_index_in_dim(masked, batch_safe, 0, keepdims=False)
        weight_now = lax.dynamic_index_in_dim(row_weight, batch_safe, 0, keepdims=False)
        own_grad = (
            lax.dynamic_index_in_dim(cot_blocks, batch_safe, 0, keepdims=False)
            * (mask_rows * weight_now)[:, None]
        )
        grad_out = jnp.where(first_layer, incoming, own_grad)
        layer_input, attn_kept, middle, before = kept_steps[forward_step]
        feed_delta, feed_terms = lax.cond(
            is_valid, run_feed_back, blank_feed_back, (middle, before, grad_out, feed_params)
        )
        grad_middle = grad_out + (feed_delta + from_partner(feed_delta, "section", 0))
        attn_delta, attn_terms = lax.cond(
            is_valid,
            run_attention_back,
            blank_attention_back,
            (layer_input, attn_kept, grad_middle, attn_params),
        )
        grad_input = grad_middle + (attn_delta + from_partner(attn_delta, "section", 0))
        attn_gain_term, attn_shift_term, joint_term, pair_term, out_term, out_bias_term = attn_terms
        ffn_gain_term, ffn_shift_term, up_term, up_bias_term, down_term, down_bias_term = feed_terms
        step_terms = (
            attn_gain_term,
            attn_shift_term,
            joint_term,
            pair_term,
            out_term,
            out_bias_term,
            ffn_gain_term,
            ffn_shift_term,
            up_term,
            up_bias_term,
            down_term,
            down_bias_term,
        )
        collected.append(step_terms)
        input_steps.append(grad_input)
        if backward_step < seq_count:
            incoming = from_behind(grad_input, "section", -2)
    summed = reduce(add_trees, collected)
    (
        attn_gain_term,
        attn_shift_term,
        joint_term,
        pair_term,
        out_term,
        out_bias_term,
        ffn_gain_term,
        ffn_shift_term,
        up_term,
        up_bias_term,
        down_term,
        down_bias_term,
    ) = summed
    shares = (
        lax.psum_scatter(attn_gain_term, "dp", scatter_dimension=0, tiled=True),
        lax.psum_scatter(attn_shift_term, "dp", scatter_dimension=0, tiled=True),
        lax.psum_scatter(joint_term, "dp", scatter_dimension=0, tiled=True),
        lax.psum_scatter(pair_term, "dp", scatter_dimension=0, tiled=True),
        lax.psum_scatter(out_term, "dp", scatter_dimension=1, tiled=True),
        lax.psum_scatter(out_bias_term, "dp", scatter_dimension=0, tiled=True),
        lax.psum_scatter(ffn_gain_term, "dp", scatter_dimension=0, tiled=True),
        lax.psum_scatter(ffn_shift_term, "dp", scatter_dimension=0, tiled=True),
        lax.psum_scatter(up_term, "dp", scatter_dimension=1, tiled=True),
        lax.psum_scatter(up_bias_term, "dp", scatter_dimension=0, tiled=True),
        lax.psum_scatter(down_term, "dp", scatter_dimension=1, tiled=True),
        lax.psum_scatter(down_bias_term, "dp", scatter_dimension=0, tiled=True),
    )
    final_rows = jnp.concatenate(leaving_steps[1:], axis=0)
    delta_rows = jnp.concatenate(
        [input_steps[seq_count - batch_number] for batch_number in range(seq_count)], axis=0
    )
    flat_mask = masked.reshape(-1)[:, None]
    input_grad = delta_rows * (1.0 - flat_mask)
    seq_sums = jnp.sum((delta_rows * flat_mask).reshape(seq_count, LEN, feature_width), axis=1)
    mask_part = jnp.sum(seq_sums, axis=0)
    local_table = jnp.einsum("st,sd->td", own_picks, seq_sums, precision=PRECISE)
    mask_grad, table_grad = lax.psum((mask_part, local_table), "dp")
    quarter = feature_width // section_count
    target = (section_index + 2) % section_count
    sending = jnp.where(
        first_layer, columns(input_grad, target, quarter), columns(final_rows, target, quarter)
    )
    got_rows, got_mask, got_table = shifted(
        (sending, columns(mask_grad, target, quarter), columns(table_grad, target, quarter)),
        "section",
        2,
    )
    output_cols = jnp.where(first_layer, got_rows, columns(final_rows, section_index, quarter))
    grad_cols = jnp.where(first_layer, columns(input_grad, section_index, quarter), got_rows)
    mask_cols = jnp.where(first_layer, columns(mask_grad, section_index, quarter), got_mask)
    table_cols = jnp.where(first_layer, columns(table_grad, section_index, quarter), got_table)
    return (
        output_cols,
        grad_cols,
        mask_cols,
        table_cols,
        shares[0][None],
        shares[1][None],
        shares[2][None],
        shares[3][None],
        shares[4][None],
        shares[5][None],
        shares[6][None],
        shares[7][None],
        shares[8][None],
        shares[9][None],
        shares[10][None],
        shares[11][None],
    )


def solution(mesh):
    placed = (
        P("dp", None),
        P("dp"),
        P(),
        P(),
        P(),
        P("section", None),
        P("section", None),
        P("section", None, None),
        P("section", None),
        P("section", None, None),
        P("section", None),
        P("section", None),
        P("section", None),
        P("section", None, None),
        P("section", None),
        P("section", None, None),
        P("section", None),
        P("dp", None),
    )
    return jax.shard_map(
        body,
        mesh=mesh,
        in_specs=placed,
        out_specs=(
            P("dp", "section"),
            P("dp", "section"),
            P("section"),
            P(None, "section"),
            P("section", "dp"),
            P("section", "dp"),
            P("section", "dp", None),
            P("section", "dp"),
            P("section", None, "dp"),
            P("section", "dp"),
            P("section", "dp"),
            P("section", "dp"),
            P("section", None, "dp"),
            P("section", "dp"),
            P("section", None, "dp"),
            P("section", "dp"),
        ),
        check_vma=False,
    )
```

profile of v0, /device:TPU:0, one launch (start us, length us, event | category | flops | bytes accessed | tf_op | source)
XLA Modules:
  0.0 3293.3 jit_solution(15987290063724156549)
XLA Ops:
  29.8 116.4 %conditional.12 = (f32[1024,384]{1,0:T(8,128)}, f32[1024,384]{1,0:T(8,128)}, f32[1024,384]{1,0:T(8,128)}, f32[1024,384]{1,0:T(8,128)}, f32[2,6,512]{2,1,0:T(8,128)}, /*index=5*/f32[1024,768]{0,1:T(8,128)}) conditional(s32[]{:T(128)} %convert_element_type.31, () %tuple.130, (f32[1024,768]{0,1:T(8,128)S(1)}, f32[1,768]{1,0:T(1,128)S(1)}, ...), branch_computations={%region_1.2_spmd, %region_2.9_spmd} | conditional | flops 19357431808 | bytes 129163592 | solution.py:296
  65.3 69.5 %while.75 = (s32[]{:T(128)}, f32[2,512,384]{2,1,0:T(8,128)}, f32[2,6,512]{2,1,0:T(8,128)}, f32[2,512,6,64]{1,0,3,2:T(2,128)}, f32[1024,6,64]{0,2,1:T(8,128)S(1)}, /*index=5*/f32[1024,6,64]{0,2,1:T(8,128)}, s32[]{:T(128)}) while((s32[]{:T(128)}, f32[2,512,384]{2,1,0:T(8,128)}, f32[2,6,512]{2,1,0:T(8,128)}, f32[2,512,6,64]{1,0,3,2:T(2,128)}, ...), condition=%wide.region_8.8_spmd, body=%wide.region_5.7_spmd.sunk | while | flops 4854051840 | bytes 53579900 | solution.py:64
  149.3 68.3 %collective-permute-done = f32[1024,768]{0,1:T(8,128)S(1)} collective-permute-done((f32[1024,768]{0,1:T(8,128)}, f32[1024,768]{0,1:T(8,128)S(1)}, u32[]{:S(2)}, u32[]{:S(2)}) %collective-permute-start) | collective-permute-done | bytes 3145760 | tf_op jit(solution)/shard_map/ppermute | solution.py:23
  221.1 67.7 %conditional.13 = (f32[1024,1536]{1,0:T(8,128)}, f32[1024,768]{0,1:T(8,128)}) conditional(s32[]{:T(128)} %convert_element_type.31, () %tuple.132, (f32[1024,768]{0,1:T(8,128)S(1)}, f32[1,768]{1,0:T(1,128)S(1)}, f32[1,768]{1,0:T(1,128)S(1)}, f32[768,1536]{1,0:T(8,128)}, f32[1,1536]{1,0:T(1,128)S(1)}, /*index=5*/f32[1536,768]{1,0:T(8,128)}, ...), branch_computations={%region_9.10_spmd, %region_10.13_spmd} | conditional | flops 29100343296 | bytes 47268900 | solution.py:300
  290.6 67.7 %collective-permute-done.1 = f32[1024,768]{0,1:T(8,128)S(1)} collective-permute-done((f32[1024,768]{0,1:T(8,128)}, f32[1024,768]{0,1:T(8,128)S(1)}, u32[]{:S(2)}, u32[]{:S(2)}) %collective-permute-start.1) | collective-permute-done | bytes 3145760 | tf_op jit(solution)/shard_map/ppermute | solution.py:23
  368.0 62.7 %collective-permute-done.2 = f32[1024,768]{0,1:T(8,128)S(1)} collective-permute-done((f32[1024,768]{0,1:T(8,128)}, f32[1024,768]{0,1:T(8,128)S(1)}, u32[]{:S(2)}, u32[]{:S(2)}) %collective-permute-start.2) | collective-permute-done | bytes 3145760 | tf_op jit(solution)/shard_map/ppermute | solution.py:29
  434.8 123.8 %conditional.14 = (f32[1024,384]{1,0:T(8,128)}, f32[1024,384]{1,0:T(8,128)}, f32[1024,384]{1,0:T(8,128)}, f32[1024,384]{1,0:T(8,128)}, f32[2,6,512]{2,1,0:T(8,128)}, /*index=5*/f32[1024,768]{0,1:T(8,128)}) conditional(s32[]{:T(128)} %convert_element_type.32, () %tuple.134, (f32[1024,768]{0,1:T(8,128)S(1)}, f32[1,768]{1,0:T(1,128)S(1)}, ...), branch_computations={%region_13.14_spmd, %region_14.21_spmd} | conditional | flops 19357431808 | bytes 111849728 | solution.py:296
  471.5 75.3 %while.76 = (s32[]{:T(128)}, f32[2,512,384]{2,1,0:T(8,128)}, f32[2,6,512]{2,1,0:T(8,128)}, f32[2,512,6,64]{1,0,3,2:T(2,128)}, f32[1024,6,64]{0,2,1:T(8,128)}, /*index=5*/f32[1024,6,64]{0,2,1:T(8,128)}, s32[]{:T(128)}) while((s32[]{:T(128)}, f32[2,512,384]{2,1,0:T(8,128)}, f32[2,6,512]{2,1,0:T(8,128)}, f32[2,512,6,64]{1,0,3,2:T(2,128)}, ...), condition=%wide.region_20.20_spmd, body=%wide.region_17.19_spmd.sunk | while | flops 4854051840 | bytes 53579900 | solution.py:64
  558.5 68.5 %collective-permute-start.3 = (f32[1024,768]{0,1:T(8,128)}, f32[1024,768]{0,1:T(8,128)S(1)}, u32[]{:S(2)}, u32[]{:S(2)}) collective-permute-start(f32[1024,768]{0,1:T(8,128)} %get-tuple-element.1438), channel_id=1, source_target_pairs={{0,8},{8,0},{16,24},{24,16},{1,9},{9,1},{17,25},{25,17},{2,10},{10... | collective-permute-start | bytes 9437192 | tf_op jit(solution)/shard_map/ppermute | solution.py:23
  627.1 68.0 %collective-permute-done.3 = f32[1024,768]{0,1:T(8,128)S(1)} collective-permute-done((f32[1024,768]{0,1:T(8,128)}, f32[1024,768]{0,1:T(8,128)S(1)}, u32[]{:S(2)}, u32[]{:S(2)}) %collective-permute-start.3) | collective-permute-done | bytes 3145760 | tf_op jit(solution)/shard_map/ppermute | solution.py:23
  699.7 62.8 %conditional.15 = (f32[1024,1536]{1,0:T(8,128)}, f32[1024,768]{0,1:T(8,128)}) conditional(s32[]{:T(128)} %convert_element_type.32, () %tuple.136, (f32[1024,768]{0,1:T(8,128)}, f32[1,768]{1,0:T(1,128)S(1)}, f32[1,768]{1,0:T(1,128)S(1)}, f32[768,1536]{1,0:T(8,128)}, f32[1,1536]{1,0:T(1,128)S(1)}, /*index=5*/f32[1536,768]{1,0:T(8,128)}, ...), branch_computations={%region_21.22_spmd, %region_22.25_spmd} | conditional | flops 29100343296 | bytes 72434784 | solution.py:300
  764.3 67.4 %collective-permute-done.4 = f32[1024,768]{0,1:T(8,128)S(1)} collective-permute-done((f32[1024,768]{0,1:T(8,128)}, f32[1024,768]{0,1:T(8,128)S(1)}, u32[]{:S(2)}, u32[]{:S(2)}) %collective-permute-start.4) | collective-permute-done | bytes 3145760 | tf_op jit(solution)/shard_map/ppermute | solution.py:23
  847.1 60.3 %collective-permute-done.5 = f32[1024,768]{0,1:T(8,128)} collective-permute-done((f32[1024,768]{0,1:T(8,128)S(1)}, f32[1024,768]{0,1:T(8,128)}, u32[]{:S(2)}, u32[]{:S(2)}) %collective-permute-start.5) | collective-permute-done | bytes 3145760 | tf_op jit(solution)/shard_map/ppermute | solution.py:29
  927.3 68.5 %collective-permute-start.6 = (f32[1024,768]{0,1:T(8,128)}, f32[1024,768]{0,1:T(8,128)}, u32[]{:S(2)}, u32[]{:S(2)}) collective-permute-start(f32[1024,768]{0,1:T(8,128)} %get-tuple-element.1440), channel_id=1, source_target_pairs={{0,8},{8,0},{16,24},{24,16},{1,9},{9,1},{17,25},{25,17},{2,10},{10... | collective-permute-start | bytes 9437192 | tf_op jit(solution)/shard_map/ppermute | solution.py:23
  1004.3 59.7 %collective-permute-done.6 = f32[1024,768]{0,1:T(8,128)} collective-permute-done((f32[1024,768]{0,1:T(8,128)}, f32[1024,768]{0,1:T(8,128)}, u32[]{:S(2)}, u32[]{:S(2)}) %collective-permute-start.6) | collective-permute-done | bytes 3145760 | tf_op jit(solution)/shard_map/ppermute | solution.py:23
  1100.6 67.5 %collective-permute-done.7 = f32[1024,768]{0,1:T(8,128)S(1)} collective-permute-done((f32[1024,768]{0,1:T(8,128)}, f32[1024,768]{0,1:T(8,128)S(1)}, u32[]{:S(2)}, u32[]{:S(2)}) %collective-permute-start.7) | collective-permute-done | bytes 3145760 | tf_op jit(solution)/shard_map/ppermute | solution.py:23
  1186.1 66.9 %collective-permute-done.8 = f32[1024,768]{0,1:T(8,128)S(1)} collective-permute-done((f32[1024,768]{0,1:T(8,128)}, f32[1024,768]{0,1:T(8,128)S(1)}, u32[]{:S(2)}, u32[]{:S(2)}) %collective-permute-start.8) | collective-permute-done | bytes 3145760 | tf_op jit(solution)/shard_map/ppermute | solution.py:23
  1262.3 600.5 %collective-permute-done.9 = f32[1024,768]{0,1:T(8,128)} collective-permute-done((f32[1024,768]{0,1:T(8,128)}, f32[1024,768]{0,1:T(8,128)}, u32[]{:S(2)}, u32[]{:S(2)}) %collective-permute-start.9) | collective-permute-done | bytes 3145760 | tf_op jit(solution)/shard_map/ppermute | solution.py:29
  1868.4 113.7 %conditional.20 = (f32[768]{0:T(1024)S(1)}, f32[768]{0:T(1024)S(1)}, f32[1536]{0:T(1024)S(1)}, f32[768]{0:T(1024)S(1)}, f32[1024,768]{0,1:T(8,128)}, /*index=5*/f32[768,1536]{0,1:T(8,128)}, f32[1536,768]{0,1:T(8,128)}) conditional(s32[]{:T(128)} %convert_element_type.32, () %tuple.144, (f32[1024,1536]{1,0:T(8,128)}, f32[1024,768]{0,1:T(8,128)}, ...), branch_computations={%region_61.62_spmd, %region_62.71_spmd} | conditional | flops 58118111232 | bytes 141687936 | solution.py:322
  1982.3 70.0 %collective-permute-done.10 = f32[1024,768]{0,1:T(8,128)S(1)} collective-permute-done((f32[1024,768]{0,1:T(8,128)}, f32[1024,768]{0,1:T(8,128)S(1)}, u32[]{:S(2)}, u32[]{:S(2)}) %collective-permute-start.10) | collective-permute-done | bytes 3145760 | tf_op jit(solution)/shard_map/ppermute | solution.py:23
  2057.9 222.5 %conditional.21 = (f32[768]{0:T(1024)}, f32[768]{0:T(1024)}, f32[768,1152]{1,0:T(8,128)}, f32[768]{0:T(1024)}, f32[768]{0:T(1024)}, /*index=5*/f32[1024,768]{0,1:T(8,128)}, f32[384,768]{0,1:T(8,128)}) conditional(s32[]{:T(128)} %convert_element_type.32, () %tuple.146, (f32[1024,384]{1,0:T(8,128)}, f32[1024,768]{0,1:T(8,128)}, ...), branch_computations={%region_71.72_spmd, %region_72.85_spmd} | conditional | flops 41120169984 | bytes 314091456 | solution.py:326
  2098.8 134.1 %while.79 = (s32[]{:T(128)}, f32[1024,6,64]{0,2,1:T(8,128)}, f32[1024,6,64]{0,2,1:T(8,128)}, f32[2,512,384]{1,2,0:T(8,128)}, f32[2,512,6,64]{1,0,3,2:T(2,128)S(1...) while((s32[]{:T(128)}, f32[1024,6,64]{0,2,1:T(8,128)}, ...), condition=%wide.region_75.75_spmd.clone, body=%wide.region_74.74_spmd.clone.sunk | while | flops 12103188480 | bytes 151867856 | solution.py:103
  2280.8 68.9 %collective-permute-done.11 = f32[1024,768]{0,1:T(8,128)S(1)} collective-permute-done((f32[1024,768]{0,1:T(8,128)}, f32[1024,768]{0,1:T(8,128)S(1)}, u32[]{:S(2)}, u32[]{:S(2)}) %collective-permute-start.11) | collective-permute-done | bytes 3145760 | tf_op jit(solution)/shard_map/ppermute | solution.py:23
  2358.9 134.9 %collective-permute-done.12 = f32[1024,768]{0,1:T(8,128)} collective-permute-done((f32[1024,768]{0,1:T(8,128)}, f32[1024,768]{0,1:T(8,128)}, u32[]{:S(2)}, u32[]{:S(2)}) %collective-permute-start.12) | collective-permute-done | bytes 3145760 | tf_op jit(solution)/shard_map/ppermute | solution.py:29
  2499.5 113.8 %conditional.22 = (f32[768]{0:T(1024)S(1)}, f32[768]{0:T(1024)S(1)}, f32[1536]{0:T(1024)S(1)}, f32[768]{0:T(1024)S(1)}, f32[1024,768]{0,1:T(8,128)}, /*index=5*/f32[768,1536]{0,1:T(8,128)}, f32[1536,768]{0,1:T(8,128)}) conditional(s32[]{:T(128)} %convert_element_type.31, () %tuple.148, (f32[1024,1536]{1,0:T(8,128)}, f32[1024,768]{0,1:T(8,128)}, ...), branch_computations={%region_85.86_spmd, %region_86.95_spmd} | conditional | flops 58118111232 | bytes 141687936 | solution.py:322
  2613.5 69.8 %collective-permute-done.13 = f32[1024,768]{0,1:T(8,128)S(1)} collective-permute-done((f32[1024,768]{0,1:T(8,128)}, f32[1024,768]{0,1:T(8,128)S(1)}, u32[]{:S(2)}, u32[]{:S(2)}) %collective-permute-start.13) | collective-permute-done | bytes 3145760 | tf_op jit(solution)/shard_map/ppermute | solution.py:23
  2688.9 222.7 %conditional.23 = (f32[768]{0:T(1024)}, f32[768]{0:T(1024)}, f32[768,1152]{1,0:T(8,128)}, f32[768]{0:T(1024)}, f32[768]{0:T(1024)}, /*index=5*/f32[1024,768]{0,1:T(8,128)}, f32[384,768]{0,1:T(8,128)}) conditional(s32[]{:T(128)} %convert_element_type.31, () %tuple.150, (f32[1024,384]{1,0:T(8,128)}, f32[1024,768]{0,1:T(8,128)}, ...), branch_computations={%region_95.96_spmd, %region_96.109_spmd} | conditional | flops 41120169984 | bytes 314091456 | solution.py:326
  2730.1 134.1 %while.80 = (s32[]{:T(128)}, f32[1024,6,64]{0,2,1:T(8,128)}, f32[1024,6,64]{0,2,1:T(8,128)}, f32[2,512,384]{1,2,0:T(8,128)}, f32[2,512,6,64]{1,0,3,2:T(2,128)S(1...) while((s32[]{:T(128)}, f32[1024,6,64]{0,2,1:T(8,128)}, ...), condition=%wide.region_99.99_spmd.clone, body=%wide.region_98.98_spmd.clone.sunk | while | flops 12103188480 | bytes 151867856 | solution.py:103
  2912.0 68.6 %collective-permute-done.14 = f32[1024,768]{0,1:T(8,128)S(1)} collective-permute-done((f32[1024,768]{0,1:T(8,128)}, f32[1024,768]{0,1:T(8,128)S(1)}, u32[]{:S(2)}, u32[]{:S(2)}) %collective-permute-start.14) | collective-permute-done | bytes 3145760 | tf_op jit(solution)/shard_map/ppermute | solution.py:23
  3040.0 58.3 %collective-permute-done.15 = f32[1024,768]{0,1:T(8,128)} collective-permute-done((f32[1024,768]{0,1:T(8,128)}, f32[1024,768]{0,1:T(8,128)}, u32[]{:S(2)}, u32[]{:S(2)}) %collective-permute-start.15) | collective-permute-done | bytes 3145760 | tf_op jit(solution)/shard_map/ppermute | solution.py:23
  3143.0 47.0 %collective-permute-done.17 = f32[192]{0:T(256)S(1)} collective-permute-done((f32[192]{0:T(256)S(1)}, f32[192]{0:T(256)S(1)}, u32[]{:S(2)}, u32[]{:S(2)}) %collective-permute-start.17) | collective-permute-done | bytes 800 | tf_op jit(solution)/shard_map/ppermute | solution.py:34
  3234.2 52.4 %reduce-scatter.5.cloned.1.call-done = f32[96,1152]{1,0:T(8,128)} async-done(((f32[768,1152]{1,0:T(8,128)}), f32[96,1152]{1,0:T(8,128)}) %reduce-scatter.5.cloned.1.call-update) | async-done | bytes 442384 | tf_op jit(solution)/shard_map/reduce_scatter | solution.py:371
  (686 shorter events, 1387.0 us)
Async XLA Ops:
  7.2 3132.9 %all-reduce.11.cloned.1.call-start = ((), (), s32[]{:S(2)}) async-start(), calls=%async_computation.4 | async-start | bytes 6144000 | tf_op jit(solution)/shard_map/psum | solution.py:391
  146.2 71.4 %collective-permute-start = (f32[1024,768]{0,1:T(8,128)}, f32[1024,768]{0,1:T(8,128)S(1)}, u32[]{:S(2)}, u32[]{:S(2)}) collective-permute-start(f32[1024,768]{0,1:T(8,128)} %get-tuple-element.1436), channel_id=1, source_target_pairs={{0,8},{8,0},{16,24},{24,16},{1,9},{9,1},{17,25},{25,17},{2,10},{10... | collective-permute-start | bytes 9437192 | tf_op jit(solution)/shard_map/ppermute | solution.py:23
  221.1 137.3 %copy-start.13 = (f32[1024,768]{0,1:T(8,128)}, f32[1024,768]{0,1:T(8,128)S(1)}, u32[]{:S(2)}) copy-start(f32[1024,768]{0,1:T(8,128)S(1)} %add_add_fusion.20) | copy-start | bytes 9437188
  288.8 69.6 %collective-permute-start.1 = (f32[1024,768]{0,1:T(8,128)}, f32[1024,768]{0,1:T(8,128)S(1)}, u32[]{:S(2)}, u32[]{:S(2)}) collective-permute-start(f32[1024,768]{0,1:T(8,128)} %get-tuple-element.1437), channel_id=1, source_target_pairs={{0,8},{8,0},{16,24},{24,16},{1,9},{9,1},{17,25},{25,17},{2,10},{10... | collective-permute-start | bytes 9437192 | tf_op jit(solution)/shard_map/ppermute | solution.py:23
  362.9 67.8 %collective-permute-start.2 = (f32[1024,768]{0,1:T(8,128)}, f32[1024,768]{0,1:T(8,128)S(1)}, u32[]{:S(2)}, u32[]{:S(2)}) collective-permute-start(f32[1024,768]{0,1:T(8,128)} %add_add_fusion.19), channel_id=1, source_target_pairs={{0,16},{8,24},{1,17},{9,25},{2,18},{10,26},{3,19},{11,27},{4,20},{... | collective-permute-start | bytes 9437192 | tf_op jit(solution)/shard_map/ppermute | solution.py:29
  434.7 260.4 %copy-start.17 = (f32[1024,768]{0,1:T(8,128)}, f32[1024,768]{0,1:T(8,128)S(1)}, u32[]{:S(2)}) copy-start(f32[1024,768]{0,1:T(8,128)S(1)} %fusion.561) | copy-start | bytes 9437188
  558.5 136.6 %collective-permute-start.3 = (f32[1024,768]{0,1:T(8,128)}, f32[1024,768]{0,1:T(8,128)S(1)}, u32[]{:S(2)}, u32[]{:S(2)}) collective-permute-start(f32[1024,768]{0,1:T(8,128)} %get-tuple-element.1438), channel_id=1, source_target_pairs={{0,8},{8,0},{16,24},{24,16},{1,9},{9,1},{17,25},{25,17},{2,10},{10... | collective-permute-start | bytes 9437192 | tf_op jit(solution)/shard_map/ppermute | solution.py:23
  762.5 69.3 %collective-permute-start.4 = (f32[1024,768]{0,1:T(8,128)}, f32[1024,768]{0,1:T(8,128)S(1)}, u32[]{:S(2)}, u32[]{:S(2)}) collective-permute-start(f32[1024,768]{0,1:T(8,128)} %get-tuple-element.1439), channel_id=1, source_target_pairs={{0,8},{8,0},{16,24},{24,16},{1,9},{9,1},{17,25},{25,17},{2,10},{10... | collective-permute-start | bytes 9437192 | tf_op jit(solution)/shard_map/ppermute | solution.py:23
  835.7 71.8 %collective-permute-start.5 = (f32[1024,768]{0,1:T(8,128)S(1)}, f32[1024,768]{0,1:T(8,128)}, u32[]{:S(2)}, u32[]{:S(2)}) collective-permute-start(f32[1024,768]{0,1:T(8,128)S(1)} %add_add_fusion.17), channel_id=1, source_target_pairs={{0,16},{8,24},{1,17},{9,25},{2,18},{10,26},{3,19},{11,27},{4,20},{... | collective-permute-start | bytes 9437192 | tf_op jit(solution)/shard_map/ppermute | solution.py:29
  909.7 86.1 %copy-start.84 = (f32[2,1024]{1,0:T(2,128)S(1)}, f32[2,1024]{1,0:T(2,128)}, u32[]{:S(2)}) copy-start(f32[2,1024]{1,0:T(2,128)} %copy-done.83) | copy-start | bytes 24580
  927.3 136.7 %collective-permute-start.6 = (f32[1024,768]{0,1:T(8,128)}, f32[1024,768]{0,1:T(8,128)}, u32[]{:S(2)}, u32[]{:S(2)}) collective-permute-start(f32[1024,768]{0,1:T(8,128)} %get-tuple-element.1440), channel_id=1, source_target_pairs={{0,8},{8,0},{16,24},{24,16},{1,9},{9,1},{17,25},{25,17},{2,10},{10... | collective-permute-start | bytes 9437192 | tf_op jit(solution)/shard_map/ppermute | solution.py:23
  1081.0 87.1 %copy-start.116 = (f32[1,1024]{1,0:T(1,128)S(1)}, f32[1,1024]{1,0:T(1,128)}, u32[]{:S(2)}) copy-start(f32[1,1024]{1,0:T(1,128)} %copy-done.115) | copy-start | bytes 12292
  1098.8 69.3 %collective-permute-start.7 = (f32[1024,768]{0,1:T(8,128)}, f32[1024,768]{0,1:T(8,128)S(1)}, u32[]{:S(2)}, u32[]{:S(2)}) collective-permute-start(f32[1024,768]{0,1:T(8,128)} %get-tuple-element.1442), channel_id=1, source_target_pairs={{0,8},{8,0},{16,24},{24,16},{1,9},{9,1},{17,25},{25,17},{2,10},{10... | collective-permute-start | bytes 9437192 | tf_op jit(solution)/shard_map/ppermute | solution.py:23
  1184.6 68.4 %collective-permute-start.8 = (f32[1024,768]{0,1:T(8,128)}, f32[1024,768]{0,1:T(8,128)S(1)}, u32[]{:S(2)}, u32[]{:S(2)}) collective-permute-start(f32[1024,768]{0,1:T(8,128)} %get-tuple-element.1445), channel_id=1, source_target_pairs={{0,8},{8,0},{16,24},{24,16},{1,9},{9,1},{17,25},{25,17},{2,10},{10... | collective-permute-start | bytes 9437192 | tf_op jit(solution)/shard_map/ppermute | solution.py:23
  1258.6 604.1 %collective-permute-start.9 = (f32[1024,768]{0,1:T(8,128)}, f32[1024,768]{0,1:T(8,128)}, u32[]{:S(2)}, u32[]{:S(2)}) collective-permute-start(f32[1024,768]{0,1:T(8,128)} %add_add_fusion.14), channel_id=1, source_target_pairs={{16,0},{24,8},{17,1},{25,9},{18,2},{26,10},{19,3},{27,11},{20,4},{... | collective-permute-start | bytes 9437192 | tf_op jit(solution)/shard_map/ppermute | solution.py:29
  1259.9 602.8 %copy-start.130 = (f32[1,1024]{1,0:T(1,128)S(1)}, f32[1,1024]{1,0:T(1,128)}, u32[]{:S(2)}) copy-start(f32[1,1024]{1,0:T(1,128)} %get-tuple-element.1658) | copy-start | bytes 12292
  1982.2 70.1 %collective-permute-start.10 = (f32[1024,768]{0,1:T(8,128)}, f32[1024,768]{0,1:T(8,128)S(1)}, u32[]{:S(2)}, u32[]{:S(2)}) collective-permute-start(f32[1024,768]{0,1:T(8,128)} %get-tuple-element.1447), channel_id=1, source_target_pairs={{0,8},{8,0},{16,24},{24,16},{1,9},{9,1},{17,25},{25,17},{2,10},{10... | collective-permute-start | bytes 9437192 | tf_op jit(solution)/shard_map/ppermute | solution.py:23
  2280.5 69.2 %collective-permute-start.11 = (f32[1024,768]{0,1:T(8,128)}, f32[1024,768]{0,1:T(8,128)S(1)}, u32[]{:S(2)}, u32[]{:S(2)}) collective-permute-start(f32[1024,768]{0,1:T(8,128)} %get-tuple-element.1450), channel_id=1, source_target_pairs={{0,8},{8,0},{16,24},{24,16},{1,9},{9,1},{17,25},{25,17},{2,10},{10... | collective-permute-start | bytes 9437192 | tf_op jit(solution)/shard_map/ppermute | solution.py:23
  2355.3 138.5 %collective-permute-start.12 = (f32[1024,768]{0,1:T(8,128)}, f32[1024,768]{0,1:T(8,128)}, u32[]{:S(2)}, u32[]{:S(2)}) collective-permute-start(f32[1024,768]{0,1:T(8,128)} %add_add_fusion.12), channel_id=1, source_target_pairs={{16,0},{24,8},{17,1},{25,9},{18,2},{26,10},{19,3},{27,11},{20,4},{... | collective-permute-start | bytes 9437192 | tf_op jit(solution)/shard_map/ppermute | solution.py:29
  2356.6 137.3 %copy-start.128 = (f32[1,1024]{1,0:T(1,128)S(1)}, f32[1,1024]{1,0:T(1,128)}, u32[]{:S(2)}) copy-start(f32[1,1024]{1,0:T(1,128)} %get-tuple-element.1657) | copy-start | bytes 12292
  2613.4 69.9 %collective-permute-start.13 = (f32[1024,768]{0,1:T(8,128)}, f32[1024,768]{0,1:T(8,128)S(1)}, u32[]{:S(2)}, u32[]{:S(2)}) collective-permute-start(f32[1024,768]{0,1:T(8,128)} %get-tuple-element.1452), channel_id=1, source_target_pairs={{0,8},{8,0},{16,24},{24,16},{1,9},{9,1},{17,25},{25,17},{2,10},{10... | collective-permute-start | bytes 9437192 | tf_op jit(solution)/shard_map/ppermute | solution.py:23
  2688.9 223.1 %copy-start.117 = (s32[2048]{0:T(1024)S(1)}, s32[2048]{0:T(1024)}, u32[]{:S(2)}) copy-start(s32[2048]{0:T(1024)} %param.55) | copy-start | bytes 24580
  2911.7 69.0 %collective-permute-start.14 = (f32[1024,768]{0,1:T(8,128)}, f32[1024,768]{0,1:T(8,128)S(1)}, u32[]{:S(2)}, u32[]{:S(2)}) collective-permute-start(f32[1024,768]{0,1:T(8,128)} %get-tuple-element.1455), channel_id=1, source_target_pairs={{0,8},{8,0},{16,24},{24,16},{1,9},{9,1},{17,25},{25,17},{2,10},{10... | collective-permute-start | bytes 9437192 | tf_op jit(solution)/shard_map/ppermute | solution.py:23
  3008.6 205.8 %reduce-scatter.7.cloned.1.call-start = ((), (), s32[]{:S(2)}) async-start(), calls=%async_computation.6 | async-start | bytes 1327104 | tf_op jit(solution)/shard_map/reduce_scatter | solution.py:373
  3011.9 202.5 %reduce-scatter.9.cloned.1.call-start = ((), (), s32[]{:S(2)}) async-start(), calls=%async_computation.7 | async-start | bytes 5308416 | tf_op jit(solution)/shard_map/reduce_scatter | solution.py:377
  3020.7 213.5 %reduce-scatter.11.cloned.1.call-start = ((), (), s32[]{:S(2)}) async-start(), calls=%async_computation.8 | async-start | bytes 5308416 | tf_op jit(solution)/shard_map/reduce_scatter | solution.py:379
  3030.0 256.7 %reduce-scatter.5.cloned.1.call-start = ((), (), s32[]{:S(2)}) async-start(), calls=%async_computation.5 | async-start | bytes 3981312 | tf_op jit(solution)/shard_map/reduce_scatter | solution.py:371
  3030.2 68.1 %collective-permute-start.15 = (f32[1024,768]{0,1:T(8,128)}, f32[1024,768]{0,1:T(8,128)}, u32[]{:S(2)}, u32[]{:S(2)}) collective-permute-start(f32[1024,768]{0,1:T(8,128)} %get-tuple-element.1441), channel_id=1, source_target_pairs={{0,8},{8,0},{16,24},{24,16},{1,9},{9,1},{17,25},{25,17},{2,10},{10... | collective-permute-start | bytes 9437192 | tf_op jit(solution)/shard_map/ppermute | solution.py:23
  3105.5 85.1 %collective-permute-start.16 = (f32[2048,192]{0,1:T(8,128)S(1)}, f32[2048,192]{0,1:T(8,128)}, u32[]{:S(2)}, u32[]{:S(2)}) collective-permute-start(f32[2048,192]{0,1:T(8,128)S(1)} %fusion.567), channel_id=1, source_target_pairs={{0,16},{8,24},{16,0},{24,8},{1,17},{9,25},{17,1},{25,9},{2,18},{10... | collective-permute-start | bytes 4718600 | tf_op jit(solution)/shard_map/ppermute | solution.py:34
  3131.3 58.7 %collective-permute-start.17 = (f32[192]{0:T(256)S(1)}, f32[192]{0:T(256)S(1)}, u32[]{:S(2)}, u32[]{:S(2)}) collective-permute-start(f32[192]{0:T(256)S(1)} %dynamic_slice.148), channel_id=1, source_target_pairs={{0,16},{8,24},{16,0},{24,8},{1,17},{9,25},{17,1},{25,9},{2,18},{10... | collective-permute-start | bytes 2312 | tf_op jit(solution)/shard_map/ppermute | solution.py:34
  3143.0 63.8 %collective-permute-start.18 = (f32[1000,192]{0,1:T(8,128)}, f32[1000,192]{0,1:T(8,128)}, u32[]{:S(2)}, u32[]{:S(2)}) collective-permute-start(f32[1000,192]{0,1:T(8,128)} %copy.415), channel_id=1, source_target_pairs={{0,16},{8,24},{16,0},{24,8},{1,17},{9,25},{17,1},{25,9},{2,18},{10... | collective-permute-start | bytes 2304008 | tf_op jit(solution)/shard_map/ppermute | solution.py:34
  3190.7 96.0 %copy-start.1 = (f32[1000,768]{1,0:T(8,128)S(1)}, f32[1000,768]{1,0:T(8,128)}, u32[]{:S(2)}) copy-start(f32[1000,768]{1,0:T(8,128)} %param.58) | copy-start | bytes 9216004
  (155 other events, 4270.0 us)
Sparse Core Ops, SparseCore 0:
  3008.8 68.6 all-reduce.10
  3081.2 36.8 reduce-scatter.6
  3122.5 53.8 reduce-scatter.8
  3180.3 53.8 reduce-scatter.10
  3238.5 48.0 reduce-scatter.4
where the time goes:
time: 3300 us; the launch traced here: 3290 us
  waiting for transfers between devices  1790 us (54%)
  matrix products  803 us (24%)
  local copies, waits for them, and re-layouts  248 us (8%)
  other arithmetic  196 us (6%)
  starting transfers between devices  165 us (5%)
  loops' own time  51.4 us (2%)
    ppermute x4, waiting for transfers between devices, from_behind(): lax.ppermute(value, axis, [(source, source + steps) for source in range(l...  858 us
    ppermute x12, waiting for transfers between devices, from_partner(): return lax.ppermute(block, axis, route)  801 us
    ppermute x12, starting transfers between devices, from_partner(): return lax.ppermute(block, axis, route)  149 us
    dot_general x2, matrix products, feed_back(): jnp.einsum('ld,fd->lf', grad_rows, down_matrix, precision=PRECISE)  90.2 us
    dot_general x8, matrix products, one_block(): jnp.einsum('qhd,khd->hqk', query_block, key_heads, precision=PRECISE)  85.8 us
    cond x4, matrix products, body(): lax.cond(is_valid, run_feed_back, blank_feed_back, (middle, before, grad_...  78.8 us
    another operation x38, local copies, waits for them, and re-layouts  72.4 us
    dot_general x2, matrix products, feed_half(): jnp.dot(smooth_gate(before), down_matrix, precision=PRECISE) + down_offset  70.7 us
  transfers between devices with their start and end apart: 24, of which 20 were waited for; matrix products, arithmetic and copies ran while one was open for 2% of the time, Pallas kernels for 0%

commit v1 on v0

v1 whole, which is shorter than its diff:
```python
import functools
import math

import jax
import jax.numpy as jnp
from jax import lax
from jax.experimental import pallas as pl
from jax.experimental.pallas import tpu as pltpu
from jax.sharding import PartitionSpec as P

HS = 64
LEN = 1024
EPS = 1e-05
AXES = ("section", "dp")
f32 = jnp.float32
bf16 = jnp.bfloat16

NN = ((1,), (0,))
NT = ((1,), (1,))
TN = ((0,), (0,))
BM = 256
VMEM_LIMIT = 60 * 1024 * 1024


def dot(a, b, dims):
    return lax.dot_general(a, b, (dims, ((), ())), preferred_element_type=f32)


def split(value):
    high = value.astype(bf16)
    return high, (value - high.astype(f32)).astype(bf16)


def dot3(ah, al, bh, bl, dims):
    return dot(ah, bh, dims) + (dot(ah, bl, dims) + dot(al, bh, dims))


def unit_rows(x):
    center = x - jnp.mean(x, axis=-1, keepdims=True)
    scale = lax.rsqrt(jnp.mean(center * center, axis=-1, keepdims=True) + EPS)
    return center * scale, scale


def pull_rows(n, scale, e):
    return (e - jnp.mean(e, axis=-1, keepdims=True) - n * jnp.mean(e * n, axis=-1, keepdims=True)) * scale


class Pieces:
    def __init__(self, entries):
        self.arrays, self.entries = [], []
        for array, *rest in entries:
            index = next((i for i, known in enumerate(self.arrays) if known is array), len(self.arrays))
            if index == len(self.arrays):
                self.arrays.append(array)
            self.entries.append((index, *rest))


def load_split(entries, flags, refs, stage, sems, high_out, low_out):
    quarter = stage.shape[1] // 4
    near = flags[0] == 1
    copies = {"near": [], "far": [], "all": []}
    for number, (index, first, count, slot, place, offset, when) in enumerate(entries):
        row = offset if place is None else pl.multiple_of(flags[1 + place] * quarter + offset, 8)
        copies[when].append(
            pltpu.make_async_copy(
                refs[index].at[pl.ds(first, count)], stage.at[slot, pl.ds(row, count)], sems.at[number]
            )
        )
    for act in ("start", "wait"):

        @pl.when(near)
        def _():
            for copy in copies["near"]:
                getattr(copy, act)()

        @pl.when(jnp.logical_not(near))
        def _():
            for copy in copies["far"]:
                getattr(copy, act)()

        for copy in copies["all"]:
            getattr(copy, act)()
    for slot in range(2):
        high, low = split(stage[slot])
        high_out[slot] = high
        low_out[slot] = low


def store_pieces(flags, read, order, refs):
    split_rows = order == 3
    for number, ref in enumerate(refs):
        send = number % 2 == 0
        along = 1 + number // 2 if split_rows else order
        kinds = ((1, 3) if send else (0, 2)) if along == 1 else ((2, 3) if send else (0, 1))
        count = ref.shape[2]
        for slot in range(2):
            for place, k in enumerate(kinds):
                step = 2 * count if split_rows else count
                row = pl.multiple_of(flags[1 + k] * step + (number // 2) * count, 8)
                ref[place, slot] = read(slot, row, count)


def full(shape):
    zeros = (0,) * len(shape)
    return pl.BlockSpec(shape, lambda i: zeros)


def rows(width, bm=BM):
    return pl.BlockSpec((bm, width), lambda i: (i, 0))


def lanes(height, bm=BM):
    return pl.BlockSpec((height, bm), lambda i: (0, i))


def halves(width, bm=BM):
    first = LEN // bm // 2
    return [
        pl.BlockSpec((bm, width), lambda i: (jnp.minimum(i, first - 1), 0)),
        pl.BlockSpec((bm, width), lambda i: (jnp.maximum(i - first, 0), 0)),
    ]


def read_halves(first, second):
    early = pl.program_id(0) < pl.num_programs(0) // 2
    return jnp.where(early, first[...], second[...])


def write_halves(first, second, value):
    early = pl.program_id(0) < pl.num_programs(0) // 2

    @pl.when(early)
    def _():
        first[...] = value

    @pl.when(jnp.logical_not(early))
    def _():
        second[...] = value


ANY = pl.BlockSpec(memory_space=pl.ANY)
SMEM = pl.BlockSpec(memory_space=pltpu.SMEM)


def call(kernel, grid, in_specs, out_specs, out_shapes, scratch, name, flops, nbytes, *args):
    return pl.pallas_call(
        kernel,
        grid=(grid,),
        in_specs=in_specs,
        out_specs=out_specs,
        out_shape=[jax.ShapeDtypeStruct(s, t) for s, t in out_shapes],
        scratch_shapes=scratch,
        name=name,
        cost_estimate=pl.CostEstimate(flops=int(flops), bytes_accessed=int(nbytes), transcendentals=0),
        compiler_params=pltpu.CompilerParams(
            vmem_limit_bytes=VMEM_LIMIT, dimension_semantics=("arbitrary",)
        ),
    )(*args)


def attn_in_kernel(added, entries, count, flags, *refs):
    base = refs[0]
    refs = refs[1:]
    if added:
        added_refs, refs = refs[:4], refs[4:]
    vec, bias = refs[:2]
    sources, refs = refs[2 : 2 + count], refs[2 + count :]
    if added:
        x_out = refs[0]
        refs = refs[1:]
    nh_out, nl_out, scale_out, ph_out, pl_out, wh_out, wl_out, stage, sems = refs
    inner = 3 * (ph_out.shape[0] // 6)

    @pl.when(pl.program_id(0) == 0)
    def _():
        load_split(entries, flags, sources, stage, sems, wh_out, wl_out)

    x = base[...]
    if added:
        x = x + (read_halves(*added_refs[:2]) + read_halves(*added_refs[2:]))
        x_out[...] = x
    n, scale = unit_rows(x)
    high, low = split(n)
    nh_out[...] = high
    nl_out[...] = low
    scale_out[...] = scale
    third = inner // 3
    for slot in range(2):
        ah, al = split(n * vec[slot, 0:1, :] + vec[slot, 1:2, :])
        projected = dot3(wh_out[slot, :inner], wl_out[slot, :inner], ah, al, NT)
        projected = projected + bias[slot * inner : (slot + 1) * inner]
        queries = projected[:third] * (1.0 / math.sqrt(HS))
        for first, value in ((0, queries), (third, projected[third:])):
            high, low = split(value)
            start = slot * inner + first
            ph_out[start : start + value.shape[0]] = high
            pl_out[start : start + value.shape[0]] = low


def attn_in(flags, x, added, vec, bias, pieces):
    length, width = x.shape
    inner = bias.shape[0] // 2
    outs = [((length, width), f32)] if added else []
    out_specs = [rows(width)] if added else []
    outs += [
        ((length, width), bf16),
        ((length, width), bf16),
        ((length, 1), f32),
        ((2 * inner, length), bf16),
        ((2 * inner, length), bf16),
        ((2, width, width), bf16),
        ((2, width, width), bf16),
    ]
    out_specs += [rows(width), rows(width), rows(1), lanes(2 * inner), lanes(2 * inner)]
    out_specs += [full((2, width, width))] * 2
    in_specs = [SMEM, rows(width)] + halves(width) * (len(added) // 2) + [full(vec.shape), full(bias.shape)]
    in_specs += [ANY] * len(pieces.arrays)
    result = call(
        functools.partial(attn_in_kernel, bool(added), pieces.entries, len(pieces.arrays)),
        length // BM,
        in_specs,
        out_specs,
        outs,
        [pltpu.VMEM((2, width, width), f32), pltpu.SemaphoreType.DMA((len(pieces.entries),))],
        "attn_in",
        6 * length * width * 2 * inner,
        20e6,
        flags, x, *added, vec, bias, *pieces.arrays,
    )
    if not added:
        result = [x] + list(result)
    return result


def heads_kernel(qh, ql, kh, kl, vh, vl, wh, wl, vec, oh_out, ol_out, lse_out, part_a, part_b, oh_all, ol_all):
    head = pl.program_id(0)
    keys = jnp.concatenate([kh[...], kh[...], kl[...]], axis=0)
    values = jnp.concatenate([vh[...], vl[...]], axis=0)
    value_high = vh[...]
    for block in range(qh.shape[1] // BM):
        cut = slice(block * BM, (block + 1) * BM)
        queries = jnp.concatenate([qh[:, cut], ql[:, cut], qh[:, cut]], axis=0)
        scores = dot(keys, queries, TN)
        top = jnp.max(scores, axis=0, keepdims=True)
        weights = jnp.exp(scores - top)
        total = jnp.sum(weights, axis=0, keepdims=True)
        high, low = split(weights)
        both = dot(values, high, NN)
        attended = (both[:HS] + (both[HS:] + dot(value_high, low, NN))) / total
        high, low = split(attended)
        oh_out[:, cut] = high
        ol_out[:, cut] = low
        lse_out[0, :, cut] = top + jnp.log(total)
    place = pl.ds(pl.multiple_of(head * HS, HS), HS)
    oh_all[place, :] = oh_out[...]
    ol_all[place, :] = ol_out[...]

    @pl.when(head == pl.num_programs(0) - 1)
    def _():
        inner, width = oh_all.shape[0], wh.shape[2]
        offset = 0.5 * (vec[0, 3:4, :] + vec[1, 3:4, :])
        for part, cut in ((part_a, slice(0, LEN // 2)), (part_b, slice(LEN // 2, LEN))):
            part[...] = offset + dot3(
                oh_all[:, cut], ol_all[:, cut], wh[...].reshape(inner, width), wl[...].reshape(inner, width), TN
            )


def head_spec(length, which, half_heads):
    return pl.BlockSpec(
        (HS, length), lambda h: (3 * half_heads * (h // half_heads) + which * half_heads + h % half_heads, 0)
    )


def attn_heads(ph, pl_, wh, wl, vec):
    inner2, length = ph.shape
    width = wh.shape[2]
    heads = inner2 // (3 * HS)
    half = heads // 2
    out_rows = half * HS
    specs = []
    for which in range(3):
        specs += [head_spec(length, which, half)] * 2
    tail = pl.BlockSpec((2, out_rows, width), lambda h: (0, width // out_rows - 1, 0))
    return call(
        heads_kernel,
        heads,
        specs + [tail, tail, full(vec.shape)],
        [
            pl.BlockSpec((HS, length), lambda h: (h, 0)),
            pl.BlockSpec((HS, length), lambda h: (h, 0)),
            pl.BlockSpec((1, 1, length), lambda h: (h, 0, 0)),
            full((length // 2, width)),
            full((length // 2, width)),
        ],
        [
            ((heads * HS, length), bf16),
            ((heads * HS, length), bf16),
            ((heads, 1, length), f32),
            ((length // 2, width), f32),
            ((length // 2, width), f32),
        ],
        [pltpu.VMEM((heads * HS, length), bf16)] * 2,
        "attn_heads",
        heads * length * length * HS * 2 * 10,
        15e6,
        ph, pl_, ph, pl_, ph, pl_, wh, wl, vec,
    )


def gate(u):
    phi = 0.5 * (1.0 + lax.erf(u * math.sqrt(0.5)))
    slope = phi + u * (jnp.exp(-0.5 * u * u) * (1.0 / math.sqrt(2.0 * math.pi)))
    return u * phi, slope


def feed_up_kernel(entries, count, flags, base, mine_a, mine_b, other_a, other_b, vec, bias, *refs):
    y_out, nh_out, nl_out, scale_out, hh_out, hl_out, slope_out, uh_out, ul_out, stage, sems = refs[count:]
    hidden = stage.shape[1]

    @pl.when(pl.program_id(0) == 0)
    def _():
        load_split(entries, flags, refs[:count], stage, sems, uh_out, ul_out)

    y = base[...] + (read_halves(mine_a, mine_b) + read_halves(other_a, other_b))
    y_out[...] = y
    n, scale = unit_rows(y)
    high, low = split(n)
    nh_out[...] = high
    nl_out[...] = low
    scale_out[...] = scale
    for slot in range(2):
        ah, al = split(n * vec[slot, 4:5, :] + vec[slot, 5:6, :])
        before = dot3(ah, al, uh_out[slot], ul_out[slot], NT) + bias[slot : slot + 1, :]
        active, slope = gate(before)
        cut = slice(slot * hidden, (slot + 1) * hidden)
        slope_out[:, cut] = slope
        high, low = split(active)
        hh_out[:, cut] = high
        hl_out[:, cut] = low


def feed_up(flags, base, added, vec, bias, pieces):
    length, width = base.shape
    hidden = bias.shape[1]
    weight = ((2, hidden, width), bf16)
    return call(
        functools.partial(feed_up_kernel, pieces.entries, len(pieces.arrays)),
        length // BM,
        [SMEM, rows(width)] + halves(width) * 2 + [full(vec.shape), full(bias.shape)] + [ANY] * len(pieces.arrays),
        [rows(width)] * 3 + [rows(1)] + [rows(2 * hidden)] * 3 + [full(weight[0])] * 2,
        [
            ((length, width), f32),
            ((length, width), bf16),
            ((length, width), bf16),
            ((length, 1), f32),
            ((length, 2 * hidden), bf16),
            ((length, 2 * hidden), bf16),
            ((length, 2 * hidden), f32),
            weight, weight,
        ],
        [pltpu.VMEM((2, hidden, width), f32), pltpu.SemaphoreType.DMA((len(pieces.entries),))],
        "feed_up",
        6 * length * width * 2 * hidden,
        40e6,
        flags, base, *added, vec, bias, *pieces.arrays,
    )


def feed_down_kernel(entries, count, flags, hh, hl, vec, *refs):
    part_a, part_b, dh_out, dl_out, stage, sems = refs[count:]
    hidden = stage.shape[1]

    @pl.when(pl.program_id(0) == 0)
    def _():
        load_split(entries, flags, refs[:count], stage, sems, dh_out, dl_out)

    partial = 0.5 * (vec[0, 6:7, :] + vec[1, 6:7, :])
    for slot in range(2):
        cut = slice(slot * hidden, (slot + 1) * hidden)
        partial = partial + dot3(hh[:, cut], hl[:, cut], dh_out[slot], dl_out[slot], NN)
    write_halves(part_a, part_b, partial)


def feed_down(flags, hh, hl, vec, pieces):
    length, hidden, width = hh.shape[0], hh.shape[1] // 2, vec.shape[2]
    weight = ((2, hidden, width), bf16)
    return call(
        functools.partial(feed_down_kernel, pieces.entries, len(pieces.arrays)),
        length // BM,
        [SMEM] + [rows(2 * hidden)] * 2 + [full(vec.shape)] + [ANY] * len(pieces.arrays),
        halves(width) + [full(weight[0])] * 2,
        [((length // 2, width), f32)] * 2 + [weight, weight],
        [pltpu.VMEM((2, hidden, width), f32), pltpu.SemaphoreType.DMA((len(pieces.entries),))],
        "feed_down",
        6 * length * width * 2 * hidden,
        25e6,
        flags, hh, hl, vec, *pieces.arrays,
    )


def piece_outs(width, order):
    count = 4 if order == 3 else 2
    shape = (2, 2, width // 2 // count, width)
    return [full(shape)] * count, [(shape, f32)] * count


def feed_back_one_kernel(pulled, order, flags, g_in, *refs):
    if pulled:
        added_refs, (nh, nl, scale) = refs[:4], refs[4:7]
        refs = refs[7:]
    (dh, dl, hh, hl, slope, g_out, uh_out, ul_out, *piece_refs, bias_out, total_out, acc) = refs
    step = pl.program_id(0)
    hidden = dh.shape[1]
    g = g_in[...]
    if pulled:
        n = nh[...].astype(f32) + nl[...].astype(f32)
        g = g + pull_rows(n, scale[...], read_halves(*added_refs[:2]) + read_halves(*added_refs[2:]))
    g_out[...] = g

    @pl.when(step == 0)
    def _():
        acc[...] = jnp.zeros_like(acc)
        bias_out[...] = jnp.zeros_like(bias_out)
        total_out[...] = jnp.zeros_like(total_out)

    total_out[...] += jnp.sum(g, axis=0, keepdims=True)
    gh, gl = split(g)
    for slot in range(2):
        cut = slice(slot * hidden, (slot + 1) * hidden)
        delta = dot3(gh, gl, dh[slot], dl[slot], NT) * slope[:, cut]
        bias_out[slot : slot + 1, :] += jnp.sum(delta, axis=0, keepdims=True)
        high, low = split(delta)
        uh_out[:, cut] = high
        ul_out[:, cut] = low
        acc[slot] += dot3(gh, gl, hh[:, cut], hl[:, cut], TN)

    @pl.when(step == pl.num_programs(0) - 1)
    def _():
        store_pieces(flags, lambda slot, row, count: acc[slot, pl.ds(row, count), :], order, piece_refs)


def feed_back_one(order, flags, g, pulled, dh, dl, hh, hl, slope):
    length, width = g.shape
    hidden = dh.shape[1]
    piece_specs, piece_shapes = piece_outs(width, order)
    pulled_specs = halves(width) * 2 + [rows(width)] * 2 + [rows(1)] if pulled else []
    return call(
        functools.partial(feed_back_one_kernel, bool(pulled), order),
        length // BM,
        [SMEM, rows(width)] + pulled_specs + [full(dh.shape)] * 2 + [rows(2 * hidden)] * 3,
        [rows(width)] + [rows(2 * hidden)] * 2 + piece_specs + [full((2, hidden)), full((1, width))],
        [((length, width), f32), ((length, 2 * hidden), bf16), ((length, 2 * hidden), bf16)]
        + piece_shapes
        + [((2, hidden), f32), ((1, width), f32)],
        [pltpu.VMEM((2, width, hidden), f32)],
        "feed_back_one",
        6 * length * width * 4 * hidden,
        40e6,
        flags, g, *pulled, dh, dl, hh, hl, slope,
    )


def feed_back_two_kernel(parts, order, flags, uh, ul, nh, nl, vec, *refs):
    if "e" in parts:
        wh, wl, e_a, e_b, vec_out = refs
    else:
        *piece_refs, acc = refs
    step = pl.program_id(0)
    hidden = uh.shape[1] // 2

    @pl.when(step == 0)
    def _():
        if "e" in parts:
            vec_out[...] = jnp.zeros_like(vec_out)
        else:
            acc[...] = jnp.zeros_like(acc)

    n = nh[...].astype(f32) + nl[...].astype(f32)
    e = None
    for slot in range(2):
        cut = slice(slot * hidden, (slot + 1) * hidden)
        gain = vec[slot, 4:5, :]
        if "e" in parts:
            delta = dot3(uh[:, cut], ul[:, cut], wh[slot], wl[slot], NN)
            vec_out[2 * slot : 2 * slot + 1, :] += jnp.sum(delta * n, axis=0, keepdims=True)
            vec_out[2 * slot + 1 : 2 * slot + 2, :] += jnp.sum(delta, axis=0, keepdims=True)
            e = delta * gain if e is None else e + delta * gain
        else:
            ah, al = split(n * gain + vec[slot, 5:6, :])
            acc[slot] += dot3(uh[:, cut], ul[:, cut], ah, al, TN)
    if "e" in parts:
        write_halves(e_a, e_b, e)
    else:

        @pl.when(step == pl.num_programs(0) - 1)
        def _():
            store_pieces(flags, lambda slot, row, count: acc[slot, pl.ds(row, count), :], order, piece_refs)


def feed_back_two(parts, order, flags, uh, ul, nh, nl, vec, wh, wl):
    length, width = nh.shape
    hidden = wh.shape[1]
    piece_specs, piece_shapes = piece_outs(width, order)
    if parts == "e":
        weights, out_specs = (wh, wl), halves(width) + [full((4, width))]
        out_shapes = [((length // 2, width), f32)] * 2 + [((4, width), f32)]
    else:
        weights, out_specs, out_shapes = (), piece_specs, piece_shapes
    return call(
        functools.partial(feed_back_two_kernel, parts, order),
        length // BM,
        [SMEM] + [rows(2 * hidden)] * 2 + [rows(width)] * 2 + [full(vec.shape)] + [full(w.shape) for w in weights],
        out_specs,
        out_shapes,
        [pltpu.VMEM((2, hidden, width), f32)] if parts == "w" else [],
        "feed_back_two_" + parts,
        6 * length * width * 2 * hidden,
        25e6,
        flags, uh, ul, nh, nl, vec, *weights,
    )


def attn_back_one_kernel(
    g_in, mine_a, mine_b, other_a, other_b, nh, nl, scale, wh, wl, oh, ol, g_out, dh_out, dl_out, do_out, total_out
):
    step = pl.program_id(0)
    inner, width = oh.shape[0], g_in.shape[1]

    @pl.when(step == 0)
    def _():
        do_out[...] = jnp.zeros_like(do_out)
        total_out[...] = jnp.zeros_like(total_out)

    n = nh[...].astype(f32) + nl[...].astype(f32)
    g = g_in[...] + pull_rows(n, scale[...], read_halves(mine_a, mine_b) + read_halves(other_a, other_b))
    g_out[...] = g
    total_out[...] += jnp.sum(g, axis=0, keepdims=True)
    gh, gl = split(g)
    delta = dot3(wh[...].reshape(inner, width), wl[...].reshape(inner, width), gh, gl, NT)
    high, low = split(delta)
    dh_out[...] = high
    dl_out[...] = low
    do_out[...] += dot3(oh[...], ol[...], gh, gl, NN)


def attn_back_one(g, added, nh, nl, scale, wh, wl, oh, ol):
    length, width = g.shape
    inner = oh.shape[0]
    out_rows = inner // 2
    tail = pl.BlockSpec((2, out_rows, width), lambda i: (0, width // out_rows - 1, 0))
    return call(
        attn_back_one_kernel,
        length // BM,
        [rows(width)] + halves(width) * 2 + [rows(width)] * 2 + [rows(1)] + [tail, tail] + [lanes(inner)] * 2,
        [rows(width), lanes(inner), lanes(inner), full((inner, width)), full((1, width))],
        [
            ((length, width), f32),
            ((inner, length), bf16),
            ((inner, length), bf16),
            ((inner, width), f32),
            ((1, width), f32),
        ],
        [],
        "attn_back_one",
        6 * length * width * 2 * inner,
        20e6,
        g, *added, nh, nl, scale, wh, wl, oh, ol,
    )


def heads_back_kernel(qh, ql, kh, kl, vh, vl, dh, dl, oh, ol, lse, dqh, dql, dkh, dkl, dvh, dvl, acc_k, acc_v):
    keys = jnp.concatenate([kh[...], kh[...], kl[...]], axis=0)
    keys_two = jnp.concatenate([kh[...], kl[...]], axis=0)
    values = jnp.concatenate([vh[...], vh[...], vl[...]], axis=0)
    key_high = kh[...]
    for block in range(qh.shape[1] // BM):
        cut = slice(block * BM, (block + 1) * BM)
        q_high, q_low = qh[:, cut], ql[:, cut]
        d_high, d_low = dh[:, cut], dl[:, cut]
        delta = d_high.astype(f32) + d_low.astype(f32)
        attended = oh[:, cut].astype(f32) + ol[:, cut].astype(f32)
        diagonal = jnp.sum(delta * attended, axis=0, keepdims=True)
        scores = dot(keys, jnp.concatenate([q_high, q_low, q_high], axis=0), TN)
        probs = jnp.exp(scores - lse[0, :, cut])
        p_high, p_low = split(probs)
        delta_probs = dot(values, jnp.concatenate([d_high, d_low, d_high], axis=0), TN)
        delta_scores = probs * (delta_probs - diagonal)
        s_high, s_low = split(delta_scores)
        both = dot(jnp.concatenate([d_high, d_low], axis=0), p_high, NT)
        part_v = both[:HS] + (both[HS:] + dot(d_high, p_low, NT))
        both = dot(jnp.concatenate([q_high, q_low], axis=0), s_high, NT)
        part_k = both[:HS] + (both[HS:] + dot(q_high, s_low, NT))
        if block == 0:
            acc_v[...] = part_v
            acc_k[...] = part_k
        else:
            acc_v[...] += part_v
            acc_k[...] += part_k
        both = dot(keys_two, s_high, NN)
        delta_q = (both[:HS] + (both[HS:] + dot(key_high, s_low, NN))) * (1.0 / math.sqrt(HS))
        high, low = split(delta_q)
        dqh[:, cut] = high
        dql[:, cut] = low
    high, low = split(acc_k[...])
    dkh[...] = high
    dkl[...] = low
    high, low = split(acc_v[...])
    dvh[...] = high
    dvl[...] = low


def attn_heads_back(ph, pl_, dh, dl, oh, ol, lse):
    inner2, length = ph.shape
    heads = inner2 // (3 * HS)
    half = heads // 2
    specs = []
    for which in range(3):
        specs += [head_spec(length, which, half)] * 2
    plain = pl.BlockSpec((HS, length), lambda h: (h, 0))
    return call(
        heads_back_kernel,
        heads,
        specs + [plain] * 4 + [pl.BlockSpec((1, 1, length), lambda h: (h, 0, 0))],
        [plain] * 6,
        [((heads * HS, length), bf16)] * 6,
        [pltpu.VMEM((HS, length), f32)] * 2,
        "attn_heads_back",
        heads * length * length * HS * 2 * 26,
        15e6,
        ph, pl_, ph, pl_, ph, pl_, dh, dl, oh, ol, lse,
    )


def attn_back_two_kernel(parts, order, flags, *refs):
    dqh, dql, dkh, dkl, dvh, dvl, nh, nl, vec = refs[:9]
    refs = refs[9:]
    if "e" in parts:
        (wh, wl), refs = refs[:2], refs[2:]
    if "w" in parts:
        do, refs = refs[0], refs[1:]
    if "e" in parts:
        (e_a, e_b, vec_out), refs = refs[:3], refs[3:]
    if "w" in parts:
        *piece_refs, pair_out, acc, turned = refs
    step = pl.program_id(0)
    third = dqh.shape[0] // 2
    inner = 3 * third

    @pl.when(step == 0)
    def _():
        if "e" in parts:
            vec_out[...] = jnp.zeros_like(vec_out)
        if "w" in parts:
            acc[...] = jnp.zeros_like(acc)
            pair_out[...] = jnp.zeros_like(pair_out)

    n = nh[...].astype(f32) + nl[...].astype(f32)
    ones = jnp.ones((8, n.shape[0]), bf16)
    e = None
    for slot in range(2):
        cut = slice(slot * third, (slot + 1) * third)
        high = jnp.concatenate([dqh[cut], dkh[cut], dvh[cut]], axis=0)
        low = jnp.concatenate([dql[cut], dkl[cut], dvl[cut]], axis=0)
        gain = vec[slot, 0:1, :]
        if "w" in parts:
            ah, al = split(n * gain + vec[slot, 1:2, :])
            acc[slot] += dot3(high, low, ah, al, NN)
            pair_out[slot] += dot(ones, high, NT) + dot(ones, low, NT)
        if "e" in parts:
            delta = dot3(high, low, wh[slot, :inner], wl[slot, :inner], TN)
            vec_out[2 * slot : 2 * slot + 1, :] += jnp.sum(delta * n, axis=0, keepdims=True)
            vec_out[2 * slot + 1 : 2 * slot + 2, :] += jnp.sum(delta, axis=0, keepdims=True)
            e = delta * gain if e is None else e + delta * gain
    if "e" in parts:
        write_halves(e_a, e_b, e)

    if "w" in parts:

        @pl.when(step == pl.num_programs(0) - 1)
        def _():
            for slot in range(2):
                whole = jnp.concatenate([acc[slot], do[slot * third : (slot + 1) * third]], axis=0)
                turned[slot] = jnp.transpose(whole)
            store_pieces(flags, lambda slot, row, count: turned[slot, pl.ds(row, count), :], order, piece_refs)


def attn_back_two(parts, order, flags, grads, nh, nl, vec, wh, wl, do):
    length, width = nh.shape
    heads_rows = grads[0].shape[0]
    inner = 3 * heads_rows // 2
    piece_specs, piece_shapes = piece_outs(width, order)
    in_specs = [SMEM] + [lanes(heads_rows)] * 6 + [rows(width)] * 2 + [full(vec.shape)]
    args = [flags, *grads, nh, nl, vec]
    out_specs, out_shapes, scratch = [], [], []
    if "e" in parts:
        in_specs += [full(wh.shape)] * 2
        args += [wh, wl]
        out_specs += halves(width) + [full((4, width))]
        out_shapes += [((length // 2, width), f32)] * 2 + [((4, width), f32)]
    if "w" in parts:
        in_specs += [full(do.shape)]
        args += [do]
        out_specs += piece_specs + [full((2, 8, inner))]
        out_shapes += piece_shapes + [((2, 8, inner), f32)]
        scratch = [pltpu.VMEM((2, inner, width), f32), pltpu.VMEM((2, width, width), f32)]
    return call(
        functools.partial(attn_back_two_kernel, parts, order),
        length // BM,
        in_specs,
        out_specs,
        out_shapes,
        scratch,
        "attn_back_two_" + parts,
        6 * length * width * 2 * inner * len(parts),
        15e6 * len(parts),
        *args,
    )


def finish_kernel(g_in, mine_a, mine_b, other_a, other_b, nh, nl, scale, mask, grad_out, sums_out):
    @pl.when(pl.program_id(0) == 0)
    def _():
        sums_out[...] = jnp.zeros_like(sums_out)

    n = nh[...].astype(f32) + nl[...].astype(f32)
    g = g_in[...] + pull_rows(n, scale[...], read_halves(mine_a, mine_b) + read_halves(other_a, other_b))
    absorbed = mask[...]
    grad_out[...] = g * (1.0 - absorbed)
    sums_out[...] += jnp.sum(g * absorbed, axis=0, keepdims=True)


def finish(g, added, nh, nl, scale, mask):
    length, width = g.shape
    return call(
        finish_kernel,
        length // BM,
        [rows(width)] + halves(width) * 2 + [rows(width)] * 2 + [rows(1)] * 2,
        [rows(width), full((1, width))],
        [((length, width), f32), ((1, width), f32)],
        [],
        "finish",
        10 * length * width,
        15e6,
        g, *added, nh, nl, scale, mask,
    )


VEC_ROWS = 10


def pack_kernel(columns, flags, *refs):
    table = refs[-1]
    row_sum = refs[-2]
    width = row_sum.shape[1]
    odd, core, sequence = flags[0], flags[1], flags[2]
    table[...] = jnp.zeros_like(table)

    def place(parts):
        zero = jnp.zeros_like(parts[0])
        first = jnp.concatenate([v for p in parts for v in (p, zero)], axis=1)
        second = jnp.concatenate([v for p in parts for v in (zero, p)], axis=1)
        return jnp.where(core == 0, first, second)

    for layer in range(2):
        attn_vec, pair_sum, out_total, ffn_vec, up_sum, down_total = refs[6 * layer : 6 * layer + 6]
        third = pair_sum.shape[2] // 3
        block = up_sum.shape[1] // columns
        for slot in range(2):
            section = 2 * layer + jnp.where(odd == 1, 1 - slot, slot)
            base = section * VEC_ROWS

            def put(row, value):
                table[pl.ds(base + row, 1), :] = value

            put(0, attn_vec[2 * slot : 2 * slot + 1, :])
            put(1, attn_vec[2 * slot + 1 : 2 * slot + 2, :])
            pair = pair_sum[slot, 0:1, :]
            put(2, place([pair[:, :third], pair[:, 2 * third :]]))
            put(3, 0.5 * out_total[...])
            put(4, ffn_vec[2 * slot : 2 * slot + 1, :])
            put(5, ffn_vec[2 * slot + 1 : 2 * slot + 2, :])
            put(6, 0.5 * down_total[...])
            ups = up_sum[slot : slot + 1, :]
            spread = place([ups[:, k * block : (k + 1) * block] for k in range(columns)])
            for k in range(spread.shape[1] // width):
                put(7 + k, spread[:, k * width : (k + 1) * width])
    table[pl.ds(4 * VEC_ROWS + sequence, 1), :] = 0.5 * row_sum[...]


def pack(flags, small, row_sum, columns, sequences):
    width = row_sum.shape[1]
    arrays = [*small[0], *small[1], row_sum]
    count = -(-(4 * VEC_ROWS + sequences) // 8) * 8
    return call(
        functools.partial(pack_kernel, columns),
        1,
        [SMEM] + [full(v.shape) for v in arrays],
        [full((count, width))],
        [((count, width), f32)],
        [],
        "pack",
        1e4,
        1e6,
        flags, *arrays,
    )[0]


def after(value, *others):
    return lax.optimization_barrier((value, *others))[0]


class Plan:
    def __init__(self, planes, dp):
        self.planes, self.dp, self.columns = planes, dp, dp // 2
        self.z = lax.axis_index("section")
        device = lax.axis_index("dp")
        self.column, self.core = device // 2, device % 2

    def permute(self, value, target):
        pairs = []
        for z in range(self.planes):
            for d in range(self.dp):
                to = target(z, d)
                if to is not None:
                    pairs.append((z * self.dp + d, to[0] * self.dp + to[1]))
        return lax.ppermute(value, AXES, pairs)

    def groups(self):
        return [
            [z * self.dp + 2 * j + c for j in range(self.columns)] for z in range(self.planes) for c in range(2)
        ]

    def across(self, value):
        return self.permute(value, lambda z, d: (z, d ^ 1))

    def added(self, first, second):
        return (first, second, self.across(first), self.across(second))

    def along_z(self, value, bit, planes=None):
        return self.permute(value, lambda z, d: (z ^ bit, d) if planes is None or z in planes else None)

    def in_plane(self, value, bit):
        return self.permute(value, lambda z, d: (z, d ^ (2 * bit)))

    def whole(self, shard):
        return lax.all_gather(shard, AXES, axis_index_groups=self.groups(), axis=0, tiled=True)

    def all_sum(self, table):
        if self.columns == 4:
            for step in (self.across, *[functools.partial(self.in_plane, bit=b) for b in (1, 2)]):
                table = table + step(table)
            for bit in (1, 2):
                table = table + self.along_z(table, bit)
            return table
        return lax.psum(table, AXES)


class Group:
    def __init__(self, plan, shard, order):
        self.plan, self.shard, self.order = plan, shard, order
        if plan.columns == 4:
            self.got = plan.in_plane(shard, order)

    def step(self, *others):
        if self.plan.columns != 4:
            return self.shard
        self.kept = after(self.got, *others)
        on = jnp.concatenate([self.shard, self.kept])
        self.last = self.plan.in_plane(on, 3 - self.order)
        return on

    def pieces(self, first, count, slot, offset, when):
        if self.plan.columns != 4:
            whole = self.plan.whole(self.shard[first : first + count])
            return [(whole, 0, whole.shape[0], slot, None, 0, when)]
        rows_all = self.shard.shape[0]
        near, far = (1, 2) if self.order == 1 else (2, 1)
        return [
            (self.shard, first, count, slot, 0, offset, when),
            (self.kept, first, count, slot, near, offset, when),
            (self.last, first, count, slot, far, offset, when),
            (self.last, rows_all + first, count, slot, 3, offset, when),
        ]


class Sum:
    def __init__(self, plan, layer, order, pieces):
        self.plan, self.layer, self.stage = plan, layer, 0
        self.ways = [1, 2] if order == 3 else [order]
        self.send, self.keep = pieces[0::2], pieces[1::2]
        if plan.columns == 4:
            self.got = [plan.in_plane(v, way) for v, way in zip(self.send, self.ways)]
        else:
            parts = []
            for k in range(4):
                for send, keep, way in zip(self.send, self.keep, self.ways):
                    kinds = ((0, 2), (1, 3)) if way == 1 else ((0, 1), (2, 3))
                    parts.append(keep[kinds[0].index(k)] if k in kinds[0] else send[kinds[1].index(k)])
            whole = jnp.concatenate(parts, axis=1)
            self.done = [
                lax.psum_scatter(whole, AXES, axis_index_groups=plan.groups(), scatter_dimension=1, tiled=True)
            ]
            self.stage = 1

    def advance(self, *others):
        plan = self.plan
        if self.stage == 4:
            return ()
        self.stage += 1
        if self.stage == 1:
            got = [after(v, *others) for v in self.got]
            self.mine = [k[0] + v[0] for k, v in zip(self.keep, got)]
            on = [k[1] + v[1] for k, v in zip(self.keep, got)]
            self.got = [plan.in_plane(v, 3 - way) for v, way in zip(on, self.ways)]
            return on
        if self.stage == 2:
            if plan.columns == 4:
                got = [after(v, *others) for v in self.got]
                opposite = [m[1] + v[1] for m, v in zip(self.mine, got)]
                par = [m[0] + v[0] for m, v in zip(self.mine, got)]
            else:
                opposite, par = [v[1] for v in self.done], [v[0] for v in self.done]
            opposite = jnp.concatenate(opposite)
            self.par = jnp.concatenate(par)
            self.got = plan.along_z(opposite, 1)
            return (opposite,)
        if self.stage == 3:
            self.par = self.par + after(self.got, *others)
            far = (0, 1) if self.layer == 1 else (2, 3)
            self.got = plan.along_z(self.par, 2, far)
            return (self.par,)
        self.par = self.par + after(self.got, *others)
        return (self.par,)

    def finish(self):
        while self.stage < 4:
            self.advance()
        return self.par


def body(
    tokens, absorbed, timesteps, mask_embedding, time_table,
    attn_gain, attn_shift, joint_weight, pair_bias, out_weight, out_bias,
    ffn_gain, ffn_shift, up_weight, up_bias, down_weight, down_bias, cotangent,
):
    plan = Plan(lax.axis_size("section"), lax.axis_size("dp"))
    z, column, core = plan.z, plan.column, plan.core
    columns = plan.columns
    width = tokens.shape[1]
    inner = out_weight.shape[1]
    hidden = up_weight.shape[2]
    inner_half, hidden_half = inner // 2, hidden // 2
    block = hidden_half // columns
    low_planes = z < 2

    joint_half = lax.dynamic_index_in_dim(joint_weight[0].reshape(width, 3, 2, inner_half), core, 2, keepdims=False)
    joint_half = joint_half.reshape(width, 3 * inner_half).T
    out_half = lax.dynamic_slice_in_dim(out_weight[0], core * inner_half, inner_half, 0)
    own_attn = jnp.concatenate([joint_half, out_half], axis=0)
    up_half = lax.dynamic_index_in_dim(up_weight[0].reshape(width, columns, 2, block), core, 2, keepdims=False)
    own_up = up_half.reshape(width, hidden_half).T
    down_half = lax.dynamic_index_in_dim(down_weight[0].reshape(columns, 2, block, width), core, 1, keepdims=False)
    own_down = down_half.reshape(hidden_half, width)
    own = (own_attn, own_up, own_down)

    own_vec = jnp.stack(
        [attn_gain[0], attn_shift[0], pair_bias[0], out_bias[0], ffn_gain[0], ffn_shift[0], down_bias[0]]
        + [up_bias[0, k * width : (k + 1) * width] for k in range(hidden // width)]
    )
    vec_count = own_vec.shape[0]
    count = width // columns

    def shard_of(matrix):
        return lax.dynamic_slice_in_dim(matrix, column * count, count, 0)

    tail = jnp.zeros((-vec_count % 8, width), f32)
    shards = [jnp.concatenate([shard_of(own[0]), own_vec, tail]), shard_of(own[1]), shard_of(own[2])]
    far, far_opp = [], []
    for shard in shards:
        far.append(plan.along_z(after(shard, *far[-1:]), 2))
    near_attn = plan.along_z(shards[0], 1)
    far_opp.append(plan.along_z(far[0], 1))
    near_feed = plan.along_z(after(jnp.concatenate(shards[1:]), far_opp[0]), 1)
    near_opp = (near_attn, near_feed[:count], near_feed[count:])
    far_opp += [plan.along_z(far[1], 1), plan.along_z(far[2], 1)]
    opp = [
        [jnp.where(low_planes == (layer == 0), near_opp[k], far_opp[k]) for k in range(3)] for layer in range(2)
    ]

    near_vec = jnp.stack([own_vec, near_attn[count : count + vec_count]])
    far_vec = jnp.stack([far[0][count : count + vec_count], far_opp[0][count : count + vec_count]])
    vectors = jnp.stack([jnp.where(low_planes, near_vec, far_vec), jnp.where(low_planes, far_vec, near_vec)])
    pair_all = lax.dynamic_index_in_dim(vectors[:, :, 2].reshape(2, 2, 2, 2, inner_half), core, 3, keepdims=False)
    pair_rows = jnp.stack([pair_all[:, :, 0], jnp.zeros_like(pair_all[:, :, 0]), pair_all[:, :, 1]], axis=2)
    pair_cols = pair_rows.reshape(2, 2 * 3 * inner_half, 1)
    up_rows = lax.dynamic_index_in_dim(
        vectors[:, :, 7:].reshape(2, 2, columns, 2, block), core, 3, keepdims=False
    ).reshape(2, 2, hidden_half)

    natural = jnp.arange(4, dtype=jnp.int32)
    order = column ^ natural if columns == 4 else natural
    flags = [
        jnp.concatenate([(low_planes == (layer == 0)).astype(jnp.int32)[None], order.astype(jnp.int32)])
        for layer in range(2)
    ]

    local = core == z // 2
    which = z % 2

    def fetch(array):
        piece = lax.dynamic_slice_in_dim(array, which * LEN, LEN, 0)
        other = plan.permute(piece, lambda zz, d: (zz, d ^ 1) if d % 2 == zz // 2 else None)
        return jnp.where(local, piece, other)

    absorbed, tokens, cotangent = (after(v, far[0]) for v in (absorbed, tokens, cotangent))
    mask_row = fetch(absorbed).astype(f32)
    sequence = 4 * column + z
    step = lax.dynamic_index_in_dim(timesteps, sequence, 0, keepdims=False)
    step_row = lax.dynamic_slice_in_dim(time_table, step, 1, 0)
    mask = mask_row[:, None]
    x = jnp.where(mask > 0.5, mask_embedding[None, :] + step_row, fetch(tokens))
    weight = LEN / jnp.maximum(jnp.sum(mask_row), 1.0)
    g = fetch(cotangent) * (mask * weight)

    half = count // 2
    far_group, near_group = Group(plan, far[0], 1), Group(plan, near_attn, 2)
    rest = [Group(plan, far_opp[0][:half], 1), Group(plan, far_opp[0][half:count], 2)]
    for group in (far_group, near_group, *rest):
        group.step()
    ups = Group(plan, jnp.concatenate([far[1], opp[0][1]]), 1)
    downs = Group(plan, jnp.concatenate([far[2], opp[0][2]]), 2)
    lasts = Group(plan, jnp.concatenate([opp[1][1], opp[1][2]]), 1)

    def own_rows(matrix):
        return [(matrix, 0, matrix.shape[0], 0, None, 0, "near")]

    attn_pieces = Pieces(
        own_rows(own[0])
        + far_group.pieces(0, count, 0, 0, "far")
        + near_group.pieces(0, count, 1, 0, "near")
        + (
            rest[0].pieces(0, half, 1, 0, "far") + rest[1].pieces(0, half, 1, half, "far")
            if columns == 4
            else [(plan.whole(far_opp[0][:count]), 0, width, 1, None, 0, "far")]
        )
    )

    kept = []
    added = ()
    for layer in range(2):
        vec = vectors[layer]
        if layer == 0:
            x = after(x, g, ups.shard)
        x, xh, xl, x_scale, ph, pl_, wh, wl = attn_in(flags[layer], x, added, vec, pair_cols[layer], attn_pieces)
        if layer == 0:
            ph = after(ph, downs.shard, ups.step(ph))
        oh, ol, lse, *part = attn_heads(ph, pl_, wh, wl, vec)
        if layer == 0:
            part[0] = after(part[0], downs.step(part[0]))
            up_opp, down_opp = ups.pieces(count, count, 1, 0, "all"), downs.pieces(count, count, 1, 0, "all")
        else:
            up_opp, down_opp = lasts.pieces(0, count, 1, 0, "all"), lasts.pieces(count, count, 1, 0, "all")
        up_pieces = Pieces(own_rows(own[1]) + ups.pieces(0, count, 0, 0, "far") + up_opp)
        y, yh, yl, y_scale, hh, hl, slope, uh, ul = feed_up(
            flags[layer], x, plan.added(*part), vec, up_rows[layer], up_pieces
        )
        down_pieces = Pieces(own_rows(own[2]) + downs.pieces(0, count, 0, 0, "far") + down_opp)
        *feed_part, dh, dl = feed_down(flags[layer], hh, hl, vec, down_pieces)
        if layer == 0:
            feed_part[0] = after(feed_part[0], lasts.step(feed_part[0]))
        kept.append((vec, xh, xl, x_scale, ph, pl_, wh, wl, oh, ol, lse, yh, yl, y_scale, hh, hl, slope, uh, ul, dh, dl))
        added = plan.added(*feed_part)
        x = y
    last = (x, *added)

    quarter = width // plan.planes

    def spread(value):
        def cut(plane):
            cols = lax.dynamic_slice_in_dim(value, plane * quarter, quarter, 1)
            return jnp.concatenate([cols[: LEN // 2], cols[LEN // 2 :]], axis=1)

        def open_up(packed):
            return jnp.concatenate([packed[:, :quarter], packed[:, quarter:]], axis=0)

        arrived = [cut(z)]
        for step in range(1, plan.planes):
            arrived.append(
                plan.permute(cut(z ^ step), lambda zz, d: (zz ^ step, d) if d % 2 == zz // 2 else None)
            )
        result = []
        for index in range(2):
            distance = z ^ (2 * core + index)
            result.append(open_up(lax.select_n(distance, *arrived)))
        return jnp.concatenate(result, axis=0)

    def steps(token, *numbers):
        return [v for number in numbers for v in sums[number].advance(token)]

    pulled = ()
    small = [None] * 2
    sums = []
    for layer in (1, 0):
        (vec, xh, xl, x_scale, ph, pl_, wh, wl, oh, ol, lse, yh, yl, y_scale, hh, hl, slope, uh, ul, dh, dl) = kept[layer]
        order = 1 if layer == 1 else 2
        g, duh, dul, *pieces, up_bias_sum, down_bias_sum = feed_back_one(
            order, flags[layer], g, pulled, dh, dl, hh, hl, slope
        )
        sums.append(Sum(plan, layer, order, pieces))
        if layer == 1:
            final = after(last[0], up_bias_sum) + jnp.concatenate([last[1] + last[3], last[2] + last[4]])
            out_rows = spread(final)
        else:
            duh = after(duh, *steps(up_bias_sum, 0, 1))
        *e, ffn_vec = feed_back_two("e", 0, flags[layer], duh, dul, yh, yl, vec, uh, ul)
        e = plan.added(*e)
        duh = after(duh, ffn_vec)
        if layer == 0:
            duh = after(duh, *steps(ffn_vec, 2))
        pieces = feed_back_two("w", 3 - order, flags[layer], duh, dul, yh, yl, vec, uh, ul)
        sums.append(Sum(plan, layer, 3 - order, pieces))
        g, e = after(g, pieces[0]), (*e[:2], after(e[2], pieces[0]), after(e[3], pieces[0]))
        if layer == 0:
            g = after(g, *steps(pieces[0], 1, 2))
        g, doh, dol, do, out_bias_sum = attn_back_one(g, e, yh, yl, y_scale, wh, wl, oh, ol)
        grads = attn_heads_back(ph, pl_, doh, dol, oh, ol, lse)
        if layer == 1:
            do, first = after(do, *steps(grads[0], 0, 1)), after(grads[0], out_rows)
            *e, attn_vec = attn_back_two("e", 0, flags[layer], [first, *grads[1:]], xh, xl, vec, wh, wl, do)
            e = plan.added(*e)
            do = after(do, *steps(attn_vec, 0))
            *pieces, pair_sum = attn_back_two("w", order, flags[layer], grads, xh, xl, vec, wh, wl, do)
            sums.append(Sum(plan, layer, order, pieces))
            g = after(g, pair_sum, *steps(pair_sum, 0, 1))
            e = (*e[:2], after(e[2], pair_sum), after(e[3], pair_sum))
        else:
            do = after(do, *steps(grads[0], 2, 3, 4))
            *pieces, pair_sum = attn_back_two("w", 3, flags[layer], grads, xh, xl, vec, wh, wl, do)
            sums.append(Sum(plan, layer, 3, pieces))
            first = after(grads[0], *steps(pair_sum, 3))
            *e, attn_vec = attn_back_two("e", 0, flags[layer], [first, *grads[1:]], xh, xl, vec, wh, wl, do)
            e = plan.added(*e)
        pulled = (*e, xh, xl, x_scale)
        small[layer] = (attn_vec, pair_sum, out_bias_sum, ffn_vec, up_bias_sum, down_bias_sum)
    input_grad, row_sum = finish(g, pulled[:4], *pulled[4:], mask)
    grad_rows = spread(input_grad)

    pack_flags = jnp.stack([z % 2, core, sequence]).astype(jnp.int32)
    table = plan.all_sum(pack(pack_flags, small, row_sum, columns, timesteps.shape[0]))

    def settle(index):
        return jnp.where(low_planes, sums[3 + index].finish(), sums[index].finish())

    down_mine, up_mine, attn_mine = (settle(index) for index in range(3))

    def exchange(rows_all):
        halves = rows_all.reshape(2, -1, width)
        mine = lax.dynamic_index_in_dim(halves, core, 0, keepdims=False)
        theirs = plan.across(lax.dynamic_index_in_dim(halves, 1 - core, 0, keepdims=False))
        first = core == 0
        return jnp.where(first, mine, theirs), jnp.where(first, theirs, mine)

    zero, one = exchange(attn_mine)
    count = zero.shape[0]
    joint = jnp.stack([v[:, : 3 * inner_half].reshape(count, 3, inner_half) for v in (zero, one)], axis=2)
    joint_grad = joint.reshape(count, 3 * inner)
    out_grad = jnp.concatenate([zero[:, 3 * inner_half :], one[:, 3 * inner_half :]], axis=1).T
    zero, one = exchange(down_mine)
    down_grad = jnp.stack([v.reshape(count, columns, block) for v in (zero, one)], axis=2).reshape(count, hidden).T
    up_grad = up_mine.reshape(-1, width).T

    mine = lax.dynamic_slice_in_dim(table, VEC_ROWS * z, VEC_ROWS, 0)
    device = 2 * column + core
    share = lax.dynamic_slice_in_dim(mine, device * (width // plan.dp), width // plan.dp, 1)
    up_count = hidden // width
    up_share = lax.dynamic_slice_in_dim(
        mine[7 : 7 + up_count].reshape(-1), device * (hidden // plan.dp), hidden // plan.dp, 0
    )

    seq_rows = table[4 * VEC_ROWS : 4 * VEC_ROWS + timesteps.shape[0]]
    seq_cols = lax.dynamic_slice_in_dim(seq_rows, z * quarter, quarter, 1)
    picks = (timesteps[:, None] == jnp.arange(time_table.shape[0], dtype=jnp.int32)[None, :]).astype(f32)
    table_grad = jnp.einsum("st,sd->td", picks, seq_cols, precision=lax.Precision.HIGHEST)
    mask_grad = jnp.sum(seq_cols, axis=0)

    return (
        out_rows,
        grad_rows,
        mask_grad,
        table_grad,
        share[0:1],
        share[1:2],
        joint_grad[None],
        share[2:3],
        out_grad[None],
        share[3:4],
        share[4:5],
        share[5:6],
        up_grad[None],
        up_share[None],
        down_grad[None],
        share[6:7],
    )


def solution(mesh):
    placed = (
        P("dp", None), P("dp"), P(), P(), P(),
        P("section", None), P("section", None), P("section", None, None), P("section", None),
        P("section", None, None), P("section", None), P("section", None), P("section", None),
        P("section", None, None), P("section", None), P("section", None, None), P("section", None),
        P("dp", None),
    )
    vector = P("section", "dp")
    return jax.shard_map(
        body,
        mesh=mesh,
        in_specs=placed,
        out_specs=(
            P("dp", "section"), P("dp", "section"), P("section"), P(None, "section"),
            vector, vector, P("section", "dp", None), vector, P("section", None, "dp"), vector,
            vector, vector, P("section", None, "dp"), vector, P("section", None, "dp"), vector,
        ),
        check_vma=False,
    )
```

time: 3300 us -> 960 us (0.29)
  waiting for transfers between devices: 1790 us -> 279 us
  matrix products: 803 us -> 1.47 us
  Pallas kernels: 0 us -> 389 us
  local copies, waits for them, and re-layouts: 248 us -> 68.7 us
  other arithmetic: 196 us -> 104 us
  starting transfers between devices: 165 us -> 105 us
  loops' own time: 51.4 us -> 0 us
    ppermute x19 -> x80, waiting for transfers between devices: 1720 us -> 279 us  [permute(): return lax.ppermute(value, AXES, pairs)]
    dot_general x48 -> x1, matrix products: 709 us -> 1.47 us  [body(): jnp.einsum('st,sd->td', picks, seq_cols, precision=lax.Precision.HIGHEST)]
    pallas_call x0 -> x24, Pallas kernels: none -> 389 us  [call(): pl.pallas_call(kernel, grid=(grid,), in_specs=in_specs, out_specs=out_spe...]
    cond x6 -> x0, matrix products: 93.9 us -> none  [the longest x4 78.8 us: body(): lax.cond(is_valid, run_feed_back, blank_feed_back, (middle, before, grad_...]
    reduce_scatter x4 -> x0, waiting for transfers between devices: 72.2 us -> none  [the longest x1 52.4 us: body(): lax.psum_scatter(joint_term, 'dp', scatter_dimension=0, tiled=True)]
    another operation x38 -> x9, local copies, waits for them, and re-layouts: 72.4 us -> 6.64 us  [the longest x2 2.1 us: body(): jnp.stack([far[0][count:count + vec_count], far_opp[0][count:count + vec_...]
    ppermute x19 -> x80, starting transfers between devices: 165 us -> 105 us  [permute(): return lax.ppermute(value, AXES, pairs)]
    reduce_sum x36 -> x2, other arithmetic: 54.8 us -> 1.25 us  [the longest x1 0.65 us: body(): mask_grad = jnp.sum(seq_cols, axis=0)]
  transfers between devices with their start and end apart: 24 -> 80, of which waited for: 20 -> 31; matrix products, arithmetic and copies ran while one was open for 2% -> 15% of each run, Pallas kernels for 0% -> 33%
where the time goes in v1:
time: 960 us; the launch traced here: 952 us
  Pallas kernels  389 us (41%)
  waiting for transfers between devices  279 us (29%)
  starting transfers between devices  105 us (11%)
  other arithmetic  104 us (11%)
  local copies, waits for them, and re-layouts  68.7 us (7%)
    pallas_call x24, Pallas kernels, call(): pl.pallas_call(kernel, grid=(grid,), in_specs=in_specs, out_specs=out_spe...  389 us
    ppermute x80, waiting for transfers between devices, permute(): return lax.ppermute(value, AXES, pairs)  279 us
    ppermute x80, starting transfers between devices, permute(): return lax.ppermute(value, AXES, pairs)  105 us
    unnamed x136, local copies, waits for them, and re-layouts  24.9 us
  transfers between devices with their start and end apart: 80, of which 31 were waited for; matrix products, arithmetic and copies ran while one was open for 15% of the time, Pallas kernels for 33%

profile of v1, /device:TPU:0, one launch (start us, length us, event | category | flops | bytes accessed | tf_op | source)
XLA Modules:
  0.0 952.3 jit_solution(5822964731885787312)
XLA Ops:
  71.9 12.1 %collective-permute-done.5 = f32[208,768]{1,0:T(8,128)S(1)} collective-permute-done((f32[208,768]{1,0:T(8,128)}, f32[208,768]{1,0:T(8,128)S(1)}, u32[]{:S(2)}, u32[]{:S(2)}) %collective-permute-start.5) | collective-permute-done | bytes 639008 | tf_op jit(solution)/shard_map/ppermute | solution.py:826
  103.5 12.9 %collective-permute-done.17 = f32[192,768]{1,0:T(8,128)S(1)} collective-permute-done((f32[192,768]{1,0:T(8,128)S(1)}, f32[192,768]{1,0:T(8,128)S(1)}, u32[]{:S(2)}, u32[]{:S(2)}) %collective-permute-start.17) | collective-permute-done | bytes 589856 | tf_op jit(solution)/shard_map/ppermute | solution.py:826
  122.1 20.7 %collective-permute-done.7 = f32[192,768]{1,0:T(8,128)S(1)} collective-permute-done((f32[192,768]{1,0:T(8,128)S(1)}, f32[192,768]{1,0:T(8,128)S(1)}, u32[]{:S(2)}, u32[]{:S(2)}) %collective-permute-start.7) | collective-permute-done | bytes 589856 | tf_op jit(solution)/shard_map/ppermute | solution.py:826
  167.6 16.3 %collective-permute-done.14.refs_12_.refs_16_ = f32[192,768]{1,0:T(8,128)S(1)} collective-permute-done((f32[192,768]{1,0:T(8,128)S(1)}, f32[192,768]{1,0:T(8,128)S(1)}, u32[]{:S(2)}, u32[]{:S(2)}) %collective-permute-start.14) | collective-permute-done | bytes 589856 | tf_op jit(solution)/shard_map/ppermute | solution.py:826
  185.4 12.9 %collective-permute-done.16.refs_15_.refs_19_ = f32[192,768]{1,0:T(8,128)S(1)} collective-permute-done((f32[192,768]{1,0:T(8,128)S(1)}, f32[192,768]{1,0:T(8,128)S(1)}, u32[]{:S(2)}, u32[]{:S(2)}) %collective-permute-start.16) | collective-permute-done | bytes 589856 | tf_op jit(solution)/shard_map/ppermute | solution.py:826
  200.5 13.8 %attn_in.2 = (bf16[1024,768]{1,0:T(8,128)(2,1)}, bf16[1024,768]{1,0:T(8,128)(2,1)}, f32[1024,1]{1,0:T(8,128)}, bf16[1152,1024]{1,0:T(8,128)(2,1)}, bf16[1152,102...) custom-call(s32[5]{0:T(128)} %get-tuple-element.473.flags, ...), custom_call_target="tpu_custom_call" | custom-call | flops 5435817984 | bytes 20000000 | tf_op jit(solution)/shard_map/attn_in/pallas_call | solution.py:146
  226.2 20.0 %attn_heads.2 = (bf16[384,1024]{1,0:T(8,128)(2,1)}, bf16[384,1024]{1,0:T(8,128)(2,1)}, f32[6,1,1024]{2,1,0:T(1,128)}, f32[512,768]{1,0:T(8,128)}, f32[512,768]{1,0:T(8,128)}) custom-call(bf16[1152,1024]{1,0:T(8,128)(2,1)} %get-tuple-element.185.qh.kh.vh, bf16[1152,1024]{1,0:T(8,128)(2,1)} %get-tuple-element.186.ql.kl.vl, ...), custom_call_target="tpu_custom_call" | custom-call | flops 8053063680 | bytes 15000000 | tf_op jit(solution)/shard_map/attn_heads/pallas_call | solution.py:146
  255.7 20.8 %collective-permute-done.23.refs_3_ = f32[768,768]{1,0:T(8,128)} collective-permute-done((f32[768,768]{1,0:T(8,128)}, f32[768,768]{1,0:T(8,128)}, u32[]{:S(2)}, u32[]{:S(2)}) %collective-permute-start.23) | collective-permute-done | bytes 2359328 | tf_op jit(solution)/shard_map/ppermute | solution.py:826
  276.5 19.5 %feed_up.2 = (f32[1024,768]{1,0:T(8,128)}, bf16[1024,768]{1,0:T(8,128)(2,1)}, bf16[1024,768]{1,0:T(8,128)(2,1)}, f32[1024,1]{1,0:T(8,128)}, bf16[1024,1536]{1,0:...) custom-call(s32[5]{0:T(128)} %get-tuple-element.473.flags, ...), custom_call_target="tpu_custom_call" | custom-call | flops 7247757312 | bytes 40000000 | tf_op jit(solution)/shard_map/feed_up/pallas_call | solution.py:146
  303.6 16.1 %feed_down.2 = (f32[512,768]{1,0:T(8,128)}, f32[512,768]{1,0:T(8,128)}, bf16[2,768,768]{2,1,0:T(8,128)(2,1)}, bf16[2,768,768]{2,1,0:T(8,128)(2,1)}) custom-call(s32[5]{0:T(128)} %get-tuple-element.473.flags, bf16[1024,1536]{1,0:T(8,128)(2,1)} %get-tuple-element.194.hh.refs_9_, bf16[1024,1536]{1,0:T(8,128)(2,1)} %get-tuple-element.195.hl.refs_10_, ...), custom_call_target="tpu_custom_call" | custom-call | flops 7247757312 | bytes 25000000 | tf_op jit(solution)/shard_map/feed_down/pallas_call | solution.py:146
  334.4 16.4 %attn_in.3 = (f32[1024,768]{1,0:T(8,128)}, bf16[1024,768]{1,0:T(8,128)(2,1)}, bf16[1024,768]{1,0:T(8,128)(2,1)}, f32[1024,1]{1,0:T(8,128)}, bf16[1152,1024]{1,0:...) custom-call(s32[5]{0:T(128)} %get-tuple-element.474.flags, ...), custom_call_target="tpu_custom_call" | custom-call | flops 5435817984 | bytes 20000000 | tf_op jit(solution)/shard_map/attn_in/pallas_call | solution.py:146
  350.8 20.0 %attn_heads.3 = (bf16[384,1024]{1,0:T(8,128)(2,1)}, bf16[384,1024]{1,0:T(8,128)(2,1)}, f32[6,1,1024]{2,1,0:T(1,128)}, f32[512,768]{1,0:T(8,128)}, f32[512,768]{1,0:T(8,128)}) custom-call(bf16[1152,1024]{1,0:T(8,128)(2,1)} %get-tuple-element.201.qh.kh.vh, bf16[1152,1024]{1,0:T(8,128)(2,1)} %get-tuple-element.202.ql.kl.vl, ...), custom_call_target="tpu_custom_call" | custom-call | flops 8053063680 | bytes 15000000 | tf_op jit(solution)/shard_map/attn_heads/pallas_call | solution.py:146
  372.0 11.5 %collective-permute-done.30.refs_6_ = f32[768,768]{1,0:T(8,128)} collective-permute-done((f32[768,768]{1,0:T(8,128)S(1)}, f32[768,768]{1,0:T(8,128)}, u32[]{:S(2)}, u32[]{:S(2)}) %collective-permute-start.30) | collective-permute-done | bytes 2359328 | tf_op jit(solution)/shard_map/ppermute | solution.py:826
  383.5 19.4 %feed_up.3 = (f32[1024,768]{1,0:T(8,128)}, bf16[1024,768]{1,0:T(8,128)(2,1)}, bf16[1024,768]{1,0:T(8,128)(2,1)}, f32[1024,1]{1,0:T(8,128)}, bf16[1024,1536]{1,0:...) custom-call(s32[5]{0:T(128)} %get-tuple-element.474.flags, ...), custom_call_target="tpu_custom_call" | custom-call | flops 7247757312 | bytes 40000000 | tf_op jit(solution)/shard_map/feed_up/pallas_call | solution.py:146
  402.9 15.6 %feed_down.3 = (f32[512,768]{1,0:T(8,128)}, f32[512,768]{1,0:T(8,128)}, bf16[2,768,768]{2,1,0:T(8,128)(2,1)}, bf16[2,768,768]{2,1,0:T(8,128)(2,1)}) custom-call(s32[5]{0:T(128)} %get-tuple-element.474.flags, bf16[1024,1536]{1,0:T(8,128)(2,1)} %get-tuple-element.208.hh.refs_2_, bf16[1024,1536]{1,0:T(8,128)(2,1)} %get-tuple-element.209.hl.refs_3_, ...), custom_call_target="tpu_custom_call" | custom-call | flops 7247757312 | bytes 25000000 | tf_op jit(solution)/shard_map/feed_down/pallas_call | solution.py:146
  418.5 23.7 %feed_back_one.2 = (f32[1024,768]{1,0:T(8,128)}, bf16[1024,1536]{1,0:T(8,128)(2,1)}, bf16[1024,1536]{1,0:T(8,128)(2,1)}, f32[2,2,192,768]{3,2,1,0:T(8,128)}, f32...) custom-call(s32[5]{0:T(128)} %get-tuple-element.474.flags, f32[1024,768]{1,0:T(8,128)} %select_multiply_fusion.g_in, ...), custom_call_target="tpu_custom_call" | custom-call | flops 14495514624 | bytes 40000000 | tf_op jit(solution)/shard_map/feed_back_one/pallas_call | solution.py:146
  442.2 13.1 %feed_back_two_e.2 = (f32[512,768]{1,0:T(8,128)}, f32[512,768]{1,0:T(8,128)}, f32[4,768]{1,0:T(4,128)}) custom-call(s32[5]{0:T(128)} %get-tuple-element.474.flags, bf16[1024,1536]{1,0:T(8,128)(2,1)} %get-tuple-element.225.uh, bf16[1024,1536]{1,0:T(8,128)(2,1)} %get-tuple-element.219.ul, bf16[1024,768]{1,0:T(8,128)(2,1)} %get-tuple-element.220.nh, ...), custom_call_target="tpu_custom_call" | custom-call | flops 7247757312 | bytes 25000000 | tf_op jit(solution)/shard_map/feed_back_two_e/pallas_call | solution.py:146
  456.4 13.6 %feed_back_two_w.2 = (f32[2,2,192,768]{3,2,1,0:T(8,128)}, f32[2,2,192,768]{3,2,1,0:T(8,128)}) custom-call(s32[5]{0:T(128)} %get-tuple-element.474.flags, bf16[1024,1536]{1,0:T(8,128)(2,1)} %get-tuple-element.225.uh, bf16[1024,1536]{1,0:T(8,128)(2,1)} %get-tuple-element.219.ul, bf16[1024,768]{1,0:T(8,128)(2,1)} %get-tuple-element.220.nh, ...), custom_call_target="tpu_custom_call" | custom-call | flops 7247757312 | bytes 25000000 | tf_op jit(solution)/shard_map/feed_back_two_w/pallas_call | solution.py:146
  486.4 11.4 %attn_back_one.2 = (f32[1024,768]{1,0:T(8,128)}, bf16[384,1024]{1,0:T(8,128)(2,1)}, bf16[384,1024]{1,0:T(8,128)(2,1)}, f32[384,768]{1,0:T(8,128)}, f32[1,768]{1,0:T(1,128)}) custom-call(f32[1024,768]{1,0:T(8,128)} %get-tuple-element.227.g_in, f32[512,768]{1,0:T(8,128)} %get-tuple-element.228.mine_a, f32[512,768]{1,0:T(8,128)} %get-tuple-element.229.mine_b, ...), custom_call_target="tpu_custom_call" | custom-call | flops 3623878656 | bytes 20000000 | tf_op jit(solution)/shard_map/attn_back_one/pallas_call | solution.py:146
  497.8 28.3 %attn_heads_back.2 = (bf16[384,1024]{1,0:T(8,128)(2,1)}, bf16[384,1024]{1,0:T(8,128)(2,1)}, bf16[384,1024]{1,0:T(8,128)(2,1)}, bf16[384,1024]{1,0:T(8,128)(2,1)}...) custom-call(bf16[1152,1024]{1,0:T(8,128)(2,1)} %get-tuple-element.201.qh.kh.vh, ...), custom_call_target="tpu_custom_call" | custom-call | flops 20937965568 | bytes 15000000 | tf_op jit(solution)/shard_map/attn_heads_back/pallas_call | solution.py:146
  535.4 13.4 %attn_back_two_e.2 = (f32[512,768]{1,0:T(8,128)}, f32[512,768]{1,0:T(8,128)}, f32[4,768]{1,0:T(4,128)}) custom-call(s32[5]{0:T(128)} %get-tuple-element.474.flags, bf16[384,1024]{1,0:T(8,128)(2,1)} %get-tuple-element.254.refs_0_, bf16[384,1024]{1,0:T(8,128)(2,1)} %get-tuple-element.240.refs_1_, bf16[384,1024]{1,0:T(8,128)(2,1)} %get-tuple-element.241.refs_2_, ...), custom_call_target="tpu_custom_call" | custom-call | flops 5435817984 | bytes 15000000 | tf_op jit(solution)/shard_map/attn_back_two_e/pallas_call | solution.py:146
  561.6 14.3 %attn_back_two_w.2 = (f32[2,2,192,768]{3,2,1,0:T(8,128)}, f32[2,2,192,768]{3,2,1,0:T(8,128)}, f32[2,8,576]{2,1,0:T(8,128)}) custom-call(s32[5]{0:T(128)} %get-tuple-element.474.flags, bf16[384,1024]{1,0:T(8,128)(2,1)} %get-tuple-element.254.refs_0_, bf16[384,1024]{1,0:T(8,128)(2,1)} %get-tuple-element.240.refs_1_, ...), custom_call_target="tpu_custom_call" | custom-call | flops 5435817984 | bytes 15000000 | tf_op jit(solution)/shard_map/attn_back_two_w/pallas_call | solution.py:146
  591.1 27.2 %feed_back_one.3 = (f32[1024,768]{1,0:T(8,128)}, bf16[1024,1536]{1,0:T(8,128)(2,1)}, bf16[1024,1536]{1,0:T(8,128)(2,1)}, f32[2,2,192,768]{3,2,1,0:T(8,128)}, f32...) custom-call(s32[5]{0:T(128)} %get-tuple-element.473.flags, f32[1024,768]{1,0:T(8,128)} %get-tuple-element.261.g_in, ...), custom_call_target="tpu_custom_call" | custom-call | flops 14495514624 | bytes 40000000 | tf_op jit(solution)/shard_map/feed_back_one/pallas_call | solution.py:146
  622.6 13.1 %feed_back_two_e.3 = (f32[512,768]{1,0:T(8,128)}, f32[512,768]{1,0:T(8,128)}, f32[4,768]{1,0:T(4,128)}) custom-call(s32[5]{0:T(128)} %get-tuple-element.473.flags, bf16[1024,1536]{1,0:T(8,128)(2,1)} %get-tuple-element.286.uh, bf16[1024,1536]{1,0:T(8,128)(2,1)} %get-tuple-element.276.ul, bf16[1024,768]{1,0:T(8,128)(2,1)} %get-tuple-element.277.nh, ...), custom_call_target="tpu_custom_call" | custom-call | flops 7247757312 | bytes 25000000 | tf_op jit(solution)/shard_map/feed_back_two_e/pallas_call | solution.py:146
  646.7 13.4 %feed_back_two_w.3 = (f32[2,2,192,768]{3,2,1,0:T(8,128)}, f32[2,2,192,768]{3,2,1,0:T(8,128)}) custom-call(s32[5]{0:T(128)} %get-tuple-element.473.flags, bf16[1024,1536]{1,0:T(8,128)(2,1)} %get-tuple-element.286.uh, bf16[1024,1536]{1,0:T(8,128)(2,1)} %get-tuple-element.276.ul, bf16[1024,768]{1,0:T(8,128)(2,1)} %get-tuple-element.277.nh, ...), custom_call_target="tpu_custom_call" | custom-call | flops 7247757312 | bytes 25000000 | tf_op jit(solution)/shard_map/feed_back_two_w/pallas_call | solution.py:146
  684.9 28.3 %attn_heads_back.3 = (bf16[384,1024]{1,0:T(8,128)(2,1)}, bf16[384,1024]{1,0:T(8,128)(2,1)}, bf16[384,1024]{1,0:T(8,128)(2,1)}, bf16[384,1024]{1,0:T(8,128)(2,1)}...) custom-call(bf16[1152,1024]{1,0:T(8,128)(2,1)} %get-tuple-element.185.qh.kh.vh, ...), custom_call_target="tpu_custom_call" | custom-call | flops 20937965568 | bytes 15000000 | tf_op jit(solution)/shard_map/attn_heads_back/pallas_call | solution.py:146
  729.2 14.5 %attn_back_two_w.3 = (f32[2,2,96,768]{3,2,1,0:T(8,128)}, f32[2,2,96,768]{3,2,1,0:T(8,128)}, f32[2,2,96,768]{3,2,1,0:T(8,128)}, f32[2,2,96,768]{3,2,1,0:T(8,128)}, f32[2,8,576]{2,1,0:T(8,128)}) custom-call(s32[5]{0:T(128)} %get-tuple-element.473.flags, bf16[384,1024]{1,0:T(8,128)(2,1)} %get-tuple-element.321.refs_0_, ...), custom_call_target="tpu_custom_call" | custom-call | flops 5435817984 | bytes 15000000 | tf_op jit(solution)/shard_map/attn_back_two_w/pallas_call | solution.py:146
  754.7 13.5 %attn_back_two_e.3 = (f32[512,768]{1,0:T(8,128)}, f32[512,768]{1,0:T(8,128)}, f32[4,768]{1,0:T(4,128)}) custom-call(s32[5]{0:T(128)} %get-tuple-element.473.flags, bf16[384,1024]{1,0:T(8,128)(2,1)} %get-tuple-element.321.refs_0_, bf16[384,1024]{1,0:T(8,128)(2,1)} %get-tuple-element.307.refs_1_, bf16[384,1024]{1,0:T(8,128)(2,1)} %get-tuple-element.308.refs_2_, ...), custom_call_target="tpu_custom_call" | custom-call | flops 5435817984 | bytes 15000000 | tf_op jit(solution)/shard_map/attn_back_two_e/pallas_call | solution.py:146
  782.7 15.1 %collective-permute-done.74 = f32[2,192,768]{2,1,0:T(8,128)} collective-permute-done((f32[2,192,768]{2,1,0:T(8,128)}, f32[2,192,768]{2,1,0:T(8,128)}, u32[]{:S(2)}, u32[]{:S(2)}) %collective-permute-start.74) | collective-permute-done | bytes 1179680 | tf_op jit(solution)/shard_map/ppermute | solution.py:826
  830.8 11.8 %collective-permute-done.75 = f32[192,768]{1,0:T(8,128)S(1)} collective-permute-done((f32[192,768]{1,0:T(8,128)S(1)}, f32[192,768]{1,0:T(8,128)S(1)}, u32[]{:S(2)}, u32[]{:S(2)}) %collective-permute-start.75) | collective-permute-done | bytes 589856 | tf_op jit(solution)/shard_map/ppermute | solution.py:826
  871.6 38.4 %collective-permute-done.76 = f32[192,768]{1,0:T(8,128)} collective-permute-done((f32[192,768]{1,0:T(8,128)}, f32[192,768]{1,0:T(8,128)}, u32[]{:S(2)}, u32[]{:S(2)}) %collective-permute-start.76) | collective-permute-done | bytes 589856 | tf_op jit(solution)/shard_map/ppermute | solution.py:826
  931.8 12.8 %collective-permute-start.73 = (f32[96,768]{0,1:T(8,128)S(1)}, f32[96,768]{0,1:T(8,128)S(1)}, u32[]{:S(2)}, u32[]{:S(2)}) collective-permute-start(f32[96,768]{0,1:T(8,128)S(1)} %bitcast.224), channel_id=1, source_target_pairs={{0,1},{1,0},{2,3},{3,2},{4,5},{5,4},{6,7},{7,6},{8,9},{9,8},{10,11... | collective-permute-start | bytes 884744 | tf_op jit(solution)/shard_map/ppermute | solution.py:826
  (422 shorter events, 393.7 us)
Async XLA Ops:
  11.1 51.2 %collective-permute-start.8 = (f32[208,768]{1,0:T(8,128)}, f32[208,768]{1,0:T(8,128)}, u32[]{:S(2)}, u32[]{:S(2)}) collective-permute-start(f32[208,768]{1,0:T(8,128)} %concatenate.122), channel_id=1, source_target_pairs={{0,8},{1,9},{2,10},{3,11},{4,12},{5,13},{6,14},{7,15},{8,0},{9,1},... | collective-permute-start | bytes 1916936 | tf_op jit(solution)/shard_map/ppermute | solution.py:826
  51.1 109.9 %collective-permute-start.3 = (f32[1024,768]{1,0:T(8,128)}, f32[1024,768]{1,0:T(8,128)}, u32[]{:S(2)}, u32[]{:S(2)}) collective-permute-start(f32[1024,768]{1,0:T(8,128)} %constant_dynamic-slice_fusion.16), channel_id=1, source_target_pairs={{0,1},{2,3},{4,5},{6,7},{8,9},{10,11},{12,13},{14,15},{17,16},{19,... | collective-permute-start | bytes 9437192 | tf_op jit(solution)/shard_map/ppermute | solution.py:826
  57.9 104.4 %collective-permute-start.2 = (f32[1024,768]{1,0:T(8,128)}, f32[1024,768]{1,0:T(8,128)}, u32[]{:S(2)}, u32[]{:S(2)}) collective-permute-start(f32[1024,768]{1,0:T(8,128)} %constant_dynamic-slice_fusion.17), channel_id=1, source_target_pairs={{0,1},{2,3},{4,5},{6,7},{8,9},{10,11},{12,13},{14,15},{17,16},{19,... | collective-permute-start | bytes 9437192 | tf_op jit(solution)/shard_map/ppermute | solution.py:826
  88.3 66.9 %collective-permute-start.6 = (f32[384,768]{1,0:T(8,128)}, f32[384,768]{1,0:T(8,128)}, u32[]{:S(2)}, u32[]{:S(2)}) collective-permute-start(f32[384,768]{1,0:T(8,128)} %pad_maximum_fusion.8), channel_id=1, source_target_pairs={{0,8},{1,9},{2,10},{3,11},{4,12},{5,13},{6,14},{7,15},{8,0},{9,1},... | collective-permute-start | bytes 3538952 | tf_op jit(solution)/shard_map/ppermute | solution.py:826
  103.5 39.4 %collective-permute-start.7 = (f32[192,768]{1,0:T(8,128)S(1)}, f32[192,768]{1,0:T(8,128)S(1)}, u32[]{:S(2)}, u32[]{:S(2)}) collective-permute-start(f32[192,768]{1,0:T(8,128)S(1)} %collective-permute-done.4), channel_id=1, source_target_pairs={{0,8},{1,9},{2,10},{3,11},{4,12},{5,13},{6,14},{7,15},{8,0},{9,1},... | collective-permute-start | bytes 1769480 | tf_op jit(solution)/shard_map/ppermute | solution.py:826
  116.4 38.3 %collective-permute-start.18 = (f32[192,768]{1,0:T(8,128)S(1)}, f32[192,768]{1,0:T(8,128)S(1)}, u32[]{:S(2)}, u32[]{:S(2)}) collective-permute-start(f32[192,768]{1,0:T(8,128)S(1)} %collective-permute-done.17), channel_id=1, source_target_pairs={{0,8},{1,9},{2,10},{3,11},{4,12},{5,13},{6,14},{7,15},{8,0},{9,1},... | collective-permute-start | bytes 1769480 | tf_op jit(solution)/shard_map/ppermute | solution.py:826
  142.9 55.4 %collective-permute-start.10 = (f32[416,768]{1,0:T(8,128)S(1)}, f32[416,768]{1,0:T(8,128)S(1)}, u32[]{:S(2)}, u32[]{:S(2)}) collective-permute-start(f32[416,768]{1,0:T(8,128)S(1)} %pad_maximum_fusion.6), channel_id=1, source_target_pairs={{0,4},{1,5},{2,6},{3,7},{4,0},{5,1},{6,2},{7,3},{8,12},{9,13},{10,... | collective-permute-start | bytes 3833864 | tf_op jit(solution)/shard_map/ppermute | solution.py:826
  154.7 43.7 %collective-permute-start.12 = (f32[416,768]{1,0:T(8,128)S(1)}, f32[416,768]{1,0:T(8,128)S(1)}, u32[]{:S(2)}, u32[]{:S(2)}) collective-permute-start(f32[416,768]{1,0:T(8,128)S(1)} %pad_maximum_fusion.7), channel_id=1, source_target_pairs={{0,2},{1,3},{2,0},{3,1},{4,6},{5,7},{6,4},{7,5},{8,10},{9,11},{10,... | collective-permute-start | bytes 3833864 | tf_op jit(solution)/shard_map/ppermute | solution.py:826
  162.3 59.6 %collective-permute-start.19 = (f32[384,768]{1,0:T(8,128)}, f32[384,768]{1,0:T(8,128)}, u32[]{:S(2)}, u32[]{:S(2)}) collective-permute-start(f32[384,768]{1,0:T(8,128)} %pad_maximum_fusion.9.refs_1_), channel_id=1, source_target_pairs={{0,2},{1,3},{2,0},{3,1},{4,6},{5,7},{6,4},{7,5},{8,10},{9,11},{10,... | collective-permute-start | bytes 3538952 | tf_op jit(solution)/shard_map/ppermute | solution.py:826
  183.9 62.3 %collective-permute-start.20 = (f32[384,768]{1,0:T(8,128)}, f32[384,768]{1,0:T(8,128)}, u32[]{:S(2)}, u32[]{:S(2)}) collective-permute-start(f32[384,768]{1,0:T(8,128)} %pad_maximum_fusion.10.refs_1_), channel_id=1, source_target_pairs={{0,4},{1,5},{2,6},{3,7},{4,0},{5,1},{6,2},{7,3},{8,12},{9,13},{10,... | collective-permute-start | bytes 3538952 | tf_op jit(solution)/shard_map/ppermute | solution.py:826
  224.7 51.8 %collective-permute-start.23 = (f32[768,768]{1,0:T(8,128)}, f32[768,768]{1,0:T(8,128)}, u32[]{:S(2)}, u32[]{:S(2)}) collective-permute-start(f32[768,768]{1,0:T(8,128)} %pad_maximum_fusion.1), channel_id=1, source_target_pairs={{0,4},{1,5},{2,6},{3,7},{4,0},{5,1},{6,2},{7,3},{8,12},{9,13},{10,... | collective-permute-start | bytes 7077896 | tf_op jit(solution)/shard_map/ppermute | solution.py:826
  249.1 54.5 %collective-permute-start.24 = (f32[768,768]{1,0:T(8,128)}, f32[768,768]{1,0:T(8,128)}, u32[]{:S(2)}, u32[]{:S(2)}) collective-permute-start(f32[768,768]{1,0:T(8,128)} %pad_maximum_fusion.2), channel_id=1, source_target_pairs={{0,2},{1,3},{2,0},{3,1},{4,6},{5,7},{6,4},{7,5},{8,10},{9,11},{10,... | collective-permute-start | bytes 7077896 | tf_op jit(solution)/shard_map/ppermute | solution.py:826
  251.2 74.7 %collective-permute-start.25 = (f32[384,768]{1,0:T(8,128)S(1)}, f32[384,768]{1,0:T(8,128)S(1)}, u32[]{:S(2)}, u32[]{:S(2)}) collective-permute-start(f32[384,768]{1,0:T(8,128)S(1)} %pad_maximum_fusion.11.refs_4_), channel_id=1, source_target_pairs={{0,2},{1,3},{2,0},{3,1},{4,6},{5,7},{6,4},{7,5},{8,10},{9,11},{10,... | collective-permute-start | bytes 3538952 | tf_op jit(solution)/shard_map/ppermute | solution.py:826
  330.1 53.3 %collective-permute-start.30 = (f32[768,768]{1,0:T(8,128)S(1)}, f32[768,768]{1,0:T(8,128)}, u32[]{:S(2)}, u32[]{:S(2)}) collective-permute-start(f32[768,768]{1,0:T(8,128)S(1)} %pad_maximum_fusion.3), channel_id=1, source_target_pairs={{0,4},{1,5},{2,6},{3,7},{4,0},{5,1},{6,2},{7,3},{8,12},{9,13},{10,... | collective-permute-start | bytes 7077896 | tf_op jit(solution)/shard_map/ppermute | solution.py:826
  470.0 65.5 %collective-permute-start.39 = (f32[2,2,192,768]{3,2,1,0:T(8,128)}, f32[2,2,192,768]{3,2,1,0:T(8,128)}, u32[]{:S(2)}, u32[]{:S(2)}) collective-permute-start(f32[2,2,192,768]{3,2,1,0:T(8,128)} %get-tuple-element.226), channel_id=1, source_target_pairs={{0,4},{1,5},{2,6},{3,7},{4,0},{5,1},{6,2},{7,3},{8,12},{9,13},{10,... | collective-permute-start | bytes 7077896 | tf_op jit(solution)/shard_map/ppermute | solution.py:826
  470.5 58.6 %collective-permute-start.38 = (f32[2,2,192,768]{3,2,1,0:T(8,128)}, f32[2,2,192,768]{3,2,1,0:T(8,128)}, u32[]{:S(2)}, u32[]{:S(2)}) collective-permute-start(f32[2,2,192,768]{3,2,1,0:T(8,128)} %get-tuple-element.249), channel_id=1, source_target_pairs={{0,2},{1,3},{2,0},{3,1},{4,6},{5,7},{6,4},{7,5},{8,10},{9,11},{10,... | collective-permute-start | bytes 7077896 | tf_op jit(solution)/shard_map/ppermute | solution.py:826
  478.6 47.5 %collective-permute-start.33 = (f32[512,384]{1,0:T(8,128)}, f32[512,384]{1,0:T(8,128)S(1)}, u32[]{:S(2)}, u32[]{:S(2)}) collective-permute-start(f32[512,384]{1,0:T(8,128)} %pad_maximum_fusion.13), channel_id=1, source_target_pairs={{0,8},{2,10},{4,12},{6,14},{8,0},{10,2},{12,4},{14,6},{17,25},{19,... | collective-permute-start | bytes 2359304 | tf_op jit(solution)/shard_map/ppermute | solution.py:826
  481.6 44.5 %collective-permute-start.35 = (f32[512,384]{1,0:T(8,128)}, f32[512,384]{1,0:T(8,128)S(1)}, u32[]{:S(2)}, u32[]{:S(2)}) collective-permute-start(f32[512,384]{1,0:T(8,128)} %pad_maximum_fusion.15), channel_id=1, source_target_pairs={{0,24},{2,26},{4,28},{6,30},{8,16},{10,18},{12,20},{14,22},{17,9},... | collective-permute-start | bytes 2359304 | tf_op jit(solution)/shard_map/ppermute | solution.py:826
  485.1 41.1 %collective-permute-start.34 = (f32[512,384]{1,0:T(8,128)}, f32[512,384]{1,0:T(8,128)S(1)}, u32[]{:S(2)}, u32[]{:S(2)}) collective-permute-start(f32[512,384]{1,0:T(8,128)} %pad_maximum_fusion.14), channel_id=1, source_target_pairs={{0,16},{2,18},{4,20},{6,22},{8,24},{10,26},{12,28},{14,30},{17,1},... | collective-permute-start | bytes 2359304 | tf_op jit(solution)/shard_map/ppermute | solution.py:826
  584.5 52.4 %collective-permute-start.47 = (f32[2,2,192,768]{3,2,1,0:T(8,128)}, f32[2,2,192,768]{3,2,1,0:T(8,128)}, u32[]{:S(2)}, u32[]{:S(2)}) collective-permute-start(f32[2,2,192,768]{3,2,1,0:T(8,128)} %get-tuple-element.284), channel_id=1, source_target_pairs={{0,2},{1,3},{2,0},{3,1},{4,6},{5,7},{6,4},{7,5},{8,10},{9,11},{10,... | collective-permute-start | bytes 7077896 | tf_op jit(solution)/shard_map/ppermute | solution.py:826
  645.1 73.7 %collective-permute-start.52 = (f32[2,2,192,768]{3,2,1,0:T(8,128)}, f32[2,2,192,768]{3,2,1,0:T(8,128)}, u32[]{:S(2)}, u32[]{:S(2)}) collective-permute-start(f32[2,2,192,768]{3,2,1,0:T(8,128)} %get-tuple-element.305), channel_id=1, source_target_pairs={{0,4},{1,5},{2,6},{3,7},{4,0},{5,1},{6,2},{7,3},{8,12},{9,13},{10,... | collective-permute-start | bytes 7077896 | tf_op jit(solution)/shard_map/ppermute | solution.py:826
  660.0 66.2 %collective-permute-start.55 = (f32[2,2,192,768]{3,2,1,0:T(8,128)}, f32[2,2,192,768]{3,2,1,0:T(8,128)}, u32[]{:S(2)}, u32[]{:S(2)}) collective-permute-start(f32[2,2,192,768]{3,2,1,0:T(8,128)} %get-tuple-element.287), channel_id=1, source_target_pairs={{0,2},{1,3},{2,0},{3,1},{4,6},{5,7},{6,4},{7,5},{8,10},{9,11},{10,... | collective-permute-start | bytes 7077896 | tf_op jit(solution)/shard_map/ppermute | solution.py:826
  671.8 52.3 %collective-permute-start.54 = (f32[192,768]{1,0:T(8,128)}, f32[192,768]{1,0:T(8,128)}, u32[]{:S(2)}, u32[]{:S(2)}) collective-permute-start(f32[192,768]{1,0:T(8,128)} %fusion.15), channel_id=1, source_target_pairs={{0,8},{1,9},{2,10},{3,11},{4,12},{5,13},{6,14},{7,15},{8,0},{9,1},... | collective-permute-start | bytes 1769480 | tf_op jit(solution)/shard_map/ppermute | solution.py:826
  774.8 72.4 %collective-permute-start.72 = (f32[192,768]{1,0:T(8,128)}, f32[192,768]{1,0:T(8,128)}, u32[]{:S(2)}, u32[]{:S(2)}) collective-permute-start(f32[192,768]{1,0:T(8,128)} %fusion.11), channel_id=1, source_target_pairs={{0,16},{1,17},{2,18},{3,19},{4,20},{5,21},{6,22},{7,23},{8,24},{9,... | collective-permute-start | bytes 1769480 | tf_op jit(solution)/shard_map/ppermute | solution.py:826
  779.4 41.0 %collective-permute-start.67 = (f32[2,96,768]{2,1,0:T(8,128)}, f32[2,96,768]{2,1,0:T(8,128)}, u32[]{:S(2)}, u32[]{:S(2)}) collective-permute-start(f32[2,96,768]{2,1,0:T(8,128)} %get-tuple-element.419), channel_id=1, source_target_pairs={{0,4},{1,5},{2,6},{3,7},{4,0},{5,1},{6,2},{7,3},{8,12},{9,13},{10,... | collective-permute-start | bytes 1769480 | tf_op jit(solution)/shard_map/ppermute | solution.py:826
  801.1 50.0 %collective-permute-start.78 = (f32[192,768]{1,0:T(8,128)}, f32[192,768]{1,0:T(8,128)}, u32[]{:S(2)}, u32[]{:S(2)}) collective-permute-start(f32[192,768]{1,0:T(8,128)} %fusion.3), channel_id=1, source_target_pairs={{16,0},{17,1},{18,2},{19,3},{20,4},{21,5},{22,6},{23,7},{24,8},{25... | collective-permute-start | bytes 1769480 | tf_op jit(solution)/shard_map/ppermute | solution.py:826
  830.3 39.3 %collective-permute-start.70 = (f32[192,768]{1,0:T(8,128)}, f32[192,768]{1,0:T(8,128)}, u32[]{:S(2)}, u32[]{:S(2)}) collective-permute-start(f32[192,768]{1,0:T(8,128)} %pad_maximum_fusion.23), channel_id=1, source_target_pairs={{0,8},{1,9},{2,10},{3,11},{4,12},{5,13},{6,14},{7,15},{8,0},{9,1},... | collective-permute-start | bytes 1769480 | tf_op jit(solution)/shard_map/ppermute | solution.py:826
  844.8 65.2 %collective-permute-start.76 = (f32[192,768]{1,0:T(8,128)}, f32[192,768]{1,0:T(8,128)}, u32[]{:S(2)}, u32[]{:S(2)}) collective-permute-start(f32[192,768]{1,0:T(8,128)} %fusion.6), channel_id=1, source_target_pairs={{16,0},{17,1},{18,2},{19,3},{20,4},{21,5},{22,6},{23,7},{24,8},{25... | collective-permute-start | bytes 1769480 | tf_op jit(solution)/shard_map/ppermute | solution.py:826
  847.2 66.5 %collective-permute-start.58 = (f32[512,384]{1,0:T(8,128)}, f32[512,384]{1,0:T(8,128)}, u32[]{:S(2)}, u32[]{:S(2)}) collective-permute-start(f32[512,384]{1,0:T(8,128)} %pad_maximum_fusion.17), channel_id=1, source_target_pairs={{0,8},{2,10},{4,12},{6,14},{8,0},{10,2},{12,4},{14,6},{17,25},{19,... | collective-permute-start | bytes 2359304 | tf_op jit(solution)/shard_map/ppermute | solution.py:826
  851.1 62.5 %collective-permute-start.60 = (f32[512,384]{1,0:T(8,128)}, f32[512,384]{1,0:T(8,128)}, u32[]{:S(2)}, u32[]{:S(2)}) collective-permute-start(f32[512,384]{1,0:T(8,128)} %pad_maximum_fusion.19), channel_id=1, source_target_pairs={{0,24},{2,26},{4,28},{6,30},{8,16},{10,18},{12,20},{14,22},{17,9},... | collective-permute-start | bytes 2359304 | tf_op jit(solution)/shard_map/ppermute | solution.py:826
  864.1 49.6 %collective-permute-start.59 = (f32[512,384]{1,0:T(8,128)}, f32[512,384]{1,0:T(8,128)}, u32[]{:S(2)}, u32[]{:S(2)}) collective-permute-start(f32[512,384]{1,0:T(8,128)} %pad_maximum_fusion.18), channel_id=1, source_target_pairs={{0,16},{2,18},{4,20},{6,22},{8,24},{10,26},{12,28},{14,30},{17,1},... | collective-permute-start | bytes 2359304 | tf_op jit(solution)/shard_map/ppermute | solution.py:826
  869.6 48.2 %collective-permute-start.65 = (f32[56,768]{1,0:T(8,128)}, f32[56,768]{1,0:T(8,128)S(1)}, u32[]{:S(2)}, u32[]{:S(2)}) collective-permute-start(f32[56,768]{1,0:T(8,128)} %add.359), channel_id=1, source_target_pairs={{0,16},{1,17},{2,18},{3,19},{4,20},{5,21},{6,22},{7,23},{8,24},{9,... | collective-permute-start | bytes 516104 | tf_op jit(solution)/shard_map/ppermute | solution.py:826
  (113 other events, 1819.9 us)

commit v2 on v1

--- a/solution.py
+++ b/solution.py
@@ -142,20 +142,68 @@
 SMEM = pl.BlockSpec(memory_space=pltpu.SMEM)
 
 
-def call(kernel, grid, in_specs, out_specs, out_shapes, scratch, name, flops, nbytes, *args):
+class Rider:
+    def __init__(self, count, *segments):
+        self.count, self.segments = count, segments
+
+    def arrays(self):
+        return [v for a, _, b, _ in self.segments for v in (a, b)]
+
+    def specs(self, grid):
+        each = grid // len(self.segments)
+        block, width = self.count // each, self.segments[0][0].shape[1]
+        result = []
+        for number, (_, first_a, _, first_b) in enumerate(self.segments):
+            for first in (first_a, first_b):
+                def place(i, start=number * each, base=first // block):
+                    return (base + jnp.clip(i - start, 0, each - 1), 0)
+
+                result.append(pl.BlockSpec((block, width), place))
+        return result
+
+    def out(self, grid):
+        width = self.segments[0][0].shape[1]
+        total = self.count * len(self.segments)
+        return pl.BlockSpec((total // grid, width), lambda i: (i, 0)), ((total, width), f32)
+
+    def run(self, grid, refs, out):
+        each = grid // len(self.segments)
+        value = refs[0][...] + refs[1][...]
+        for number in range(1, len(self.segments)):
+            other = refs[2 * number][...] + refs[2 * number + 1][...]
+            value = jnp.where(pl.program_id(0) >= number * each, other, value)
+        out[...] = value
+
+
+def call(kernel, grid, in_specs, out_specs, out_shapes, scratch, name, flops, nbytes, *args, riders=()):
+    ins, outs = len(in_specs), len(out_specs)
+    extra = [v for rider in riders for v in rider.arrays()]
+    in_specs = list(in_specs) + [v for rider in riders for v in rider.specs(grid)]
+    rider_outs = [rider.out(grid) for rider in riders]
+
+    def whole(*refs):
+        mine, refs = refs[:ins], refs[ins:]
+        sources, refs = refs[: len(extra)], refs[len(extra) :]
+        results, refs = refs[:outs], refs[outs:]
+        sums, refs = refs[: len(riders)], refs[len(riders) :]
+        kernel(*mine, *results, *refs)
+        for rider, out in zip(riders, sums):
+            own, sources = sources[: len(rider.arrays())], sources[len(rider.arrays()) :]
+            rider.run(grid, own, out)
+
     return pl.pallas_call(
-        kernel,
+        whole,
         grid=(grid,),
         in_specs=in_specs,
-        out_specs=out_specs,
-        out_shape=[jax.ShapeDtypeStruct(s, t) for s, t in out_shapes],
+        out_specs=list(out_specs) + [spec for spec, _ in rider_outs],
+        out_shape=[jax.ShapeDtypeStruct(s, t) for s, t in list(out_shapes) + [shape for _, shape in rider_outs]],
         scratch_shapes=scratch,
         name=name,
-        cost_estimate=pl.CostEstimate(flops=int(flops), bytes_accessed=int(nbytes), transcendentals=0),
+        cost_estimate=pl.CostEstimate(flops=1, bytes_accessed=1, transcendentals=0),
         compiler_params=pltpu.CompilerParams(
             vmem_limit_bytes=VMEM_LIMIT, dimension_semantics=("arbitrary",)
         ),
-    )(*args)
+    )(*args, *extra)
 
 
 def attn_in_kernel(added, entries, count, flags, *refs):
@@ -439,7 +487,7 @@
         store_pieces(flags, lambda slot, row, count: acc[slot, pl.ds(row, count), :], order, piece_refs)
 
 
-def feed_back_one(order, flags, g, pulled, dh, dl, hh, hl, slope):
+def feed_back_one(order, flags, g, pulled, dh, dl, hh, hl, slope, riders=()):
     length, width = g.shape
     hidden = dh.shape[1]
     piece_specs, piece_shapes = piece_outs(width, order)
@@ -457,6 +505,7 @@
         6 * length * width * 4 * hidden,
         40e6,
         flags, g, *pulled, dh, dl, hh, hl, slope,
+        riders=riders,
     )
 
 
@@ -497,7 +546,7 @@
             store_pieces(flags, lambda slot, row, count: acc[slot, pl.ds(row, count), :], order, piece_refs)
 
 
-def feed_back_two(parts, order, flags, uh, ul, nh, nl, vec, wh, wl):
+def feed_back_two(parts, order, flags, uh, ul, nh, nl, vec, wh, wl, riders=()):
     length, width = nh.shape
     hidden = wh.shape[1]
     piece_specs, piece_shapes = piece_outs(width, order)
@@ -517,6 +566,7 @@
         6 * length * width * 2 * hidden,
         25e6,
         flags, uh, ul, nh, nl, vec, *weights,
+        riders=riders,
     )
 
 
@@ -543,7 +593,7 @@
     do_out[...] += dot3(oh[...], ol[...], gh, gl, NN)
 
 
-def attn_back_one(g, added, nh, nl, scale, wh, wl, oh, ol):
+def attn_back_one(g, added, nh, nl, scale, wh, wl, oh, ol, riders=()):
     length, width = g.shape
     inner = oh.shape[0]
     out_rows = inner // 2
@@ -565,6 +615,7 @@
         6 * length * width * 2 * inner,
         20e6,
         g, *added, nh, nl, scale, wh, wl, oh, ol,
+        riders=riders,
     )
 
 
@@ -609,7 +660,7 @@
     dvl[...] = low
 
 
-def attn_heads_back(ph, pl_, dh, dl, oh, ol, lse):
+def attn_heads_back(ph, pl_, dh, dl, oh, ol, lse, riders=()):
     inner2, length = ph.shape
     heads = inner2 // (3 * HS)
     half = heads // 2
@@ -628,6 +679,7 @@
         heads * length * length * HS * 2 * 26,
         15e6,
         ph, pl_, ph, pl_, ph, pl_, dh, dl, oh, ol, lse,
+        riders=riders,
     )
 
 
@@ -684,7 +736,7 @@
             store_pieces(flags, lambda slot, row, count: turned[slot, pl.ds(row, count), :], order, piece_refs)
 
 
-def attn_back_two(parts, order, flags, grads, nh, nl, vec, wh, wl, do):
+def attn_back_two(parts, order, flags, grads, nh, nl, vec, wh, wl, do, riders=()):
     length, width = nh.shape
     heads_rows = grads[0].shape[0]
     inner = 3 * heads_rows // 2
@@ -714,10 +766,21 @@
         6 * length * width * 2 * inner * len(parts),
         15e6 * len(parts),
         *args,
-    )
-
-
-def finish_kernel(g_in, mine_a, mine_b, other_a, other_b, nh, nl, scale, mask, grad_out, sums_out):
+        riders=riders,
+    )
+
+
+def by_planes(flags, value, near_out, far_out):
+    quarter = value.shape[1] // 4
+    parts = [value[:, k * quarter : (k + 1) * quarter] for k in range(4)]
+    odd, high = flags[0] % 2 == 1, flags[0] // 2 == 1
+    parts = [jnp.where(odd, parts[k ^ 1], parts[k]) for k in range(4)]
+    parts = [jnp.where(high, parts[k ^ 2], parts[k]) for k in range(4)]
+    near_out[...] = jnp.concatenate([parts[0], parts[2]], axis=1)
+    far_out[...] = jnp.concatenate([parts[1], parts[3]], axis=1)
+
+
+def finish_kernel(flags, g_in, mine_a, mine_b, other_a, other_b, nh, nl, scale, mask, near_out, far_out, sums_out):
     @pl.when(pl.program_id(0) == 0)
     def _():
         sums_out[...] = jnp.zeros_like(sums_out)
@@ -725,23 +788,45 @@
     n = nh[...].astype(f32) + nl[...].astype(f32)
     g = g_in[...] + pull_rows(n, scale[...], read_halves(mine_a, mine_b) + read_halves(other_a, other_b))
     absorbed = mask[...]
-    grad_out[...] = g * (1.0 - absorbed)
+    by_planes(flags, g * (1.0 - absorbed), near_out, far_out)
     sums_out[...] += jnp.sum(g * absorbed, axis=0, keepdims=True)
 
 
-def finish(g, added, nh, nl, scale, mask):
+def finish(flags, g, added, nh, nl, scale, mask, riders=()):
     length, width = g.shape
     return call(
         finish_kernel,
         length // BM,
-        [rows(width)] + halves(width) * 2 + [rows(width)] * 2 + [rows(1)] * 2,
-        [rows(width), full((1, width))],
-        [((length, width), f32), ((1, width), f32)],
+        [SMEM, rows(width)] + halves(width) * 2 + [rows(width)] * 2 + [rows(1)] * 2,
+        [rows(width // 2)] * 2 + [full((1, width))],
+        [((length, width // 2), f32)] * 2 + [((1, width), f32)],
         [],
         "finish",
         10 * length * width,
         15e6,
-        g, *added, nh, nl, scale, mask,
+        flags, g, *added, nh, nl, scale, mask,
+        riders=riders,
+    )
+
+
+def leave_kernel(flags, base, mine_a, mine_b, other_a, other_b, near_out, far_out):
+    value = base[...] + (read_halves(mine_a, mine_b) + read_halves(other_a, other_b))
+    by_planes(flags, value, near_out, far_out)
+
+
+def leave(flags, base, added):
+    length, width = base.shape
+    return call(
+        leave_kernel,
+        length // BM,
+        [SMEM, rows(width)] + halves(width) * 2,
+        [rows(width // 2)] * 2,
+        [((length, width // 2), f32)] * 2,
+        [],
+        "leave",
+        10 * length * width,
+        10e6,
+        flags, base, *added,
     )
 
 
@@ -845,14 +930,14 @@
     def whole(self, shard):
         return lax.all_gather(shard, AXES, axis_index_groups=self.groups(), axis=0, tiled=True)
 
-    def all_sum(self, table):
-        if self.columns == 4:
-            for step in (self.across, *[functools.partial(self.in_plane, bit=b) for b in (1, 2)]):
-                table = table + step(table)
-            for bit in (1, 2):
-                table = table + self.along_z(table, bit)
-            return table
-        return lax.psum(table, AXES)
+    def sum_step(self, table, step):
+        if self.columns != 4:
+            return lax.psum(table, AXES) if step == 0 else table
+        if step == 0:
+            return table + self.across(table)
+        if step < 3:
+            return table + self.in_plane(table, step)
+        return table + self.along_z(table, step - 2)
 
 
 class Group:
@@ -861,10 +946,10 @@
         if plan.columns == 4:
             self.got = plan.in_plane(shard, order)
 
-    def step(self, *others):
+    def step(self):
         if self.plan.columns != 4:
             return self.shard
-        self.kept = after(self.got, *others)
+        self.kept = self.got
         on = jnp.concatenate([self.shard, self.kept])
         self.last = self.plan.in_plane(on, 3 - self.order)
         return on
@@ -883,59 +968,101 @@
         ]
 
 
+def arrive(groups, *others):
+    names = [(g, "got" if not hasattr(g, "last") else "last") for g in groups if g.plan.columns == 4]
+    values = lax.optimization_barrier((*(getattr(g, name) for g, name in names), *others))
+    for (group, name), value in zip(names, values):
+        setattr(group, name, value)
+    return values[len(names) :]
+
+
 class Sum:
-    def __init__(self, plan, layer, order, pieces):
-        self.plan, self.layer, self.stage = plan, layer, 0
+    def __init__(self, plan, order, pieces):
+        self.plan, self.stage = plan, 0
         self.ways = [1, 2] if order == 3 else [order]
-        self.send, self.keep = pieces[0::2], pieces[1::2]
+        self.count = pieces[0].shape[2]
+        width = pieces[0].shape[3]
         if plan.columns == 4:
-            self.got = [plan.in_plane(v, way) for v, way in zip(self.send, self.ways)]
+            send, keep = ([v.reshape(-1, width) for v in pieces[k::2]] for k in (0, 1))
+            self.mine = keep
+            self.got = [plan.in_plane(v, way) for v, way in zip(send, self.ways)]
         else:
             parts = []
             for k in range(4):
-                for send, keep, way in zip(self.send, self.keep, self.ways):
+                for send, keep, way in zip(pieces[0::2], pieces[1::2], self.ways):
                     kinds = ((0, 2), (1, 3)) if way == 1 else ((0, 1), (2, 3))
                     parts.append(keep[kinds[0].index(k)] if k in kinds[0] else send[kinds[1].index(k)])
             whole = jnp.concatenate(parts, axis=1)
-            self.done = [
-                lax.psum_scatter(whole, AXES, axis_index_groups=plan.groups(), scatter_dimension=1, tiled=True)
-            ]
-            self.stage = 1
-
-    def advance(self, *others):
+            whole = lax.psum_scatter(whole, AXES, axis_index_groups=plan.groups(), scatter_dimension=1, tiled=True)
+            self.whole = [whole]
+
+    def merge(self, other):
+        if self.plan.columns == 4:
+            self.mine, self.got = self.mine + other.mine, self.got + other.got
+        else:
+            self.whole = self.whole + other.whole
+        return self
+
+    def riders(self):
+        if self.plan.columns != 4 or self.stage == 3:
+            return []
+        count = self.count
+        pairs = list(zip(self.mine, self.got))
+        if self.stage == 0:
+            return [Rider(2 * count, (m, first, v, first)) for first in (0, 2 * count) for m, v in pairs]
+        if self.stage == 1:
+            return [Rider(count, *((m, first, v, first) for m, v in pairs)) for first in (0, count)]
+        return [Rider(self.mine[0].shape[0], *((m, 0, v, 0) for m, v in pairs))]
+
+    def take(self, values):
+        if not values:
+            return self.advance()
         plan = self.plan
-        if self.stage == 4:
-            return ()
         self.stage += 1
         if self.stage == 1:
-            got = [after(v, *others) for v in self.got]
-            self.mine = [k[0] + v[0] for k, v in zip(self.keep, got)]
-            on = [k[1] + v[1] for k, v in zip(self.keep, got)]
-            self.got = [plan.in_plane(v, 3 - way) for v, way in zip(on, self.ways)]
-            return on
-        if self.stage == 2:
-            if plan.columns == 4:
-                got = [after(v, *others) for v in self.got]
-                opposite = [m[1] + v[1] for m, v in zip(self.mine, got)]
-                par = [m[0] + v[0] for m, v in zip(self.mine, got)]
-            else:
-                opposite, par = [v[1] for v in self.done], [v[0] for v in self.done]
-            opposite = jnp.concatenate(opposite)
-            self.par = jnp.concatenate(par)
-            self.got = plan.along_z(opposite, 1)
-            return (opposite,)
+            half = len(values) // 2
+            self.mine = values[:half]
+            self.got = [plan.in_plane(v, 3 - way) for v, way in zip(values[half:], self.ways)]
+        elif self.stage == 2:
+            self.mine = values[:1]
+            self.got = [plan.along_z(values[1], 1)]
+        else:
+            self.mine = values
+        return values
+
+    def advance(self):
         if self.stage == 3:
-            self.par = self.par + after(self.got, *others)
-            far = (0, 1) if self.layer == 1 else (2, 3)
-            self.got = plan.along_z(self.par, 2, far)
-            return (self.par,)
-        self.par = self.par + after(self.got, *others)
-        return (self.par,)
+            return []
+        if self.plan.columns == 4:
+            values = []
+            for rider in self.riders():
+                parts = [
+                    a[i : i + rider.count] + b[j : j + rider.count] for a, i, b, j in rider.segments
+                ]
+                values.append(parts[0] if len(parts) == 1 else jnp.concatenate(parts))
+            return self.take(values)
+        if self.stage == 0:
+            self.stage = 1
+            return []
+        if self.stage == 1:
+            return self.take([jnp.concatenate([w[slot] for w in self.whole]) for slot in range(2)])
+        return self.take([self.mine[0] + self.got[0]])
+
+    def wait(self, *others):
+        if self.plan.columns != 4 and self.stage < 2:
+            return others
+        self.got, others = lax.optimization_barrier((self.got, others))
+        return others
+
+    def after(self, *others):
+        if self.plan.columns == 4 and self.stage < 3:
+            self.got = [after(v, *others) for v in self.got]
+        return self
 
     def finish(self):
-        while self.stage < 4:
+        while self.stage < 3:
             self.advance()
-        return self.par
+        return self.mine[0]
 
 
 def body(
@@ -973,23 +1100,49 @@
     def shard_of(matrix):
         return lax.dynamic_slice_in_dim(matrix, column * count, count, 0)
 
+    local = core == z // 2
+    which = z % 2
+    sequence = 4 * column + z
+
+    def fetch(array):
+        piece = lax.dynamic_slice_in_dim(array, which * LEN, LEN, 0)
+        return piece, plan.permute(piece, lambda zz, d: (zz, d ^ 1) if d % 2 == zz // 2 else None)
+
     tail = jnp.zeros((-vec_count % 8, width), f32)
-    shards = [jnp.concatenate([shard_of(own[0]), own_vec, tail]), shard_of(own[1]), shard_of(own[2])]
-    far, far_opp = [], []
-    for shard in shards:
-        far.append(plan.along_z(after(shard, *far[-1:]), 2))
-    near_attn = plan.along_z(shards[0], 1)
-    far_opp.append(plan.along_z(far[0], 1))
-    near_feed = plan.along_z(after(jnp.concatenate(shards[1:]), far_opp[0]), 1)
-    near_opp = (near_attn, near_feed[:count], near_feed[count:])
-    far_opp += [plan.along_z(far[1], 1), plan.along_z(far[2], 1)]
-    opp = [
-        [jnp.where(low_planes == (layer == 0), near_opp[k], far_opp[k]) for k in range(3)] for layer in range(2)
-    ]
+    shard = jnp.concatenate([shard_of(own[0]), own_vec, tail])
+    far_attn, near_attn = plan.along_z(shard, 2), plan.along_z(shard, 1)
+    mask_parts, token_parts = fetch(after(absorbed, shard)), fetch(after(tokens, shard))
+    far_attn, near_attn, mask_other, token_other, up_shard, down_shard = lax.optimization_barrier(
+        (far_attn, near_attn, mask_parts[1], token_parts[1], shard_of(own[1]), shard_of(own[2]))
+    )
+    opp_attn = plan.along_z(far_attn, 1)
+    far_up = plan.along_z(up_shard, 2)
+    token_parts = (*token_parts, token_other)
 
     near_vec = jnp.stack([own_vec, near_attn[count : count + vec_count]])
-    far_vec = jnp.stack([far[0][count : count + vec_count], far_opp[0][count : count + vec_count]])
+    far_vec = jnp.stack([far_attn[count : count + vec_count], opp_attn[count : count + vec_count]])
     vectors = jnp.stack([jnp.where(low_planes, near_vec, far_vec), jnp.where(low_planes, far_vec, near_vec)])
+
+    def opposite(near, far):
+        return jnp.where(low_planes, near, far), jnp.where(low_planes, far, near)
+
+    attn_opp = opposite(near_attn[:count], opp_attn[:count])
+    attn_groups = [Group(plan, far_attn[:count], 1), Group(plan, attn_opp[0], 2)]
+    near_up = plan.along_z(after(up_shard, attn_opp[0]), 1)
+    far_up, near_up = arrive(attn_groups, far_up, near_up)
+    sent = [group.step() for group in attn_groups]
+    mask_other, token_parts = lax.optimization_barrier((mask_other, token_parts, *sent))[:2]
+    mask_row = jnp.where(local, mask_parts[0], mask_other).astype(f32)
+    step = lax.dynamic_index_in_dim(timesteps, sequence, 0, keepdims=False)
+    step_row = lax.dynamic_slice_in_dim(time_table, step, 1, 0)
+    mask = mask_row[:, None]
+    x = jnp.where(mask > 0.5, mask_embedding[None, :] + step_row, jnp.where(local, token_parts[0], token_parts[2]))
+    weight = LEN / jnp.maximum(jnp.sum(mask_row), 1.0)
+    far_down = plan.along_z(after(down_shard, far_up), 2)
+    opp_up = plan.along_z(far_up, 1)
+    opp_up, x = arrive(attn_groups, opp_up, x)
+    near_down = plan.along_z(after(down_shard, opp_up), 1)
+    up_opp = opposite(near_up, opp_up)
     pair_all = lax.dynamic_index_in_dim(vectors[:, :, 2].reshape(2, 2, 2, 2, inner_half), core, 3, keepdims=False)
     pair_rows = jnp.stack([pair_all[:, :, 0], jnp.zeros_like(pair_all[:, :, 0]), pair_all[:, :, 1]], axis=2)
     pair_cols = pair_rows.reshape(2, 2 * 3 * inner_half, 1)
@@ -1004,154 +1157,171 @@
         for layer in range(2)
     ]
 
-    local = core == z // 2
-    which = z % 2
-
-    def fetch(array):
-        piece = lax.dynamic_slice_in_dim(array, which * LEN, LEN, 0)
-        other = plan.permute(piece, lambda zz, d: (zz, d ^ 1) if d % 2 == zz // 2 else None)
-        return jnp.where(local, piece, other)
-
-    absorbed, tokens, cotangent = (after(v, far[0]) for v in (absorbed, tokens, cotangent))
-    mask_row = fetch(absorbed).astype(f32)
-    sequence = 4 * column + z
-    step = lax.dynamic_index_in_dim(timesteps, sequence, 0, keepdims=False)
-    step_row = lax.dynamic_slice_in_dim(time_table, step, 1, 0)
-    mask = mask_row[:, None]
-    x = jnp.where(mask > 0.5, mask_embedding[None, :] + step_row, fetch(tokens))
-    weight = LEN / jnp.maximum(jnp.sum(mask_row), 1.0)
-    g = fetch(cotangent) * (mask * weight)
-
-    half = count // 2
-    far_group, near_group = Group(plan, far[0], 1), Group(plan, near_attn, 2)
-    rest = [Group(plan, far_opp[0][:half], 1), Group(plan, far_opp[0][half:count], 2)]
-    for group in (far_group, near_group, *rest):
-        group.step()
-    ups = Group(plan, jnp.concatenate([far[1], opp[0][1]]), 1)
-    downs = Group(plan, jnp.concatenate([far[2], opp[0][2]]), 2)
-    lasts = Group(plan, jnp.concatenate([opp[1][1], opp[1][2]]), 1)
-
     def own_rows(matrix):
         return [(matrix, 0, matrix.shape[0], 0, None, 0, "near")]
 
-    attn_pieces = Pieces(
-        own_rows(own[0])
-        + far_group.pieces(0, count, 0, 0, "far")
-        + near_group.pieces(0, count, 1, 0, "near")
-        + (
-            rest[0].pieces(0, half, 1, 0, "far") + rest[1].pieces(0, half, 1, half, "far")
-            if columns == 4
-            else [(plan.whole(far_opp[0][:count]), 0, width, 1, None, 0, "far")]
-        )
-    )
+    def pieces_of(matrix, par, opp):
+        return Pieces(own_rows(matrix) + par.pieces(0, count, 0, 0, "far") + opp)
 
     kept = []
-    added = ()
-    for layer in range(2):
-        vec = vectors[layer]
-        if layer == 0:
-            x = after(x, g, ups.shard)
-        x, xh, xl, x_scale, ph, pl_, wh, wl = attn_in(flags[layer], x, added, vec, pair_cols[layer], attn_pieces)
-        if layer == 0:
-            ph = after(ph, downs.shard, ups.step(ph))
-        oh, ol, lse, *part = attn_heads(ph, pl_, wh, wl, vec)
-        if layer == 0:
-            part[0] = after(part[0], downs.step(part[0]))
-            up_opp, down_opp = ups.pieces(count, count, 1, 0, "all"), downs.pieces(count, count, 1, 0, "all")
-        else:
-            up_opp, down_opp = lasts.pieces(0, count, 1, 0, "all"), lasts.pieces(count, count, 1, 0, "all")
-        up_pieces = Pieces(own_rows(own[1]) + ups.pieces(0, count, 0, 0, "far") + up_opp)
-        y, yh, yl, y_scale, hh, hl, slope, uh, ul = feed_up(
-            flags[layer], x, plan.added(*part), vec, up_rows[layer], up_pieces
-        )
-        down_pieces = Pieces(own_rows(own[2]) + downs.pieces(0, count, 0, 0, "far") + down_opp)
-        *feed_part, dh, dl = feed_down(flags[layer], hh, hl, vec, down_pieces)
-        if layer == 0:
-            feed_part[0] = after(feed_part[0], lasts.step(feed_part[0]))
-        kept.append((vec, xh, xl, x_scale, ph, pl_, wh, wl, oh, ol, lse, yh, yl, y_scale, hh, hl, slope, uh, ul, dh, dl))
-        added = plan.added(*feed_part)
-        x = y
+
+    def keep(layer, *values):
+        kept.append((vectors[layer], *values))
+
+    half = count // 2
+    up_groups = [Group(plan, far_up, 1), Group(plan, up_opp[0], 2)]
+    x, xh, xl, x_scale, ph, pl_, wh, wl = attn_in(
+        flags[0], x, (), vectors[0], pair_cols[0], pieces_of(own[0], attn_groups[0], attn_groups[1].pieces(0, count, 1, 0, "all"))
+    )
+    ph, far_down, near_down, cotangent = arrive(up_groups, ph, far_down, near_down, cotangent)
+    cot_parts = fetch(cotangent)
+    opp_down = plan.along_z(far_down, 1)
+    for group in up_groups:
+        group.step()
+    oh, ol, lse, *part = attn_heads(ph, pl_, wh, wl, vectors[0])
+    opp_down, *part = arrive(up_groups, opp_down, *part)
+    down_opp = opposite(near_down, opp_down)
+    down_groups = [Group(plan, far_down, 1), Group(plan, down_opp[0], 2)]
+    added = plan.added(*part)
+    added = added[:2] + arrive(down_groups, *added[2:])
+    for group in down_groups:
+        group.step()
+    if columns == 4:
+        last_attn = [Group(plan, attn_opp[1][:half], 1), Group(plan, attn_opp[1][half:], 2)]
+    else:
+        last_attn = [Group(plan, attn_opp[1], 1)]
+    y, yh, yl, y_scale, hh, hl, slope, uh, ul = feed_up(
+        flags[0], x, added, vectors[0], up_rows[0], pieces_of(own[1], up_groups[0], up_groups[1].pieces(0, count, 1, 0, "all"))
+    )
+    hh, cot_other = arrive(last_attn, hh, cot_parts[1])
+    for group in last_attn:
+        group.step()
+    *feed_part, dh, dl = feed_down(
+        flags[0], hh, hl, vectors[0], pieces_of(own[2], down_groups[0], down_groups[1].pieces(0, count, 1, 0, "all"))
+    )
+    keep(0, xh, xl, x_scale, ph, pl_, wh, wl, oh, ol, lse, yh, yl, y_scale, hh, hl, slope, uh, ul, dh, dl)
+
+    g = jnp.where(local, cot_parts[0], after(cot_other, dh)) * (mask * weight)
+    last_groups = [Group(plan, up_opp[1], 1), Group(plan, down_opp[1], 2)]
+    feed_part = arrive([*last_attn, *last_groups], *feed_part)
+    for group in last_groups:
+        group.step()
+    added = plan.added(*feed_part)
+    if columns == 4:
+        attn_last = last_attn[0].pieces(0, half, 1, 0, "all") + last_attn[1].pieces(0, half, 1, half, "all")
+    else:
+        attn_last = last_attn[0].pieces(0, count, 1, 0, "all")
+    x, xh, xl, x_scale, ph, pl_, wh, wl = attn_in(
+        flags[1], y, added, vectors[1], pair_cols[1], pieces_of(own[0], attn_groups[0], attn_last)
+    )
+    oh, ol, lse, *part = attn_heads(ph, pl_, wh, wl, vectors[1])
+    added = plan.added(*arrive(last_groups, *part))
+    y, yh, yl, y_scale, hh, hl, slope, uh, ul = feed_up(
+        flags[1], x, added, vectors[1], up_rows[1], pieces_of(own[1], up_groups[0], last_groups[0].pieces(0, count, 1, 0, "all"))
+    )
+    *feed_part, dh, dl = feed_down(
+        flags[1], hh, hl, vectors[1], pieces_of(own[2], down_groups[0], last_groups[1].pieces(0, count, 1, 0, "all"))
+    )
+    keep(1, xh, xl, x_scale, ph, pl_, wh, wl, oh, ol, lse, yh, yl, y_scale, hh, hl, slope, uh, ul, dh, dl)
+    x, added = y, plan.added(*feed_part)
     last = (x, *added)
 
     quarter = width // plan.planes
-
-    def spread(value):
-        def cut(plane):
-            cols = lax.dynamic_slice_in_dim(value, plane * quarter, quarter, 1)
-            return jnp.concatenate([cols[: LEN // 2], cols[LEN // 2 :]], axis=1)
-
-        def open_up(packed):
-            return jnp.concatenate([packed[:, :quarter], packed[:, quarter:]], axis=0)
-
-        arrived = [cut(z)]
-        for step in range(1, plan.planes):
-            arrived.append(
-                plan.permute(cut(z ^ step), lambda zz, d: (zz ^ step, d) if d % 2 == zz // 2 else None)
-            )
-        result = []
-        for index in range(2):
-            distance = z ^ (2 * core + index)
-            result.append(open_up(lax.select_n(distance, *arrived)))
-        return jnp.concatenate(result, axis=0)
-
-    def steps(token, *numbers):
-        return [v for number in numbers for v in sums[number].advance(token)]
-
-    pulled = ()
+    plane_flags = jnp.stack([z, core]).astype(jnp.int32)
+
+    def beside(value):
+        return plan.permute(value, lambda zz, d: (zz ^ 1, d) if d % 2 == zz // 2 else None)
+
+    def beyond(mine, theirs):
+        both = jnp.concatenate([mine[:, quarter:], theirs[:, quarter:]], axis=1)
+        return plan.permute(both, lambda zz, d: (zz ^ 2, d) if d % 2 == zz // 2 else None)
+
+    def settle_rows(mine, theirs, arrived):
+        first = jnp.where(local, mine[:, :quarter], arrived[:, :quarter])
+        second = jnp.where(local, theirs[:, :quarter], arrived[:, quarter:])
+        odd = z % 2 == 1
+        return jnp.concatenate([jnp.where(odd, second, first), jnp.where(odd, first, second)])
+
+    def ride(kernel, riding, *args):
+        lists = [total.riders() for total in riding]
+        values = list(kernel(*args, riders=[r for some in lists for r in some]))
+        taken = sum(len(some) for some in lists)
+        results, extra = values[: len(values) - taken], values[len(values) - taken :]
+        for total, some in zip(riding, lists):
+            total.take(extra[: len(some)])
+            extra = extra[len(some) :]
+        return results
+
     small = [None] * 2
-    sums = []
-    for layer in (1, 0):
-        (vec, xh, xl, x_scale, ph, pl_, wh, wl, oh, ol, lse, yh, yl, y_scale, hh, hl, slope, uh, ul, dh, dl) = kept[layer]
-        order = 1 if layer == 1 else 2
-        g, duh, dul, *pieces, up_bias_sum, down_bias_sum = feed_back_one(
-            order, flags[layer], g, pulled, dh, dl, hh, hl, slope
-        )
-        sums.append(Sum(plan, layer, order, pieces))
-        if layer == 1:
-            final = after(last[0], up_bias_sum) + jnp.concatenate([last[1] + last[3], last[2] + last[4]])
-            out_rows = spread(final)
-        else:
-            duh = after(duh, *steps(up_bias_sum, 0, 1))
-        *e, ffn_vec = feed_back_two("e", 0, flags[layer], duh, dul, yh, yl, vec, uh, ul)
-        e = plan.added(*e)
-        duh = after(duh, ffn_vec)
-        if layer == 0:
-            duh = after(duh, *steps(ffn_vec, 2))
-        pieces = feed_back_two("w", 3 - order, flags[layer], duh, dul, yh, yl, vec, uh, ul)
-        sums.append(Sum(plan, layer, 3 - order, pieces))
-        g, e = after(g, pieces[0]), (*e[:2], after(e[2], pieces[0]), after(e[3], pieces[0]))
-        if layer == 0:
-            g = after(g, *steps(pieces[0], 1, 2))
-        g, doh, dol, do, out_bias_sum = attn_back_one(g, e, yh, yl, y_scale, wh, wl, oh, ol)
-        grads = attn_heads_back(ph, pl_, doh, dol, oh, ol, lse)
-        if layer == 1:
-            do, first = after(do, *steps(grads[0], 0, 1)), after(grads[0], out_rows)
-            *e, attn_vec = attn_back_two("e", 0, flags[layer], [first, *grads[1:]], xh, xl, vec, wh, wl, do)
-            e = plan.added(*e)
-            do = after(do, *steps(attn_vec, 0))
-            *pieces, pair_sum = attn_back_two("w", order, flags[layer], grads, xh, xl, vec, wh, wl, do)
-            sums.append(Sum(plan, layer, order, pieces))
-            g = after(g, pair_sum, *steps(pair_sum, 0, 1))
-            e = (*e[:2], after(e[2], pair_sum), after(e[3], pair_sum))
-        else:
-            do = after(do, *steps(grads[0], 2, 3, 4))
-            *pieces, pair_sum = attn_back_two("w", 3, flags[layer], grads, xh, xl, vec, wh, wl, do)
-            sums.append(Sum(plan, layer, 3, pieces))
-            first = after(grads[0], *steps(pair_sum, 3))
-            *e, attn_vec = attn_back_two("e", 0, flags[layer], [first, *grads[1:]], xh, xl, vec, wh, wl, do)
-            e = plan.added(*e)
-        pulled = (*e, xh, xl, x_scale)
-        small[layer] = (attn_vec, pair_sum, out_bias_sum, ffn_vec, up_bias_sum, down_bias_sum)
-    input_grad, row_sum = finish(g, pulled[:4], *pulled[4:], mask)
-    grad_rows = spread(input_grad)
+    (vec, xh, xl, x_scale, ph, pl_, wh, wl, oh, ol, lse, yh, yl, y_scale, hh, hl, slope, uh, ul, dh, dl) = kept[1]
+    g, duh, dul, *pieces, up_bias_sum, down_bias_sum = feed_back_one(1, flags[1], g, (), dh, dl, hh, hl, slope)
+    down_1 = Sum(plan, 1, pieces)
+    out_near, out_far = leave(plane_flags, after(last[0], up_bias_sum), last[1:])
+    out_beside = beside(out_far)
+    *e, ffn_vec = feed_back_two("e", 0, flags[1], after(duh, out_near), dul, yh, yl, vec, uh, ul)
+    e = plan.added(*e)
+    pieces = feed_back_two("w", 2, flags[1], after(duh, ffn_vec), dul, yh, yl, vec, uh, ul)
+    up_1 = Sum(plan, 2, pieces)
+    g, out_beside, *others = lax.optimization_barrier((g, out_beside, *e[2:], pieces[0]))[:4]
+    g, doh, dol, do, out_bias_sum = attn_back_one(g, (*e[:2], *others), yh, yl, y_scale, wh, wl, oh, ol)
+    grads = attn_heads_back(ph, pl_, doh, dol, oh, ol, lse)
+    *e, attn_vec = ride(attn_back_two, [down_1], "e", 0, flags[1], grads, xh, xl, vec, wh, wl, do)
+    e = plan.added(*e)
+    out_beyond = beyond(out_near, after(out_beside, attn_vec))
+    *pieces, pair_sum = ride(attn_back_two, [up_1], "w", 2, flags[1], grads, xh, xl, vec, wh, wl, after(do, attn_vec))
+    attn_1 = Sum(plan, 2, pieces)
+    g, *others = lax.optimization_barrier((g, *e[2:], pair_sum))[:3]
+    pulled = (*e[:2], *others, xh, xl, x_scale)
+    small[1] = (attn_vec, pair_sum, out_bias_sum, ffn_vec, up_bias_sum, down_bias_sum)
+
+    (vec, xh, xl, x_scale, ph, pl_, wh, wl, oh, ol, lse, yh, yl, y_scale, hh, hl, slope, uh, ul, dh, dl) = kept[0]
+    g, duh, dul, *pieces, up_bias_sum, down_bias_sum = feed_back_one(1, flags[0], g, pulled, dh, dl, hh, hl, slope)
+    down_0 = Sum(plan, 1, pieces)
+    feed_1 = down_1.merge(up_1)
+    duh, out_beyond = lax.optimization_barrier((duh, out_beyond))
+    *e, ffn_vec = ride(feed_back_two, [feed_1], "e", 0, flags[0], duh, dul, yh, yl, vec, uh, ul)
+    e = plan.added(*e)
+    pieces = feed_back_two("w", 3, flags[0], after(duh, ffn_vec), dul, yh, yl, vec, uh, ul)
+    up_0 = Sum(plan, 3, pieces)
+    g, *others = lax.optimization_barrier((g, *e[2:], pieces[0]))[:3]
+    g, doh, dol, do, out_bias_sum = ride(
+        attn_back_one, [feed_1, attn_1, down_0], g, (*e[:2], *others), yh, yl, y_scale, wh, wl, oh, ol
+    )
+    grads = attn_heads_back(ph, pl_, doh, dol, oh, ol, lse)
+    mixed = attn_1.merge(down_0)
+    *pieces, pair_sum = ride(attn_back_two, [mixed, up_0], "w", 3, flags[0], grads, xh, xl, vec, wh, wl, do)
+    attn_0 = Sum(plan, 3, pieces)
+    *e, attn_vec = attn_back_two("e", 0, flags[0], [after(grads[0], pair_sum), *grads[1:]], xh, xl, vec, wh, wl, do)
+    e = plan.added(*mixed.wait(*up_0.wait(*e)))
+    small[0] = (attn_vec, pair_sum, out_bias_sum, ffn_vec, up_bias_sum, down_bias_sum)
+    grad_near, grad_far, row_sum = ride(finish, [up_0, mixed], plane_flags, g, e, xh, xl, x_scale, mask)
+    out_rows = settle_rows(out_near, out_beside, out_beyond)
 
     pack_flags = jnp.stack([z % 2, core, sequence]).astype(jnp.int32)
-    table = plan.all_sum(pack(pack_flags, small, row_sum, columns, timesteps.shape[0]))
-
-    def settle(index):
-        return jnp.where(low_planes, sums[3 + index].finish(), sums[index].finish())
-
-    down_mine, up_mine, attn_mine = (settle(index) for index in range(3))
+    grad_beside = beside(grad_far)
+    table = pack(pack_flags, small, row_sum, columns, timesteps.shape[0])
+
+    def cross(low, high):
+        on = jnp.where(low_planes, high, low)
+        return jnp.where(low_planes, low, high), on, plan.along_z(on, 2)
+
+    feed_1, mixed = feed_1.finish(), mixed.finish()
+    down_mine, down_on, down_got = cross(mixed[count:], feed_1[:count])
+    table = plan.sum_step(table, 0)
+    down_got, table = attn_0.wait(down_got, table)
+    attn_0.advance()
+    table, grad_beside = up_0.wait(*attn_0.wait(table, grad_beside))
+    attn_0.advance()
+    up_mine, up_on, up_got = cross(up_0.finish(), feed_1[count:])
+    table = plan.sum_step(table, 1)
+    up_got, table = attn_0.wait(up_got, table)
+    attn_mine, attn_on, attn_got = cross(attn_0.finish(), mixed[:count])
+    grad_beside, table = lax.optimization_barrier((grad_beside, table, attn_on))[:2]
+    grad_beyond = beyond(grad_near, grad_beside)
+    for step in (2, 3, 4):
+        table = plan.sum_step(table, step)
+    grad_rows = settle_rows(grad_near, grad_beside, grad_beyond)
+    down_mine, up_mine, attn_mine = down_mine + down_got, up_mine + up_got, attn_mine + attn_got
 
     def exchange(rows_all):
         halves = rows_all.reshape(2, -1, width)

time: 960 us -> 862 us (0.90)
  waiting for transfers between devices: 279 us -> 201 us
  other arithmetic: 104 us -> 56.3 us
  Pallas kernels: 389 us -> 408 us
    ppermute x80 -> x82, waiting for transfers between devices: 279 us -> 201 us  [permute(): return lax.ppermute(value, AXES, pairs)]
    add x31 -> x11, other arithmetic: 62.2 us -> 7.95 us  [the longest x4 2.96 us: advance(): a[i:i + rider.count] + b[j:j + rider.count]]
    pallas_call x24 -> x25, Pallas kernels: 389 us -> 408 us  [call(): pl.pallas_call(whole, grid=(grid,), in_specs=in_specs, out_specs=list(out...]
    unnamed x136 -> x170, local copies, waits for them, and re-layouts: 24.9 us -> 27.3 us
    ppermute x80 -> x82, starting transfers between devices: 105 us -> 104 us  [permute(): return lax.ppermute(value, AXES, pairs)]
  transfers between devices with their start and end apart: 80 -> 82, of which waited for: 31 -> 27; matrix products, arithmetic and copies ran while one was open for 15% -> 12% of each run, Pallas kernels for 33% -> 42%
where the time goes in v2:
time: 862 us; the launch traced here: 853 us
  Pallas kernels  408 us (47%)
  waiting for transfers between devices  201 us (23%)
  starting transfers between devices  104 us (12%)
  local copies, waits for them, and re-layouts  76.7 us (9%)
  other arithmetic  56.3 us (7%)
    pallas_call x25, Pallas kernels, call(): pl.pallas_call(whole, grid=(grid,), in_specs=in_specs, out_specs=list(out...  408 us
    ppermute x82, waiting for transfers between devices, permute(): return lax.ppermute(value, AXES, pairs)  201 us
    ppermute x82, starting transfers between devices, permute(): return lax.ppermute(value, AXES, pairs)  104 us
    unnamed x170, local copies, waits for them, and re-layouts  27.3 us
  transfers between devices with their start and end apart: 82, of which 27 were waited for; matrix products, arithmetic and copies ran while one was open for 12% of the time, Pallas kernels for 42%

profile of v2, /device:TPU:0, one launch (start us, length us, event | category | flops | bytes accessed | tf_op | source)
XLA Modules:
  0.0 853.2 jit_solution(9420757843834864145)
XLA Ops:
  38.3 13.1 %collective-permute-done = f32[208,768]{1,0:T(8,128)} collective-permute-done((f32[208,768]{1,0:T(8,128)}, f32[208,768]{1,0:T(8,128)}, u32[]{:S(2)}, u32[]{:S(2)}) %collective-permute-start) | collective-permute-done | bytes 639008 | tf_op jit(solution)/shard_map/ppermute | solution.py:911
  61.4 15.1 %collective-permute-done.5 = f32[208,768]{1,0:T(8,128)} collective-permute-done((f32[208,768]{1,0:T(8,128)}, f32[208,768]{1,0:T(8,128)}, u32[]{:S(2)}, u32[]{:S(2)}) %collective-permute-start.5) | collective-permute-done | bytes 639008 | tf_op jit(solution)/shard_map/ppermute | solution.py:911
  113.5 18.1 %collective-permute-done.12 = f32[192,768]{1,0:T(8,128)S(1)} collective-permute-done((f32[192,768]{1,0:T(8,128)S(1)}, f32[192,768]{1,0:T(8,128)S(1)}, u32[]{:S(2)}, u32[]{:S(2)}) %collective-permute-start.12) | collective-permute-done | bytes 589856 | tf_op jit(solution)/shard_map/ppermute | solution.py:911
  137.6 13.5 %attn_in.2 = (bf16[1024,768]{1,0:T(8,128)(2,1)}, bf16[1024,768]{1,0:T(8,128)(2,1)}, f32[1024,1]{1,0:T(8,128)}, bf16[1152,1024]{1,0:T(8,128)(2,1)}, bf16[1152,102...) custom-call(s32[5]{0:T(128)} %get-tuple-element.591.refs_0_, ...), custom_call_target="tpu_custom_call" | custom-call | flops 1 | bytes 1 | tf_op jit(solution)/shard_map/attn_in/pallas_call | solution.py:194
  163.7 20.0 %attn_heads.2 = (bf16[384,1024]{1,0:T(8,128)(2,1)}, bf16[384,1024]{1,0:T(8,128)(2,1)}, f32[6,1,1024]{2,1,0:T(1,128)}, f32[512,768]{1,0:T(8,128)}, f32[512,768]{1,0:T(8,128)}) custom-call(bf16[1152,1024]{1,0:T(8,128)(2,1)} %get-tuple-element.275.refs_0_.refs_2_.refs_4_, bf16[1152,1024]{1,0:T(8,128)(2,1)} %get-tuple-element.276.refs_1_.refs_3_.refs_5_, ...), custom_call_target="tpu_custom_call" | custom-call | flops 1 | bytes 1 | tf_op jit(solution)/shard_map/attn_heads/pallas_call | solution.py:194
  188.4 11.3 %collective-permute-done.21.refs_6_ = f32[192,768]{1,0:T(8,128)S(1)} collective-permute-done((f32[192,768]{1,0:T(8,128)S(1)}, f32[192,768]{1,0:T(8,128)S(1)}, u32[]{:S(2)}, u32[]{:S(2)}) %collective-permute-start.21) | collective-permute-done | bytes 589856 | tf_op jit(solution)/shard_map/ppermute | solution.py:911
  210.7 19.3 %feed_up.2 = (f32[1024,768]{1,0:T(8,128)}, bf16[1024,768]{1,0:T(8,128)(2,1)}, bf16[1024,768]{1,0:T(8,128)(2,1)}, f32[1024,1]{1,0:T(8,128)}, bf16[1024,1536]{1,0:...) custom-call(s32[5]{0:T(128)} %get-tuple-element.591.refs_0_, ...), custom_call_target="tpu_custom_call" | custom-call | flops 1 | bytes 1 | tf_op jit(solution)/shard_map/feed_up/pallas_call | solution.py:194
  247.4 15.7 %feed_down.2 = (f32[512,768]{1,0:T(8,128)}, f32[512,768]{1,0:T(8,128)}, bf16[2,768,768]{2,1,0:T(8,128)(2,1)}, bf16[2,768,768]{2,1,0:T(8,128)(2,1)}) custom-call(s32[5]{0:T(128)} %get-tuple-element.591.refs_0_, bf16[1024,1536]{1,0:T(8,128)(2,1)} %get-tuple-element.291.refs_1_.refs_11_, bf16[1024,1536]{1,0:T(8,128)(2,1)} %get-tuple-element.292.refs_2_.refs_12_, ...), custom_call_target="tpu_custom_call" | custom-call | flops 1 | bytes 1 | tf_op jit(solution)/shard_map/feed_down/pallas_call | solution.py:194
  272.6 16.2 %attn_in.3 = (f32[1024,768]{1,0:T(8,128)}, bf16[1024,768]{1,0:T(8,128)(2,1)}, bf16[1024,768]{1,0:T(8,128)(2,1)}, f32[1024,1]{1,0:T(8,128)}, bf16[1152,1024]{1,0:...) custom-call(s32[5]{0:T(128)} %get-tuple-element.590.refs_0_, ...), custom_call_target="tpu_custom_call" | custom-call | flops 1 | bytes 1 | tf_op jit(solution)/shard_map/attn_in/pallas_call | solution.py:194
  288.9 20.0 %attn_heads.3 = (bf16[384,1024]{1,0:T(8,128)(2,1)}, bf16[384,1024]{1,0:T(8,128)(2,1)}, f32[6,1,1024]{2,1,0:T(1,128)}, f32[512,768]{1,0:T(8,128)}, f32[512,768]{1,0:T(8,128)}) custom-call(bf16[1152,1024]{1,0:T(8,128)(2,1)} %get-tuple-element.309.refs_0_.refs_2_.refs_4_, bf16[1152,1024]{1,0:T(8,128)(2,1)} %get-tuple-element.310.refs_1_.refs_3_.refs_5_, ...), custom_call_target="tpu_custom_call" | custom-call | flops 1 | bytes 1 | tf_op jit(solution)/shard_map/attn_heads/pallas_call | solution.py:194
  316.9 19.2 %feed_up.3 = (f32[1024,768]{1,0:T(8,128)}, bf16[1024,768]{1,0:T(8,128)(2,1)}, bf16[1024,768]{1,0:T(8,128)(2,1)}, f32[1024,1]{1,0:T(8,128)}, bf16[1024,1536]{1,0:...) custom-call(s32[5]{0:T(128)} %get-tuple-element.590.refs_0_, ...), custom_call_target="tpu_custom_call" | custom-call | flops 1 | bytes 1 | tf_op jit(solution)/shard_map/feed_up/pallas_call | solution.py:194
  336.1 16.1 %feed_down.3 = (f32[512,768]{1,0:T(8,128)}, f32[512,768]{1,0:T(8,128)}, bf16[2,768,768]{2,1,0:T(8,128)(2,1)}, bf16[2,768,768]{2,1,0:T(8,128)(2,1)}) custom-call(s32[5]{0:T(128)} %get-tuple-element.590.refs_0_, bf16[1024,1536]{1,0:T(8,128)(2,1)} %get-tuple-element.318.refs_1_.refs_4_, bf16[1024,1536]{1,0:T(8,128)(2,1)} %get-tuple-element.319.refs_2_.refs_5_, ...), custom_call_target="tpu_custom_call" | custom-call | flops 1 | bytes 1 | tf_op jit(solution)/shard_map/feed_down/pallas_call | solution.py:194
  357.4 23.6 %feed_back_one.2 = (f32[1024,768]{1,0:T(8,128)}, bf16[1024,1536]{1,0:T(8,128)(2,1)}, bf16[1024,1536]{1,0:T(8,128)(2,1)}, f32[2,2,192,768]{3,2,1,0:T(8,128)}, f32...) custom-call(s32[5]{0:T(128)} %get-tuple-element.590.refs_0_, ...), custom_call_target="tpu_custom_call" | custom-call | flops 1 | bytes 1 | tf_op jit(solution)/shard_map/feed_back_one/pallas_call | solution.py:194
  391.1 13.3 %feed_back_two_e.2 = (f32[512,768]{1,0:T(8,128)}, f32[512,768]{1,0:T(8,128)}, f32[4,768]{1,0:T(4,128)}) custom-call(s32[5]{0:T(128)} %get-tuple-element.590.refs_0_, bf16[1024,1536]{1,0:T(8,128)(2,1)} %get-tuple-element.342.refs_1_, bf16[1024,1536]{1,0:T(8,128)(2,1)} %get-tuple-element.334.refs_2_, bf16[1024,768]{1,0:T(8,128)(2,1)} %get-tuple-element.335.refs_3_.refs_5_, ...), custom_call_target="tpu_custom_call" | custom-call | flops 1 | bytes 1 | tf_op jit(solution)/shard_map/feed_back_two_e/pallas_call | solution.py:194
  405.2 13.1 %feed_back_two_w.2 = (f32[2,2,192,768]{3,2,1,0:T(8,128)}, f32[2,2,192,768]{3,2,1,0:T(8,128)}) custom-call(s32[5]{0:T(128)} %get-tuple-element.590.refs_0_, bf16[1024,1536]{1,0:T(8,128)(2,1)} %get-tuple-element.342.refs_1_, bf16[1024,1536]{1,0:T(8,128)(2,1)} %get-tuple-element.334.refs_2_, bf16[1024,768]{1,0:T(8,128)(2,1)} %get-tuple-element.335.refs_3_.refs_5_, ...), custom_call_target="tpu_custom_call" | custom-call | flops 1 | bytes 1 | tf_op jit(solution)/shard_map/feed_back_two_w/pallas_call | solution.py:194
  419.5 11.3 %attn_back_one.2 = (f32[1024,768]{1,0:T(8,128)}, bf16[384,1024]{1,0:T(8,128)(2,1)}, bf16[384,1024]{1,0:T(8,128)(2,1)}, f32[384,768]{1,0:T(8,128)}, f32[1,768]{1,0:T(1,128)}) custom-call(f32[1024,768]{1,0:T(8,128)} %get-tuple-element.345.refs_0_, f32[512,768]{1,0:T(8,128)} %get-tuple-element.339.refs_1_, f32[512,768]{1,0:T(8,128)} %get-tuple-element.340.refs_2_, ...), custom_call_target="tpu_custom_call" | custom-call | flops 1 | bytes 1 | tf_op jit(solution)/shard_map/attn_back_one/pallas_call | solution.py:194
  430.8 28.4 %attn_heads_back.2 = (bf16[384,1024]{1,0:T(8,128)(2,1)}, bf16[384,1024]{1,0:T(8,128)(2,1)}, bf16[384,1024]{1,0:T(8,128)(2,1)}, bf16[384,1024]{1,0:T(8,128)(2,1)}...) custom-call(bf16[1152,1024]{1,0:T(8,128)(2,1)} %get-tuple-element.309.refs_0_.refs_2_.refs_4_, ...), custom_call_target="tpu_custom_call" | custom-call | flops 1 | bytes 1 | tf_op jit(solution)/shard_map/attn_heads_back/pallas_call | solution.py:194
  460.6 14.7 %attn_back_two_e.2 = (f32[512,768]{1,0:T(8,128)}, f32[512,768]{1,0:T(8,128)}, f32[4,768]{1,0:T(4,128)}, f32[384,768]{1,0:T(8,128)}, f32[384,768]{1,0:T(8,128)}) custom-call(s32[5]{0:T(128)} %get-tuple-element.590.refs_0_, bf16[384,1024]{1,0:T(8,128)(2,1)} %get-tuple-element.355.refs_1_, bf16[384,1024]{1,0:T(8,128)(2,1)} %get-tuple-element.356.refs_2_, ...), custom_call_target="tpu_custom_call" | custom-call | flops 1 | bytes 1 | tf_op jit(solution)/shard_map/attn_back_two_e/pallas_call | solution.py:194
  488.1 15.2 %attn_back_two_w.2 = (f32[2,2,192,768]{3,2,1,0:T(8,128)}, f32[2,2,192,768]{3,2,1,0:T(8,128)}, f32[2,8,576]{2,1,0:T(8,128)}, f32[384,768]{1,0:T(8,128)}, f32[384,768]{1,0:T(8,128)}) custom-call(s32[5]{0:T(128)} %get-tuple-element.590.refs_0_, bf16[384,1024]{1,0:T(8,128)(2,1)} %get-tuple-element.355.refs_1_, bf16[384,1024]{1,0:T(8,128)(2,1)} %get-tuple-element.356.refs_2_, ...), custom_call_target="tpu_custom_call" | custom-call | flops 1 | bytes 1 | tf_op jit(solution)/shard_map/attn_back_two_w/pallas_call | solution.py:194
  506.9 27.2 %feed_back_one.3 = (f32[1024,768]{1,0:T(8,128)}, bf16[1024,1536]{1,0:T(8,128)(2,1)}, bf16[1024,1536]{1,0:T(8,128)(2,1)}, f32[2,2,192,768]{3,2,1,0:T(8,128)}, f32...) custom-call(s32[5]{0:T(128)} %get-tuple-element.591.refs_0_, f32[1024,768]{1,0:T(8,128)} %get-tuple-element.372.refs_1_, ...), custom_call_target="tpu_custom_call" | custom-call | flops 1 | bytes 1 | tf_op jit(solution)/shard_map/feed_back_one/pallas_call | solution.py:194
  536.3 15.1 %feed_back_two_e.3 = (f32[512,768]{1,0:T(8,128)}, f32[512,768]{1,0:T(8,128)}, f32[4,768]{1,0:T(4,128)}, f32[384,768]{1,0:T(8,128)}, f32[384,768]{1,0:T(8,128)}) custom-call(s32[5]{0:T(128)} %get-tuple-element.591.refs_0_, bf16[1024,1536]{1,0:T(8,128)(2,1)} %get-tuple-element.395.refs_1_, bf16[1024,1536]{1,0:T(8,128)(2,1)} %get-tuple-element.383.refs_2_, ...), custom_call_target="tpu_custom_call" | custom-call | flops 1 | bytes 1 | tf_op jit(solution)/shard_map/feed_back_two_e/pallas_call | solution.py:194
  553.6 13.6 %feed_back_two_w.3 = (f32[2,2,96,768]{3,2,1,0:T(8,128)}, f32[2,2,96,768]{3,2,1,0:T(8,128)}, f32[2,2,96,768]{3,2,1,0:T(8,128)}, f32[2,2,96,768]{3,2,1,0:T(8,128)}) custom-call(s32[5]{0:T(128)} %get-tuple-element.591.refs_0_, bf16[1024,1536]{1,0:T(8,128)(2,1)} %get-tuple-element.395.refs_1_, bf16[1024,1536]{1,0:T(8,128)(2,1)} %get-tuple-element.383.refs_2_, ...), custom_call_target="tpu_custom_call" | custom-call | flops 1 | bytes 1 | tf_op jit(solution)/shard_map/feed_back_two_w/pallas_call | solution.py:194
  569.2 11.0 %collective-permute-done.52.refs_13_ = f32[384,768]{1,0:T(8,128)} collective-permute-done((f32[384,768]{1,0:T(8,128)}, f32[384,768]{1,0:T(8,128)}, u32[]{:S(2)}, u32[]{:S(2)}) %collective-permute-start.52) | collective-permute-done | bytes 1179680 | tf_op jit(solution)/shard_map/ppermute | solution.py:911
  588.7 15.3 %attn_back_one.3 = (f32[1024,768]{1,0:T(8,128)}, bf16[384,1024]{1,0:T(8,128)(2,1)}, bf16[384,1024]{1,0:T(8,128)(2,1)}, f32[384,768]{1,0:T(8,128)}, f32[1,768]{1,...) custom-call(f32[1024,768]{1,0:T(8,128)} %get-tuple-element.397.refs_, ...), custom_call_target="tpu_custom_call" | custom-call | flops 1 | bytes 1 | tf_op jit(solution)/shard_map/attn_back_one/pallas_call | solution.py:194
  605.8 28.3 %attn_heads_back.3 = (bf16[384,1024]{1,0:T(8,128)(2,1)}, bf16[384,1024]{1,0:T(8,128)(2,1)}, bf16[384,1024]{1,0:T(8,128)(2,1)}, bf16[384,1024]{1,0:T(8,128)(2,1)}...) custom-call(bf16[1152,1024]{1,0:T(8,128)(2,1)} %get-tuple-element.275.refs_0_.refs_2_.refs_4_, ...), custom_call_target="tpu_custom_call" | custom-call | flops 1 | bytes 1 | tf_op jit(solution)/shard_map/attn_heads_back/pallas_call | solution.py:194
  635.9 17.0 %attn_back_two_w.3 = (f32[2,2,96,768]{3,2,1,0:T(8,128)}, f32[2,2,96,768]{3,2,1,0:T(8,128)}, f32[2,2,96,768]{3,2,1,0:T(8,128)}, f32[2,2,96,768]{3,2,1,0:T(8,128)}...) custom-call(s32[5]{0:T(128)} %get-tuple-element.591.refs_0_, ...), custom_call_target="tpu_custom_call" | custom-call | flops 1 | bytes 1 | tf_op jit(solution)/shard_map/attn_back_two_w/pallas_call | solution.py:194
  657.0 13.5 %attn_back_two_e.3 = (f32[512,768]{1,0:T(8,128)}, f32[512,768]{1,0:T(8,128)}, f32[4,768]{1,0:T(4,128)}) custom-call(s32[5]{0:T(128)} %get-tuple-element.591.refs_0_, bf16[384,1024]{1,0:T(8,128)(2,1)} %get-tuple-element.433.refs_1_, bf16[384,1024]{1,0:T(8,128)(2,1)} %get-tuple-element.414.refs_2_, bf16[384,1024]{1,0:T(8,128)(2,1)} %get-tuple-element.415.refs_3_, ...), custom_call_target="tpu_custom_call" | custom-call | flops 1 | bytes 1 | tf_op jit(solution)/shard_map/attn_back_two_e/pallas_call | solution.py:194
  691.0 10.7 %collective-permute-start.67 = (f32[192,768]{1,0:T(8,128)}, f32[192,768]{1,0:T(8,128)}, u32[]{:S(2)}, u32[]{:S(2)}) collective-permute-start(f32[192,768]{1,0:T(8,128)} %slice_select_fusion.8), channel_id=1, source_target_pairs={{0,16},{1,17},{2,18},{3,19},{4,20},{5,21},{6,22},{7,23},{8,24},{9,... | collective-permute-start | bytes 1769480 | tf_op jit(solution)/shard_map/ppermute | solution.py:911
  709.0 19.3 %collective-permute-done.67 = f32[192,768]{1,0:T(8,128)} collective-permute-done((f32[192,768]{1,0:T(8,128)}, f32[192,768]{1,0:T(8,128)}, u32[]{:S(2)}, u32[]{:S(2)}) %collective-permute-start.67) | collective-permute-done | bytes 589856 | tf_op jit(solution)/shard_map/ppermute | solution.py:911
  733.7 10.9 %collective-permute-done.69 = f32[192,768]{1,0:T(8,128)S(1)} collective-permute-done((f32[192,768]{1,0:T(8,128)S(1)}, f32[192,768]{1,0:T(8,128)S(1)}, u32[]{:S(2)}, u32[]{:S(2)}) %collective-permute-start.69) | collective-permute-done | bytes 589856 | tf_op jit(solution)/shard_map/ppermute | solution.py:911
  758.1 16.5 %collective-permute-done.72 = f32[192,768]{1,0:T(8,128)S(1)} collective-permute-done((f32[192,768]{1,0:T(8,128)S(1)}, f32[192,768]{1,0:T(8,128)S(1)}, u32[]{:S(2)}, u32[]{:S(2)}) %collective-permute-start.72) | collective-permute-done | bytes 589856 | tf_op jit(solution)/shard_map/ppermute | solution.py:911
  806.5 23.7 %collective-permute-done.78 = f32[56,768]{1,0:T(8,128)} collective-permute-done((f32[56,768]{1,0:T(8,128)}, f32[56,768]{1,0:T(8,128)}, u32[]{:S(2)}, u32[]{:S(2)}) %collective-permute-start.78) | collective-permute-done | bytes 172064 | tf_op jit(solution)/shard_map/ppermute | solution.py:911
  (439 shorter events, 308.8 us)
Async XLA Ops:
  15.6 35.9 %collective-permute-start.3 = (f32[1024,768]{1,0:T(8,128)}, f32[1024,768]{1,0:T(8,128)}, u32[]{:S(2)}, u32[]{:S(2)}) collective-permute-start(f32[1024,768]{1,0:T(8,128)} %constant_dynamic-slice_fusion.11), channel_id=1, source_target_pairs={{0,1},{2,3},{4,5},{6,7},{8,9},{10,11},{12,13},{14,15},{17,16},{19,... | collective-permute-start | bytes 9437192 | tf_op jit(solution)/shard_map/ppermute | solution.py:911
  19.7 31.8 %collective-permute-start = (f32[208,768]{1,0:T(8,128)}, f32[208,768]{1,0:T(8,128)}, u32[]{:S(2)}, u32[]{:S(2)}) collective-permute-start(f32[208,768]{1,0:T(8,128)} %concatenate.94), channel_id=1, source_target_pairs={{0,16},{1,17},{2,18},{3,19},{4,20},{5,21},{6,22},{7,23},{8,24},{9,... | collective-permute-start | bytes 1916936 | tf_op jit(solution)/shard_map/ppermute | solution.py:911
  55.8 36.1 %collective-permute-start.4 = (f32[192,768]{1,0:T(8,128)S(1)}, f32[192,768]{1,0:T(8,128)S(1)}, u32[]{:S(2)}, u32[]{:S(2)}) collective-permute-start(f32[192,768]{1,0:T(8,128)S(1)} %slice.207.refs_5_.refs_9_), channel_id=1, source_target_pairs={{0,2},{1,3},{2,0},{3,1},{4,6},{5,7},{6,4},{7,5},{8,10},{9,11},{10,... | collective-permute-start | bytes 1769480 | tf_op jit(solution)/shard_map/ppermute | solution.py:911
  58.3 33.7 %collective-permute-start.7 = (f32[192,768]{1,0:T(8,128)}, f32[192,768]{1,0:T(8,128)S(1)}, u32[]{:S(2)}, u32[]{:S(2)}) collective-permute-start(f32[192,768]{1,0:T(8,128)} %dynamic-slice_bitcast_fusion), channel_id=1, source_target_pairs={{0,16},{1,17},{2,18},{3,19},{4,20},{5,21},{6,22},{7,23},{8,24},{9,... | collective-permute-start | bytes 1769480 | tf_op jit(solution)/shard_map/ppermute | solution.py:911
  100.0 31.5 %collective-permute-start.10 = (f32[384,768]{1,0:T(8,128)}, f32[384,768]{1,0:T(8,128)}, u32[]{:S(2)}, u32[]{:S(2)}) collective-permute-start(f32[384,768]{1,0:T(8,128)} %pad_maximum_fusion.5), channel_id=1, source_target_pairs={{0,4},{1,5},{2,6},{3,7},{4,0},{5,1},{6,2},{7,3},{8,12},{9,13},{10,... | collective-permute-start | bytes 3538952 | tf_op jit(solution)/shard_map/ppermute | solution.py:911
  105.4 45.7 %collective-permute-start.9 = (f32[192,768]{1,0:T(8,128)S(1)}, f32[192,768]{1,0:T(8,128)S(1)}, u32[]{:S(2)}, u32[]{:S(2)}) collective-permute-start(f32[192,768]{1,0:T(8,128)S(1)} %collective-permute-done.7.refs_9_), channel_id=1, source_target_pairs={{0,2},{1,3},{2,0},{3,1},{4,6},{5,7},{6,4},{7,5},{8,10},{9,11},{10,... | collective-permute-start | bytes 1769480 | tf_op jit(solution)/shard_map/ppermute | solution.py:911
  106.2 45.0 %collective-permute-start.14 = (f32[192,768]{1,0:T(8,128)}, f32[192,768]{1,0:T(8,128)S(1)}, u32[]{:S(2)}, u32[]{:S(2)}) collective-permute-start(f32[192,768]{1,0:T(8,128)} %constant_dynamic-slice_fusion.8), channel_id=1, source_target_pairs={{0,16},{1,17},{2,18},{3,19},{4,20},{5,21},{6,22},{7,23},{8,24},{9,... | collective-permute-start | bytes 1769480 | tf_op jit(solution)/shard_map/ppermute | solution.py:911
  152.5 31.2 %collective-permute-start.18 = (f32[384,768]{1,0:T(8,128)}, f32[384,768]{1,0:T(8,128)}, u32[]{:S(2)}, u32[]{:S(2)}) collective-permute-start(f32[384,768]{1,0:T(8,128)} %pad_maximum_fusion.7), channel_id=1, source_target_pairs={{0,4},{1,5},{2,6},{3,7},{4,0},{5,1},{6,2},{7,3},{8,12},{9,13},{10,... | collective-permute-start | bytes 3538952 | tf_op jit(solution)/shard_map/ppermute | solution.py:911
  160.6 80.3 %collective-permute-start.25 = (f32[1024,768]{1,0:T(8,128)}, f32[1024,768]{1,0:T(8,128)}, u32[]{:S(2)}, u32[]{:S(2)}) collective-permute-start(f32[1024,768]{1,0:T(8,128)} %constant_dynamic-slice_fusion.5), channel_id=1, source_target_pairs={{0,1},{2,3},{4,5},{6,7},{8,9},{10,11},{12,13},{14,15},{17,16},{19,... | collective-permute-start | bytes 9437192 | tf_op jit(solution)/shard_map/ppermute | solution.py:911
  202.9 42.7 %collective-permute-start.26 = (f32[384,768]{1,0:T(8,128)}, f32[384,768]{1,0:T(8,128)S(1)}, u32[]{:S(2)}, u32[]{:S(2)}) collective-permute-start(f32[384,768]{1,0:T(8,128)} %pad_maximum_fusion.9), channel_id=1, source_target_pairs={{0,4},{1,5},{2,6},{3,7},{4,0},{5,1},{6,2},{7,3},{8,12},{9,13},{10,... | collective-permute-start | bytes 3538952 | tf_op jit(solution)/shard_map/ppermute | solution.py:911
  205.8 41.6 %collective-permute-start.27 = (f32[384,768]{1,0:T(8,128)}, f32[384,768]{1,0:T(8,128)}, u32[]{:S(2)}, u32[]{:S(2)}) collective-permute-start(f32[384,768]{1,0:T(8,128)} %pad_maximum_fusion.10), channel_id=1, source_target_pairs={{0,2},{1,3},{2,0},{3,1},{4,6},{5,7},{6,4},{7,5},{8,10},{9,11},{10,... | collective-permute-start | bytes 3538952 | tf_op jit(solution)/shard_map/ppermute | solution.py:911
  206.2 32.7 %collective-permute-start.16 = (f32[96,768]{1,0:T(8,128)S(1)}, f32[96,768]{1,0:T(8,128)S(1)}, u32[]{:S(2)}, u32[]{:S(2)}) collective-permute-start(f32[96,768]{1,0:T(8,128)S(1)} %get-tuple-element.572.refs_12_), channel_id=1, source_target_pairs={{0,2},{1,3},{2,0},{3,1},{4,6},{5,7},{6,4},{7,5},{8,10},{9,11},{10,... | collective-permute-start | bytes 884744 | tf_op jit(solution)/shard_map/ppermute | solution.py:911
  208.0 31.9 %collective-permute-start.17 = (f32[96,768]{1,0:T(8,128)S(1)}, f32[96,768]{1,0:T(8,128)}, u32[]{:S(2)}, u32[]{:S(2)}) collective-permute-start(f32[96,768]{1,0:T(8,128)S(1)} %get-tuple-element.571.refs_15_), channel_id=1, source_target_pairs={{0,4},{1,5},{2,6},{3,7},{4,0},{5,1},{6,2},{7,3},{8,12},{9,13},{10,... | collective-permute-start | bytes 884744 | tf_op jit(solution)/shard_map/ppermute | solution.py:911
  267.1 41.8 %collective-permute-start.34 = (f32[384,768]{1,0:T(8,128)}, f32[384,768]{1,0:T(8,128)S(1)}, u32[]{:S(2)}, u32[]{:S(2)}) collective-permute-start(f32[384,768]{1,0:T(8,128)} %pad_maximum_fusion.11), channel_id=1, source_target_pairs={{0,4},{1,5},{2,6},{3,7},{4,0},{5,1},{6,2},{7,3},{8,12},{9,13},{10,... | collective-permute-start | bytes 3538952 | tf_op jit(solution)/shard_map/ppermute | solution.py:911
  270.2 38.7 %collective-permute-start.35 = (f32[384,768]{1,0:T(8,128)}, f32[384,768]{1,0:T(8,128)S(1)}, u32[]{:S(2)}, u32[]{:S(2)}) collective-permute-start(f32[384,768]{1,0:T(8,128)} %pad_maximum_fusion.12), channel_id=1, source_target_pairs={{0,2},{1,3},{2,0},{3,1},{4,6},{5,7},{6,4},{7,5},{8,10},{9,11},{10,... | collective-permute-start | bytes 3538952 | tf_op jit(solution)/shard_map/ppermute | solution.py:911
  381.1 78.1 %collective-permute-start.43 = (f32[768,768]{1,0:T(8,128)}, f32[768,768]{1,0:T(8,128)S(1)}, u32[]{:S(2)}, u32[]{:S(2)}) collective-permute-start(f32[768,768]{1,0:T(8,128)} %bitcast.126), channel_id=1, source_target_pairs={{0,2},{1,3},{2,0},{3,1},{4,6},{5,7},{6,4},{7,5},{8,10},{9,11},{10,... | collective-permute-start | bytes 7077896 | tf_op jit(solution)/shard_map/ppermute | solution.py:911
  418.3 69.8 %collective-permute-start.46 = (f32[768,768]{1,0:T(8,128)}, f32[768,768]{1,0:T(8,128)}, u32[]{:S(2)}, u32[]{:S(2)}) collective-permute-start(f32[768,768]{1,0:T(8,128)} %bitcast.128), channel_id=1, source_target_pairs={{0,4},{1,5},{2,6},{3,7},{4,0},{5,1},{6,2},{7,3},{8,12},{9,13},{10,... | collective-permute-start | bytes 7077896 | tf_op jit(solution)/shard_map/ppermute | solution.py:911
  475.6 31.4 %collective-permute-start.45 = (f32[512,768]{1,0:T(8,128)}, f32[512,768]{1,0:T(8,128)}, u32[]{:S(2)}, u32[]{:S(2)}) collective-permute-start(f32[512,768]{1,0:T(8,128)} %get-tuple-element.366.refs_3_), channel_id=1, source_target_pairs={{0,1},{1,0},{2,3},{3,2},{4,5},{5,4},{6,7},{7,6},{8,9},{9,8},{10,11... | collective-permute-start | bytes 4718600 | tf_op jit(solution)/shard_map/ppermute | solution.py:911
  480.5 54.7 %collective-permute-start.47 = (f32[1024,384]{1,0:T(8,128)}, f32[1024,384]{1,0:T(8,128)}, u32[]{:S(2)}, u32[]{:S(2)}) collective-permute-start(f32[1024,384]{1,0:T(8,128)} %pad_maximum_fusion.3), channel_id=1, source_target_pairs={{0,16},{2,18},{4,20},{6,22},{8,24},{10,26},{12,28},{14,30},{17,1},... | collective-permute-start | bytes 4718600 | tf_op jit(solution)/shard_map/ppermute | solution.py:911
  487.5 47.8 %collective-permute-start.48 = (f32[384,768]{1,0:T(8,128)}, f32[384,768]{1,0:T(8,128)S(1)}, u32[]{:S(2)}, u32[]{:S(2)}) collective-permute-start(f32[384,768]{1,0:T(8,128)} %get-tuple-element.389), channel_id=1, source_target_pairs={{0,4},{1,5},{2,6},{3,7},{4,0},{5,1},{6,2},{7,3},{8,12},{9,13},{10,... | collective-permute-start | bytes 3538952 | tf_op jit(solution)/shard_map/ppermute | solution.py:911
  503.4 31.9 %collective-permute-start.49 = (f32[384,768]{1,0:T(8,128)}, f32[384,768]{1,0:T(8,128)}, u32[]{:S(2)}, u32[]{:S(2)}) collective-permute-start(f32[384,768]{1,0:T(8,128)} %get-tuple-element.391), channel_id=1, source_target_pairs={{0,2},{1,3},{2,0},{3,1},{4,6},{5,7},{6,4},{7,5},{8,10},{9,11},{10,... | collective-permute-start | bytes 3538952 | tf_op jit(solution)/shard_map/ppermute | solution.py:911
  505.8 63.3 %collective-permute-start.53 = (f32[768,768]{1,0:T(8,128)}, f32[768,768]{1,0:T(8,128)S(1)}, u32[]{:S(2)}, u32[]{:S(2)}) collective-permute-start(f32[768,768]{1,0:T(8,128)} %bitcast.125), channel_id=1, source_target_pairs={{0,4},{1,5},{2,6},{3,7},{4,0},{5,1},{6,2},{7,3},{8,12},{9,13},{10,... | collective-permute-start | bytes 7077896 | tf_op jit(solution)/shard_map/ppermute | solution.py:911
  534.1 54.6 %collective-permute-start.54 = (f32[768,768]{1,0:T(8,128)}, f32[768,768]{1,0:T(8,128)}, u32[]{:S(2)}, u32[]{:S(2)}) collective-permute-start(f32[768,768]{1,0:T(8,128)} %bitcast.127), channel_id=1, source_target_pairs={{0,2},{1,3},{2,0},{3,1},{4,6},{5,7},{6,4},{7,5},{8,10},{9,11},{10,... | collective-permute-start | bytes 7077896 | tf_op jit(solution)/shard_map/ppermute | solution.py:911
  567.2 66.9 %collective-permute-start.57 = (f32[384,768]{1,0:T(8,128)}, f32[384,768]{1,0:T(8,128)S(1)}, u32[]{:S(2)}, u32[]{:S(2)}) collective-permute-start(f32[384,768]{1,0:T(8,128)} %bitcast.130), channel_id=1, source_target_pairs={{0,2},{1,3},{2,0},{3,1},{4,6},{5,7},{6,4},{7,5},{8,10},{9,11},{10,... | collective-permute-start | bytes 3538952 | tf_op jit(solution)/shard_map/ppermute | solution.py:911
  568.3 65.8 %collective-permute-start.58 = (f32[384,768]{1,0:T(8,128)}, f32[384,768]{1,0:T(8,128)}, u32[]{:S(2)}, u32[]{:S(2)}) collective-permute-start(f32[384,768]{1,0:T(8,128)} %bitcast.129), channel_id=1, source_target_pairs={{0,4},{1,5},{2,6},{3,7},{4,0},{5,1},{6,2},{7,3},{8,12},{9,13},{10,... | collective-permute-start | bytes 3538952 | tf_op jit(solution)/shard_map/ppermute | solution.py:911
  672.9 36.1 %collective-permute-start.65 = (f32[384,768]{1,0:T(8,128)}, f32[384,768]{1,0:T(8,128)}, u32[]{:S(2)}, u32[]{:S(2)}) collective-permute-start(f32[384,768]{1,0:T(8,128)} %bitcast.38), channel_id=1, source_target_pairs={{0,2},{1,3},{2,0},{3,1},{4,6},{5,7},{6,4},{7,5},{8,10},{9,11},{10,... | collective-permute-start | bytes 3538952 | tf_op jit(solution)/shard_map/ppermute | solution.py:911
  672.9 36.1 %collective-permute-start.66 = (f32[384,768]{1,0:T(8,128)}, f32[384,768]{1,0:T(8,128)}, u32[]{:S(2)}, u32[]{:S(2)}) collective-permute-start(f32[384,768]{1,0:T(8,128)} %bitcast.39), channel_id=1, source_target_pairs={{0,4},{1,5},{2,6},{3,7},{4,0},{5,1},{6,2},{7,3},{8,12},{9,13},{10,... | collective-permute-start | bytes 3538952 | tf_op jit(solution)/shard_map/ppermute | solution.py:911
  691.0 37.4 %collective-permute-start.67 = (f32[192,768]{1,0:T(8,128)}, f32[192,768]{1,0:T(8,128)}, u32[]{:S(2)}, u32[]{:S(2)}) collective-permute-start(f32[192,768]{1,0:T(8,128)} %slice_select_fusion.8), channel_id=1, source_target_pairs={{0,16},{1,17},{2,18},{3,19},{4,20},{5,21},{6,22},{7,23},{8,24},{9,... | collective-permute-start | bytes 1769480 | tf_op jit(solution)/shard_map/ppermute | solution.py:911
  702.2 44.5 %collective-permute-start.71 = (f32[1024,384]{1,0:T(8,128)}, f32[1024,384]{1,0:T(8,128)S(1)}, u32[]{:S(2)}, u32[]{:S(2)}) collective-permute-start(f32[1024,384]{1,0:T(8,128)} %get-tuple-element.464), channel_id=1, source_target_pairs={{0,8},{2,10},{4,12},{6,14},{8,0},{10,2},{12,4},{14,6},{17,25},{19,... | collective-permute-start | bytes 4718600 | tf_op jit(solution)/shard_map/ppermute | solution.py:911
  780.6 51.3 %collective-permute-start.79 = (f32[192,768]{1,0:T(8,128)}, f32[192,768]{1,0:T(8,128)}, u32[]{:S(2)}, u32[]{:S(2)}) collective-permute-start(f32[192,768]{1,0:T(8,128)} %slice_select_fusion.6), channel_id=1, source_target_pairs={{0,16},{1,17},{2,18},{3,19},{4,20},{5,21},{6,22},{7,23},{8,24},{9,... | collective-permute-start | bytes 1769480 | tf_op jit(solution)/shard_map/ppermute | solution.py:911
  794.5 35.7 %collective-permute-start.78 = (f32[56,768]{1,0:T(8,128)}, f32[56,768]{1,0:T(8,128)}, u32[]{:S(2)}, u32[]{:S(2)}) collective-permute-start(f32[56,768]{1,0:T(8,128)} %add.152), channel_id=1, source_target_pairs={{0,16},{1,17},{2,18},{3,19},{4,20},{5,21},{6,22},{7,23},{8,24},{9,... | collective-permute-start | bytes 516104 | tf_op jit(solution)/shard_map/ppermute | solution.py:911
  804.3 44.8 %collective-permute-start.75 = (f32[1024,384]{1,0:T(8,128)}, f32[1024,384]{1,0:T(8,128)S(1)}, u32[]{:S(2)}, u32[]{:S(2)}) collective-permute-start(f32[1024,384]{1,0:T(8,128)} %pad_maximum_fusion.4), channel_id=1, source_target_pairs={{0,16},{2,18},{4,20},{6,22},{8,24},{10,26},{12,28},{14,30},{17,1},... | collective-permute-start | bytes 4718600 | tf_op jit(solution)/shard_map/ppermute | solution.py:911
  (132 other events, 2064.9 us)

commit v3 on v2

--- a/solution.py
+++ b/solution.py
@@ -1111,13 +1111,12 @@
     tail = jnp.zeros((-vec_count % 8, width), f32)
     shard = jnp.concatenate([shard_of(own[0]), own_vec, tail])
     far_attn, near_attn = plan.along_z(shard, 2), plan.along_z(shard, 1)
-    mask_parts, token_parts = fetch(after(absorbed, shard)), fetch(after(tokens, shard))
-    far_attn, near_attn, mask_other, token_other, up_shard, down_shard = lax.optimization_barrier(
-        (far_attn, near_attn, mask_parts[1], token_parts[1], shard_of(own[1]), shard_of(own[2]))
+    far_attn, near_attn, up_shard, down_shard = lax.optimization_barrier(
+        (far_attn, near_attn, shard_of(own[1]), shard_of(own[2]))
     )
     opp_attn = plan.along_z(far_attn, 1)
     far_up = plan.along_z(up_shard, 2)
-    token_parts = (*token_parts, token_other)
+    mask_parts, token_parts = fetch(after(absorbed, far_attn)), fetch(after(tokens, far_attn))
 
     near_vec = jnp.stack([own_vec, near_attn[count : count + vec_count]])
     far_vec = jnp.stack([far_attn[count : count + vec_count], opp_attn[count : count + vec_count]])
@@ -1129,14 +1128,14 @@
     attn_opp = opposite(near_attn[:count], opp_attn[:count])
     attn_groups = [Group(plan, far_attn[:count], 1), Group(plan, attn_opp[0], 2)]
     near_up = plan.along_z(after(up_shard, attn_opp[0]), 1)
-    far_up, near_up = arrive(attn_groups, far_up, near_up)
+    far_up, near_up, mask_parts, token_parts = arrive(attn_groups, far_up, near_up, mask_parts, token_parts)
     sent = [group.step() for group in attn_groups]
-    mask_other, token_parts = lax.optimization_barrier((mask_other, token_parts, *sent))[:2]
-    mask_row = jnp.where(local, mask_parts[0], mask_other).astype(f32)
+    mask_parts, token_parts = lax.optimization_barrier((mask_parts, token_parts, *sent))[:2]
+    mask_row = jnp.where(local, *mask_parts).astype(f32)
     step = lax.dynamic_index_in_dim(timesteps, sequence, 0, keepdims=False)
     step_row = lax.dynamic_slice_in_dim(time_table, step, 1, 0)
     mask = mask_row[:, None]
-    x = jnp.where(mask > 0.5, mask_embedding[None, :] + step_row, jnp.where(local, token_parts[0], token_parts[2]))
+    x = jnp.where(mask > 0.5, mask_embedding[None, :] + step_row, jnp.where(local, *token_parts))
     weight = LEN / jnp.maximum(jnp.sum(mask_row), 1.0)
     far_down = plan.along_z(after(down_shard, far_up), 2)
     opp_up = plan.along_z(far_up, 1)
@@ -1285,21 +1284,17 @@
     up_0 = Sum(plan, 3, pieces)
     g, *others = lax.optimization_barrier((g, *e[2:], pieces[0]))[:3]
     g, doh, dol, do, out_bias_sum = ride(
-        attn_back_one, [feed_1, attn_1, down_0], g, (*e[:2], *others), yh, yl, y_scale, wh, wl, oh, ol
-    )
-    grads = attn_heads_back(ph, pl_, doh, dol, oh, ol, lse)
+        attn_back_one, [attn_1], g, (*e[:2], *others), yh, yl, y_scale, wh, wl, oh, ol
+    )
+    doh = after(doh, *down_0.after(out_bias_sum).advance())
+    grads = ride(attn_heads_back, [feed_1], ph, pl_, doh, dol, oh, ol, lse)
     mixed = attn_1.merge(down_0)
-    *pieces, pair_sum = ride(attn_back_two, [mixed, up_0], "w", 3, flags[0], grads, xh, xl, vec, wh, wl, do)
+    grads[0] = after(grads[0], *mixed.after(grads[0]).advance())
+    *pieces, pair_sum = ride(attn_back_two, [up_0], "w", 3, flags[0], grads, xh, xl, vec, wh, wl, do)
     attn_0 = Sum(plan, 3, pieces)
     *e, attn_vec = attn_back_two("e", 0, flags[0], [after(grads[0], pair_sum), *grads[1:]], xh, xl, vec, wh, wl, do)
     e = plan.added(*mixed.wait(*up_0.wait(*e)))
     small[0] = (attn_vec, pair_sum, out_bias_sum, ffn_vec, up_bias_sum, down_bias_sum)
-    grad_near, grad_far, row_sum = ride(finish, [up_0, mixed], plane_flags, g, e, xh, xl, x_scale, mask)
-    out_rows = settle_rows(out_near, out_beside, out_beyond)
-
-    pack_flags = jnp.stack([z % 2, core, sequence]).astype(jnp.int32)
-    grad_beside = beside(grad_far)
-    table = pack(pack_flags, small, row_sum, columns, timesteps.shape[0])
 
     def cross(low, high):
         on = jnp.where(low_planes, high, low)
@@ -1307,21 +1302,28 @@
 
     feed_1, mixed = feed_1.finish(), mixed.finish()
     down_mine, down_on, down_got = cross(mixed[count:], feed_1[:count])
+    g = after(g, down_on, *up_0.advance())
+    grad_near, grad_far, row_sum = finish(plane_flags, g, e, xh, xl, x_scale, mask)
+    out_rows = settle_rows(out_near, out_beside, out_beyond)
+    grad_beside = beside(after(grad_far, down_got))
+
+    up_mine, up_on, up_got = cross(up_0.after(grad_far).finish(), feed_1[count:])
+    pack_flags = jnp.stack([z % 2, core, sequence]).astype(jnp.int32)
+    table = pack(pack_flags, small, row_sum, columns, timesteps.shape[0])
     table = plan.sum_step(table, 0)
-    down_got, table = attn_0.wait(down_got, table)
+    (table,) = attn_0.after(up_on).wait(table)
     attn_0.advance()
-    table, grad_beside = up_0.wait(*attn_0.wait(table, grad_beside))
-    attn_0.advance()
-    up_mine, up_on, up_got = cross(up_0.finish(), feed_1[count:])
-    table = plan.sum_step(table, 1)
+    table = plan.sum_step(table, 3)
+    grad_beside, table = attn_0.wait(grad_beside, table)
+    on = attn_0.advance()
+    (grad_beside,) = arrive([], grad_beside, *on)[:1]
+    grad_beyond = beyond(grad_near, grad_beside)
+    table = plan.sum_step(table, 4)
     up_got, table = attn_0.wait(up_got, table)
     attn_mine, attn_on, attn_got = cross(attn_0.finish(), mixed[:count])
-    grad_beside, table = lax.optimization_barrier((grad_beside, table, attn_on))[:2]
-    grad_beyond = beyond(grad_near, grad_beside)
-    for step in (2, 3, 4):
+    for step in (1, 2):
         table = plan.sum_step(table, step)
-    grad_rows = settle_rows(grad_near, grad_beside, grad_beyond)
-    down_mine, up_mine, attn_mine = down_mine + down_got, up_mine + up_got, attn_mine + attn_got
+    down_mine, up_mine = down_mine + down_got, up_mine + up_got
 
     def exchange(rows_all):
         halves = rows_all.reshape(2, -1, width)
@@ -1330,14 +1332,15 @@
         first = core == 0
         return jnp.where(first, mine, theirs), jnp.where(first, theirs, mine)
 
-    zero, one = exchange(attn_mine)
-    count = zero.shape[0]
-    joint = jnp.stack([v[:, : 3 * inner_half].reshape(count, 3, inner_half) for v in (zero, one)], axis=2)
-    joint_grad = joint.reshape(count, 3 * inner)
+    zero, one = exchange(down_mine)
+    down_grad = jnp.stack([v.reshape(-1, columns, block) for v in (zero, one)], axis=2).reshape(-1, hidden).T
+    up_grad = up_mine.reshape(-1, width).T
+    attn_got, table = lax.optimization_barrier((attn_got, table, down_grad, up_grad))[:2]
+    zero, one = exchange(attn_mine + attn_got)
+    grad_rows = settle_rows(grad_near, grad_beside, grad_beyond)
+    joint = jnp.stack([v[:, : 3 * inner_half].reshape(-1, 3, inner_half) for v in (zero, one)], axis=2)
+    joint_grad = joint.reshape(-1, 3 * inner)
     out_grad = jnp.concatenate([zero[:, 3 * inner_half :], one[:, 3 * inner_half :]], axis=1).T
-    zero, one = exchange(down_mine)
-    down_grad = jnp.stack([v.reshape(count, columns, block) for v in (zero, one)], axis=2).reshape(count, hidden).T
-    up_grad = up_mine.reshape(-1, width).T
 
     mine = lax.dynamic_slice_in_dim(table, VEC_ROWS * z, VEC_ROWS, 0)
     device = 2 * column + core

time: 862 us -> 840 us (0.974)
  waiting for transfers between devices: 201 us -> 167 us
  other arithmetic: 56.3 us -> 70.4 us
    ppermute x82, waiting for transfers between devices: 201 us -> 167 us  [permute(): return lax.ppermute(value, AXES, pairs)]
    add x4 -> x10, other arithmetic: 2.96 us -> 13.3 us  [advance(): a[i:i + rider.count] + b[j:j + rider.count]]
    unnamed x170 -> x164, local copies, waits for them, and re-layouts: 27.3 us -> 26.2 us
  transfers between devices with their start and end apart: 82 -> 82, of which waited for: 27 -> 23; matrix products, arithmetic and copies ran while one was open for 12% -> 15% of each run, Pallas kernels for 42% -> 44%
where the time goes in v3:
time: 840 us; the launch traced here: 831 us
  Pallas kernels  402 us (48%)
  waiting for transfers between devices  167 us (20%)
  starting transfers between devices  102 us (12%)
  local copies, waits for them, and re-layouts  83.8 us (10%)
  other arithmetic  70.4 us (8%)
    pallas_call x25, Pallas kernels, call(): pl.pallas_call(whole, grid=(grid,), in_specs=in_specs, out_specs=list(out...  402 us
    ppermute x82, waiting for transfers between devices, permute(): return lax.ppermute(value, AXES, pairs)  167 us
    ppermute x82, starting transfers between devices, permute(): return lax.ppermute(value, AXES, pairs)  102 us
    unnamed x164, local copies, waits for them, and re-layouts  26.2 us
  transfers between devices with their start and end apart: 82, of which 23 were waited for; matrix products, arithmetic and copies ran while one was open for 15% of the time, Pallas kernels for 44%

profile of v3, /device:TPU:0, one launch (start us, length us, event | category | flops | bytes accessed | tf_op | source)
XLA Modules:
  0.0 830.9 jit_solution(7854918810766174313)
XLA Ops:
  28.4 15.2 %collective-permute-done = f32[208,768]{1,0:T(8,128)} collective-permute-done((f32[208,768]{1,0:T(8,128)}, f32[208,768]{1,0:T(8,128)}, u32[]{:S(2)}, u32[]{:S(2)}) %collective-permute-start) | collective-permute-done | bytes 639008 | tf_op jit(solution)/shard_map/ppermute | solution.py:911
  61.9 10.4 %collective-permute-done.3 = f32[208,768]{1,0:T(8,128)} collective-permute-done((f32[208,768]{1,0:T(8,128)}, f32[208,768]{1,0:T(8,128)}, u32[]{:S(2)}, u32[]{:S(2)}) %collective-permute-start.3) | collective-permute-done | bytes 639008 | tf_op jit(solution)/shard_map/ppermute | solution.py:911
  110.8 11.1 %collective-permute-done.12 = f32[192,768]{1,0:T(8,128)S(1)} collective-permute-done((f32[192,768]{1,0:T(8,128)S(1)}, f32[192,768]{1,0:T(8,128)S(1)}, u32[]{:S(2)}, u32[]{:S(2)}) %collective-permute-start.12) | collective-permute-done | bytes 589856 | tf_op jit(solution)/shard_map/ppermute | solution.py:911
  129.5 13.5 %attn_in.2 = (bf16[1024,768]{1,0:T(8,128)(2,1)}, bf16[1024,768]{1,0:T(8,128)(2,1)}, f32[1024,1]{1,0:T(8,128)}, bf16[1152,1024]{1,0:T(8,128)(2,1)}, bf16[1152,102...) custom-call(s32[5]{0:T(128)} %get-tuple-element.609.refs_0_, ...), custom_call_target="tpu_custom_call" | custom-call | flops 1 | bytes 1 | tf_op jit(solution)/shard_map/attn_in/pallas_call | solution.py:194
  155.6 20.0 %attn_heads.2 = (bf16[384,1024]{1,0:T(8,128)(2,1)}, bf16[384,1024]{1,0:T(8,128)(2,1)}, f32[6,1,1024]{2,1,0:T(1,128)}, f32[512,768]{1,0:T(8,128)}, f32[512,768]{1,0:T(8,128)}) custom-call(bf16[1152,1024]{1,0:T(8,128)(2,1)} %get-tuple-element.281.refs_0_.refs_2_.refs_4_, bf16[1152,1024]{1,0:T(8,128)(2,1)} %get-tuple-element.282.refs_1_.refs_3_.refs_5_, ...), custom_call_target="tpu_custom_call" | custom-call | flops 1 | bytes 1 | tf_op jit(solution)/shard_map/attn_heads/pallas_call | solution.py:194
  179.4 12.2 %collective-permute-done.21.refs_6_ = f32[192,768]{1,0:T(8,128)S(1)} collective-permute-done((f32[192,768]{1,0:T(8,128)S(1)}, f32[192,768]{1,0:T(8,128)S(1)}, u32[]{:S(2)}, u32[]{:S(2)}) %collective-permute-start.21) | collective-permute-done | bytes 589856 | tf_op jit(solution)/shard_map/ppermute | solution.py:911
  202.4 19.3 %feed_up.2 = (f32[1024,768]{1,0:T(8,128)}, bf16[1024,768]{1,0:T(8,128)(2,1)}, bf16[1024,768]{1,0:T(8,128)(2,1)}, f32[1024,1]{1,0:T(8,128)}, bf16[1024,1536]{1,0:...) custom-call(s32[5]{0:T(128)} %get-tuple-element.609.refs_0_, ...), custom_call_target="tpu_custom_call" | custom-call | flops 1 | bytes 1 | tf_op jit(solution)/shard_map/feed_up/pallas_call | solution.py:194
  238.8 15.7 %feed_down.2 = (f32[512,768]{1,0:T(8,128)}, f32[512,768]{1,0:T(8,128)}, bf16[2,768,768]{2,1,0:T(8,128)(2,1)}, bf16[2,768,768]{2,1,0:T(8,128)(2,1)}) custom-call(s32[5]{0:T(128)} %get-tuple-element.609.refs_0_, bf16[1024,1536]{1,0:T(8,128)(2,1)} %get-tuple-element.297.refs_1_.refs_11_, bf16[1024,1536]{1,0:T(8,128)(2,1)} %get-tuple-element.298.refs_2_.refs_12_, ...), custom_call_target="tpu_custom_call" | custom-call | flops 1 | bytes 1 | tf_op jit(solution)/shard_map/feed_down/pallas_call | solution.py:194
  264.3 16.2 %attn_in.3 = (f32[1024,768]{1,0:T(8,128)}, bf16[1024,768]{1,0:T(8,128)(2,1)}, bf16[1024,768]{1,0:T(8,128)(2,1)}, f32[1024,1]{1,0:T(8,128)}, bf16[1152,1024]{1,0:...) custom-call(s32[5]{0:T(128)} %get-tuple-element.608.refs_0_, ...), custom_call_target="tpu_custom_call" | custom-call | flops 1 | bytes 1 | tf_op jit(solution)/shard_map/attn_in/pallas_call | solution.py:194
  280.6 20.0 %attn_heads.3 = (bf16[384,1024]{1,0:T(8,128)(2,1)}, bf16[384,1024]{1,0:T(8,128)(2,1)}, f32[6,1,1024]{2,1,0:T(1,128)}, f32[512,768]{1,0:T(8,128)}, f32[512,768]{1,0:T(8,128)}) custom-call(bf16[1152,1024]{1,0:T(8,128)(2,1)} %get-tuple-element.315.refs_0_.refs_2_.refs_4_, bf16[1152,1024]{1,0:T(8,128)(2,1)} %get-tuple-element.316.refs_1_.refs_3_.refs_5_, ...), custom_call_target="tpu_custom_call" | custom-call | flops 1 | bytes 1 | tf_op jit(solution)/shard_map/attn_heads/pallas_call | solution.py:194
  308.6 19.2 %feed_up.3 = (f32[1024,768]{1,0:T(8,128)}, bf16[1024,768]{1,0:T(8,128)(2,1)}, bf16[1024,768]{1,0:T(8,128)(2,1)}, f32[1024,1]{1,0:T(8,128)}, bf16[1024,1536]{1,0:...) custom-call(s32[5]{0:T(128)} %get-tuple-element.608.refs_0_, ...), custom_call_target="tpu_custom_call" | custom-call | flops 1 | bytes 1 | tf_op jit(solution)/shard_map/feed_up/pallas_call | solution.py:194
  327.8 16.1 %feed_down.3 = (f32[512,768]{1,0:T(8,128)}, f32[512,768]{1,0:T(8,128)}, bf16[2,768,768]{2,1,0:T(8,128)(2,1)}, bf16[2,768,768]{2,1,0:T(8,128)(2,1)}) custom-call(s32[5]{0:T(128)} %get-tuple-element.608.refs_0_, bf16[1024,1536]{1,0:T(8,128)(2,1)} %get-tuple-element.324.refs_1_.refs_4_, bf16[1024,1536]{1,0:T(8,128)(2,1)} %get-tuple-element.325.refs_2_.refs_5_, ...), custom_call_target="tpu_custom_call" | custom-call | flops 1 | bytes 1 | tf_op jit(solution)/shard_map/feed_down/pallas_call | solution.py:194
  349.2 23.6 %feed_back_one.2 = (f32[1024,768]{1,0:T(8,128)}, bf16[1024,1536]{1,0:T(8,128)(2,1)}, bf16[1024,1536]{1,0:T(8,128)(2,1)}, f32[2,2,192,768]{3,2,1,0:T(8,128)}, f32...) custom-call(s32[5]{0:T(128)} %get-tuple-element.608.refs_0_, ...), custom_call_target="tpu_custom_call" | custom-call | flops 1 | bytes 1 | tf_op jit(solution)/shard_map/feed_back_one/pallas_call | solution.py:194
  384.5 13.3 %feed_back_two_e.2 = (f32[512,768]{1,0:T(8,128)}, f32[512,768]{1,0:T(8,128)}, f32[4,768]{1,0:T(4,128)}) custom-call(s32[5]{0:T(128)} %get-tuple-element.608.refs_0_, bf16[1024,1536]{1,0:T(8,128)(2,1)} %get-tuple-element.348.refs_1_, bf16[1024,1536]{1,0:T(8,128)(2,1)} %get-tuple-element.340.refs_2_, bf16[1024,768]{1,0:T(8,128)(2,1)} %get-tuple-element.341.refs_3_.refs_5_, ...), custom_call_target="tpu_custom_call" | custom-call | flops 1 | bytes 1 | tf_op jit(solution)/shard_map/feed_back_two_e/pallas_call | solution.py:194
  398.4 13.1 %feed_back_two_w.2 = (f32[2,2,192,768]{3,2,1,0:T(8,128)}, f32[2,2,192,768]{3,2,1,0:T(8,128)}) custom-call(s32[5]{0:T(128)} %get-tuple-element.608.refs_0_, bf16[1024,1536]{1,0:T(8,128)(2,1)} %get-tuple-element.348.refs_1_, bf16[1024,1536]{1,0:T(8,128)(2,1)} %get-tuple-element.340.refs_2_, bf16[1024,768]{1,0:T(8,128)(2,1)} %get-tuple-element.341.refs_3_.refs_5_, ...), custom_call_target="tpu_custom_call" | custom-call | flops 1 | bytes 1 | tf_op jit(solution)/shard_map/feed_back_two_w/pallas_call | solution.py:194
  412.0 11.3 %attn_back_one.2 = (f32[1024,768]{1,0:T(8,128)}, bf16[384,1024]{1,0:T(8,128)(2,1)}, bf16[384,1024]{1,0:T(8,128)(2,1)}, f32[384,768]{1,0:T(8,128)}, f32[1,768]{1,0:T(1,128)}) custom-call(f32[1024,768]{1,0:T(8,128)} %get-tuple-element.351.refs_0_, f32[512,768]{1,0:T(8,128)} %get-tuple-element.345.refs_1_, f32[512,768]{1,0:T(8,128)} %get-tuple-element.346.refs_2_, ...), custom_call_target="tpu_custom_call" | custom-call | flops 1 | bytes 1 | tf_op jit(solution)/shard_map/attn_back_one/pallas_call | solution.py:194
  423.3 28.3 %attn_heads_back.2 = (bf16[384,1024]{1,0:T(8,128)(2,1)}, bf16[384,1024]{1,0:T(8,128)(2,1)}, bf16[384,1024]{1,0:T(8,128)(2,1)}, bf16[384,1024]{1,0:T(8,128)(2,1)}...) custom-call(bf16[1152,1024]{1,0:T(8,128)(2,1)} %get-tuple-element.315.refs_0_.refs_2_.refs_4_, ...), custom_call_target="tpu_custom_call" | custom-call | flops 1 | bytes 1 | tf_op jit(solution)/shard_map/attn_heads_back/pallas_call | solution.py:194
  453.1 14.7 %attn_back_two_e.2 = (f32[512,768]{1,0:T(8,128)}, f32[512,768]{1,0:T(8,128)}, f32[4,768]{1,0:T(4,128)}, f32[384,768]{1,0:T(8,128)}, f32[384,768]{1,0:T(8,128)}) custom-call(s32[5]{0:T(128)} %get-tuple-element.608.refs_0_, bf16[384,1024]{1,0:T(8,128)(2,1)} %get-tuple-element.361.refs_1_, bf16[384,1024]{1,0:T(8,128)(2,1)} %get-tuple-element.362.refs_2_, ...), custom_call_target="tpu_custom_call" | custom-call | flops 1 | bytes 1 | tf_op jit(solution)/shard_map/attn_back_two_e/pallas_call | solution.py:194
  473.1 10.7 %collective-permute-start.47 = (f32[1024,384]{1,0:T(8,128)}, f32[1024,384]{1,0:T(8,128)}, u32[]{:S(2)}, u32[]{:S(2)}) collective-permute-start(f32[1024,384]{1,0:T(8,128)} %pad_maximum_fusion.3), channel_id=1, source_target_pairs={{0,16},{2,18},{4,20},{6,22},{8,24},{10,26},{12,28},{14,30},{17,1},... | collective-permute-start | bytes 4718600 | tf_op jit(solution)/shard_map/ppermute | solution.py:911
  484.8 15.2 %attn_back_two_w.2 = (f32[2,2,192,768]{3,2,1,0:T(8,128)}, f32[2,2,192,768]{3,2,1,0:T(8,128)}, f32[2,8,576]{2,1,0:T(8,128)}, f32[384,768]{1,0:T(8,128)}, f32[384,768]{1,0:T(8,128)}) custom-call(s32[5]{0:T(128)} %get-tuple-element.608.refs_0_, bf16[384,1024]{1,0:T(8,128)(2,1)} %get-tuple-element.361.refs_1_, bf16[384,1024]{1,0:T(8,128)(2,1)} %get-tuple-element.362.refs_2_, ...), custom_call_target="tpu_custom_call" | custom-call | flops 1 | bytes 1 | tf_op jit(solution)/shard_map/attn_back_two_w/pallas_call | solution.py:194
  503.3 27.2 %feed_back_one.3 = (f32[1024,768]{1,0:T(8,128)}, bf16[1024,1536]{1,0:T(8,128)(2,1)}, bf16[1024,1536]{1,0:T(8,128)(2,1)}, f32[2,2,192,768]{3,2,1,0:T(8,128)}, f32...) custom-call(s32[5]{0:T(128)} %get-tuple-element.609.refs_0_, f32[1024,768]{1,0:T(8,128)} %get-tuple-element.378.refs_1_, ...), custom_call_target="tpu_custom_call" | custom-call | flops 1 | bytes 1 | tf_op jit(solution)/shard_map/feed_back_one/pallas_call | solution.py:194
  532.7 15.0 %feed_back_two_e.3 = (f32[512,768]{1,0:T(8,128)}, f32[512,768]{1,0:T(8,128)}, f32[4,768]{1,0:T(4,128)}, f32[384,768]{1,0:T(8,128)}, f32[384,768]{1,0:T(8,128)}) custom-call(s32[5]{0:T(128)} %get-tuple-element.609.refs_0_, bf16[1024,1536]{1,0:T(8,128)(2,1)} %get-tuple-element.401.refs_1_, bf16[1024,1536]{1,0:T(8,128)(2,1)} %get-tuple-element.389.refs_2_, ...), custom_call_target="tpu_custom_call" | custom-call | flops 1 | bytes 1 | tf_op jit(solution)/shard_map/feed_back_two_e/pallas_call | solution.py:194
  551.4 13.8 %feed_back_two_w.3 = (f32[2,2,96,768]{3,2,1,0:T(8,128)}, f32[2,2,96,768]{3,2,1,0:T(8,128)}, f32[2,2,96,768]{3,2,1,0:T(8,128)}, f32[2,2,96,768]{3,2,1,0:T(8,128)}) custom-call(s32[5]{0:T(128)} %get-tuple-element.609.refs_0_, bf16[1024,1536]{1,0:T(8,128)(2,1)} %get-tuple-element.401.refs_1_, bf16[1024,1536]{1,0:T(8,128)(2,1)} %get-tuple-element.389.refs_2_, ...), custom_call_target="tpu_custom_call" | custom-call | flops 1 | bytes 1 | tf_op jit(solution)/shard_map/feed_back_two_w/pallas_call | solution.py:194
  568.4 12.5 %attn_back_one.3 = (f32[1024,768]{1,0:T(8,128)}, bf16[384,1024]{1,0:T(8,128)(2,1)}, bf16[384,1024]{1,0:T(8,128)(2,1)}, f32[384,768]{1,0:T(8,128)}, f32[1,768]{1,...) custom-call(f32[1024,768]{1,0:T(8,128)} %get-tuple-element.403.refs_0_, f32[512,768]{1,0:T(8,128)} %get-tuple-element.398.refs_1_, ...), custom_call_target="tpu_custom_call" | custom-call | flops 1 | bytes 1 | tf_op jit(solution)/shard_map/attn_back_one/pallas_call | solution.py:194
  593.4 28.5 %attn_heads_back.3 = (bf16[384,1024]{1,0:T(8,128)(2,1)}, bf16[384,1024]{1,0:T(8,128)(2,1)}, bf16[384,1024]{1,0:T(8,128)(2,1)}, bf16[384,1024]{1,0:T(8,128)(2,1)}...) custom-call(bf16[1152,1024]{1,0:T(8,128)(2,1)} %get-tuple-element.281.refs_0_.refs_2_.refs_4_, ...), custom_call_target="tpu_custom_call" | custom-call | flops 1 | bytes 1 | tf_op jit(solution)/shard_map/attn_heads_back/pallas_call | solution.py:194
  639.6 15.0 %attn_back_two_w.3 = (f32[2,2,96,768]{3,2,1,0:T(8,128)}, f32[2,2,96,768]{3,2,1,0:T(8,128)}, f32[2,2,96,768]{3,2,1,0:T(8,128)}, f32[2,2,96,768]{3,2,1,0:T(8,128)}...) custom-call(s32[5]{0:T(128)} %get-tuple-element.609.refs_0_, ...), custom_call_target="tpu_custom_call" | custom-call | flops 1 | bytes 1 | tf_op jit(solution)/shard_map/attn_back_two_w/pallas_call | solution.py:194
  656.7 13.6 %attn_back_two_e.3 = (f32[512,768]{1,0:T(8,128)}, f32[512,768]{1,0:T(8,128)}, f32[4,768]{1,0:T(4,128)}) custom-call(s32[5]{0:T(128)} %get-tuple-element.609.refs_0_, bf16[384,1024]{1,0:T(8,128)(2,1)} %get-tuple-element.445.refs_1_, bf16[384,1024]{1,0:T(8,128)(2,1)} %get-tuple-element.427.refs_2_, bf16[384,1024]{1,0:T(8,128)(2,1)} %get-tuple-element.428.refs_3_, ...), custom_call_target="tpu_custom_call" | custom-call | flops 1 | bytes 1 | tf_op jit(solution)/shard_map/attn_back_two_e/pallas_call | solution.py:194
  684.1 8.3 finish.1
  692.4 12.7 %collective-permute-done.70 = f32[192,768]{1,0:T(8,128)} collective-permute-done((f32[192,768]{1,0:T(8,128)}, f32[192,768]{1,0:T(8,128)}, u32[]{:S(2)}, u32[]{:S(2)}) %collective-permute-start.70) | collective-permute-done | bytes 589856 | tf_op jit(solution)/shard_map/ppermute | solution.py:911
  720.3 26.9 %collective-permute-done.72 = f32[56,768]{1,0:T(8,128)S(1)} collective-permute-done((f32[56,768]{1,0:T(8,128)S(1)}, f32[56,768]{1,0:T(8,128)S(1)}, u32[]{:S(2)}, u32[]{:S(2)}) %collective-permute-start.72) | collective-permute-done | bytes 172064 | tf_op jit(solution)/shard_map/ppermute | solution.py:911
  748.4 10.3 %collective-permute-done.76 = f32[56,768]{1,0:T(8,128)} collective-permute-done((f32[56,768]{1,0:T(8,128)S(1)}, f32[56,768]{1,0:T(8,128)}, u32[]{:S(2)}, u32[]{:S(2)}) %collective-permute-start.76) | collective-permute-done | bytes 172064 | tf_op jit(solution)/shard_map/ppermute | solution.py:911
  782.9 25.6 %collective-permute-done.77 = f32[192,768]{1,0:T(8,128)} collective-permute-done((f32[192,768]{1,0:T(8,128)}, f32[192,768]{1,0:T(8,128)}, u32[]{:S(2)}, u32[]{:S(2)}) %collective-permute-start.77) | collective-permute-done | bytes 589856 | tf_op jit(solution)/shard_map/ppermute | solution.py:911
  (442 shorter events, 297.3 us)
Async XLA Ops:
  11.1 32.5 %collective-permute-start = (f32[208,768]{1,0:T(8,128)}, f32[208,768]{1,0:T(8,128)}, u32[]{:S(2)}, u32[]{:S(2)}) collective-permute-start(f32[208,768]{1,0:T(8,128)} %concatenate.106), channel_id=1, source_target_pairs={{0,16},{1,17},{2,18},{3,19},{4,20},{5,21},{6,22},{7,23},{8,24},{9,... | collective-permute-start | bytes 1916936 | tf_op jit(solution)/shard_map/ppermute | solution.py:911
  47.8 43.1 %collective-permute-start.8 = (f32[1024,768]{1,0:T(8,128)}, f32[1024,768]{1,0:T(8,128)}, u32[]{:S(2)}, u32[]{:S(2)}) collective-permute-start(f32[1024,768]{1,0:T(8,128)} %constant_dynamic-slice_fusion.8), channel_id=1, source_target_pairs={{0,1},{2,3},{4,5},{6,7},{8,9},{10,11},{12,13},{14,15},{17,16},{19,... | collective-permute-start | bytes 9437192 | tf_op jit(solution)/shard_map/ppermute | solution.py:911
  99.0 44.0 %collective-permute-start.9 = (f32[192,768]{1,0:T(8,128)S(1)}, f32[192,768]{1,0:T(8,128)S(1)}, u32[]{:S(2)}, u32[]{:S(2)}) collective-permute-start(f32[192,768]{1,0:T(8,128)S(1)} %collective-permute-done.5.refs_9_), channel_id=1, source_target_pairs={{0,2},{1,3},{2,0},{3,1},{4,6},{5,7},{6,4},{7,5},{8,10},{9,11},{10,... | collective-permute-start | bytes 1769480 | tf_op jit(solution)/shard_map/ppermute | solution.py:911
  99.5 43.5 %collective-permute-start.14 = (f32[192,768]{1,0:T(8,128)}, f32[192,768]{1,0:T(8,128)S(1)}, u32[]{:S(2)}, u32[]{:S(2)}) collective-permute-start(f32[192,768]{1,0:T(8,128)} %constant_dynamic-slice_fusion.9), channel_id=1, source_target_pairs={{0,16},{1,17},{2,18},{3,19},{4,20},{5,21},{6,22},{7,23},{8,24},{9,... | collective-permute-start | bytes 1769480 | tf_op jit(solution)/shard_map/ppermute | solution.py:911
  152.5 80.3 %collective-permute-start.25 = (f32[1024,768]{1,0:T(8,128)}, f32[1024,768]{1,0:T(8,128)}, u32[]{:S(2)}, u32[]{:S(2)}) collective-permute-start(f32[1024,768]{1,0:T(8,128)} %constant_dynamic-slice_fusion.5), channel_id=1, source_target_pairs={{0,1},{2,3},{4,5},{6,7},{8,9},{10,11},{12,13},{14,15},{17,16},{19,... | collective-permute-start | bytes 9437192 | tf_op jit(solution)/shard_map/ppermute | solution.py:911
  194.7 43.1 %collective-permute-start.26 = (f32[384,768]{1,0:T(8,128)}, f32[384,768]{1,0:T(8,128)S(1)}, u32[]{:S(2)}, u32[]{:S(2)}) collective-permute-start(f32[384,768]{1,0:T(8,128)} %pad_maximum_fusion.9), channel_id=1, source_target_pairs={{0,4},{1,5},{2,6},{3,7},{4,0},{5,1},{6,2},{7,3},{8,12},{9,13},{10,... | collective-permute-start | bytes 3538952 | tf_op jit(solution)/shard_map/ppermute | solution.py:911
  196.8 41.6 %collective-permute-start.27 = (f32[384,768]{1,0:T(8,128)}, f32[384,768]{1,0:T(8,128)}, u32[]{:S(2)}, u32[]{:S(2)}) collective-permute-start(f32[384,768]{1,0:T(8,128)} %pad_maximum_fusion.10), channel_id=1, source_target_pairs={{0,2},{1,3},{2,0},{3,1},{4,6},{5,7},{6,4},{7,5},{8,10},{9,11},{10,... | collective-permute-start | bytes 3538952 | tf_op jit(solution)/shard_map/ppermute | solution.py:911
  199.0 33.1 %collective-permute-start.17 = (f32[96,768]{1,0:T(8,128)S(1)}, f32[96,768]{1,0:T(8,128)}, u32[]{:S(2)}, u32[]{:S(2)}) collective-permute-start(f32[96,768]{1,0:T(8,128)S(1)} %get-tuple-element.589.refs_15_), channel_id=1, source_target_pairs={{0,4},{1,5},{2,6},{3,7},{4,0},{5,1},{6,2},{7,3},{8,12},{9,13},{10,... | collective-permute-start | bytes 884744 | tf_op jit(solution)/shard_map/ppermute | solution.py:911
  259.2 41.4 %collective-permute-start.34 = (f32[384,768]{1,0:T(8,128)}, f32[384,768]{1,0:T(8,128)S(1)}, u32[]{:S(2)}, u32[]{:S(2)}) collective-permute-start(f32[384,768]{1,0:T(8,128)} %pad_maximum_fusion.11), channel_id=1, source_target_pairs={{0,4},{1,5},{2,6},{3,7},{4,0},{5,1},{6,2},{7,3},{8,12},{9,13},{10,... | collective-permute-start | bytes 3538952 | tf_op jit(solution)/shard_map/ppermute | solution.py:911
  262.1 38.5 %collective-permute-start.35 = (f32[384,768]{1,0:T(8,128)}, f32[384,768]{1,0:T(8,128)S(1)}, u32[]{:S(2)}, u32[]{:S(2)}) collective-permute-start(f32[384,768]{1,0:T(8,128)} %pad_maximum_fusion.12), channel_id=1, source_target_pairs={{0,2},{1,3},{2,0},{3,1},{4,6},{5,7},{6,4},{7,5},{8,10},{9,11},{10,... | collective-permute-start | bytes 3538952 | tf_op jit(solution)/shard_map/ppermute | solution.py:911
  372.8 78.9 %collective-permute-start.43 = (f32[768,768]{1,0:T(8,128)}, f32[768,768]{1,0:T(8,128)S(1)}, u32[]{:S(2)}, u32[]{:S(2)}) collective-permute-start(f32[768,768]{1,0:T(8,128)} %bitcast.128), channel_id=1, source_target_pairs={{0,2},{1,3},{2,0},{3,1},{4,6},{5,7},{6,4},{7,5},{8,10},{9,11},{10,... | collective-permute-start | bytes 7077896 | tf_op jit(solution)/shard_map/ppermute | solution.py:911
  411.5 73.3 %collective-permute-start.46 = (f32[768,768]{1,0:T(8,128)}, f32[768,768]{1,0:T(8,128)}, u32[]{:S(2)}, u32[]{:S(2)}) collective-permute-start(f32[768,768]{1,0:T(8,128)} %bitcast.129), channel_id=1, source_target_pairs={{0,4},{1,5},{2,6},{3,7},{4,0},{5,1},{6,2},{7,3},{8,12},{9,13},{10,... | collective-permute-start | bytes 7077896 | tf_op jit(solution)/shard_map/ppermute | solution.py:911
  467.9 33.2 %collective-permute-start.44 = (f32[512,768]{1,0:T(8,128)}, f32[512,768]{1,0:T(8,128)S(1)}, u32[]{:S(2)}, u32[]{:S(2)}) collective-permute-start(f32[512,768]{1,0:T(8,128)} %get-tuple-element.371.refs_2_), channel_id=1, source_target_pairs={{0,1},{1,0},{2,3},{3,2},{4,5},{5,4},{6,7},{7,6},{8,9},{9,8},{10,11... | collective-permute-start | bytes 4718600 | tf_op jit(solution)/shard_map/ppermute | solution.py:911
  468.0 35.4 %collective-permute-start.45 = (f32[512,768]{1,0:T(8,128)}, f32[512,768]{1,0:T(8,128)}, u32[]{:S(2)}, u32[]{:S(2)}) collective-permute-start(f32[512,768]{1,0:T(8,128)} %get-tuple-element.372.refs_3_), channel_id=1, source_target_pairs={{0,1},{1,0},{2,3},{3,2},{4,5},{5,4},{6,7},{7,6},{8,9},{9,8},{10,11... | collective-permute-start | bytes 4718600 | tf_op jit(solution)/shard_map/ppermute | solution.py:911
  473.1 58.5 %collective-permute-start.47 = (f32[1024,384]{1,0:T(8,128)}, f32[1024,384]{1,0:T(8,128)}, u32[]{:S(2)}, u32[]{:S(2)}) collective-permute-start(f32[1024,384]{1,0:T(8,128)} %pad_maximum_fusion.3), channel_id=1, source_target_pairs={{0,16},{2,18},{4,20},{6,22},{8,24},{10,26},{12,28},{14,30},{17,1},... | collective-permute-start | bytes 4718600 | tf_op jit(solution)/shard_map/ppermute | solution.py:911
  483.8 47.9 %collective-permute-start.48 = (f32[384,768]{1,0:T(8,128)}, f32[384,768]{1,0:T(8,128)S(1)}, u32[]{:S(2)}, u32[]{:S(2)}) collective-permute-start(f32[384,768]{1,0:T(8,128)} %get-tuple-element.395), channel_id=1, source_target_pairs={{0,4},{1,5},{2,6},{3,7},{4,0},{5,1},{6,2},{7,3},{8,12},{9,13},{10,... | collective-permute-start | bytes 3538952 | tf_op jit(solution)/shard_map/ppermute | solution.py:911
  500.0 31.6 %collective-permute-start.49 = (f32[384,768]{1,0:T(8,128)}, f32[384,768]{1,0:T(8,128)}, u32[]{:S(2)}, u32[]{:S(2)}) collective-permute-start(f32[384,768]{1,0:T(8,128)} %get-tuple-element.397), channel_id=1, source_target_pairs={{0,2},{1,3},{2,0},{3,1},{4,6},{5,7},{6,4},{7,5},{8,10},{9,11},{10,... | collective-permute-start | bytes 3538952 | tf_op jit(solution)/shard_map/ppermute | solution.py:911
  502.3 64.6 %collective-permute-start.52 = (f32[768,768]{1,0:T(8,128)}, f32[768,768]{1,0:T(8,128)S(1)}, u32[]{:S(2)}, u32[]{:S(2)}) collective-permute-start(f32[768,768]{1,0:T(8,128)} %bitcast.126), channel_id=1, source_target_pairs={{0,4},{1,5},{2,6},{3,7},{4,0},{5,1},{6,2},{7,3},{8,12},{9,13},{10,... | collective-permute-start | bytes 7077896 | tf_op jit(solution)/shard_map/ppermute | solution.py:911
  530.5 51.4 %collective-permute-start.53 = (f32[768,768]{1,0:T(8,128)}, f32[768,768]{1,0:T(8,128)}, u32[]{:S(2)}, u32[]{:S(2)}) collective-permute-start(f32[768,768]{1,0:T(8,128)} %bitcast.127), channel_id=1, source_target_pairs={{0,2},{1,3},{2,0},{3,1},{4,6},{5,7},{6,4},{7,5},{8,10},{9,11},{10,... | collective-permute-start | bytes 7077896 | tf_op jit(solution)/shard_map/ppermute | solution.py:911
  580.9 41.1 %collective-permute-start.55 = (f32[384,768]{1,0:T(8,128)}, f32[384,768]{1,0:T(8,128)}, u32[]{:S(2)}, u32[]{:S(2)}) collective-permute-start(f32[384,768]{1,0:T(8,128)} %get-tuple-element.423), channel_id=1, source_target_pairs={{0,2},{1,3},{2,0},{3,1},{4,6},{5,7},{6,4},{7,5},{8,10},{9,11},{10,... | collective-permute-start | bytes 3538952 | tf_op jit(solution)/shard_map/ppermute | solution.py:911
  585.7 38.1 %collective-permute-start.56 = (f32[384,768]{1,0:T(8,128)}, f32[384,768]{1,0:T(8,128)}, u32[]{:S(2)}, u32[]{:S(2)}) collective-permute-start(f32[384,768]{1,0:T(8,128)} %get-tuple-element.546), channel_id=1, source_target_pairs={{0,4},{1,5},{2,6},{3,7},{4,0},{5,1},{6,2},{7,3},{8,12},{9,13},{10,... | collective-permute-start | bytes 3538952 | tf_op jit(solution)/shard_map/ppermute | solution.py:911
  586.7 47.4 %collective-permute-start.57 = (f32[384,768]{1,0:T(8,128)}, f32[384,768]{1,0:T(8,128)S(1)}, u32[]{:S(2)}, u32[]{:S(2)}) collective-permute-start(f32[384,768]{1,0:T(8,128)} %bitcast.34), channel_id=1, source_target_pairs={{0,2},{1,3},{2,0},{3,1},{4,6},{5,7},{6,4},{7,5},{8,10},{9,11},{10,... | collective-permute-start | bytes 3538952 | tf_op jit(solution)/shard_map/ppermute | solution.py:911
  587.6 50.9 %collective-permute-start.58 = (f32[384,768]{1,0:T(8,128)}, f32[384,768]{1,0:T(8,128)S(1)}, u32[]{:S(2)}, u32[]{:S(2)}) collective-permute-start(f32[384,768]{1,0:T(8,128)} %bitcast.36), channel_id=1, source_target_pairs={{0,4},{1,5},{2,6},{3,7},{4,0},{5,1},{6,2},{7,3},{8,12},{9,13},{10,... | collective-permute-start | bytes 3538952 | tf_op jit(solution)/shard_map/ppermute | solution.py:911
  627.1 43.2 %collective-permute-start.63 = (f32[384,768]{1,0:T(8,128)}, f32[384,768]{1,0:T(8,128)S(1)}, u32[]{:S(2)}, u32[]{:S(2)}) collective-permute-start(f32[384,768]{1,0:T(8,128)} %pad_maximum_fusion.14), channel_id=1, source_target_pairs={{0,8},{1,9},{2,10},{3,11},{4,12},{5,13},{6,14},{7,15},{8,0},{9,1},... | collective-permute-start | bytes 3538952 | tf_op jit(solution)/shard_map/ppermute | solution.py:911
  670.9 41.2 %collective-permute-start.59 = (f32[384,768]{1,0:T(8,128)}, f32[384,768]{1,0:T(8,128)}, u32[]{:S(2)}, u32[]{:S(2)}) collective-permute-start(f32[384,768]{1,0:T(8,128)} %bitcast.131), channel_id=1, source_target_pairs={{0,2},{1,3},{2,0},{3,1},{4,6},{5,7},{6,4},{7,5},{8,10},{9,11},{10,... | collective-permute-start | bytes 3538952 | tf_op jit(solution)/shard_map/ppermute | solution.py:911
  671.9 40.2 %collective-permute-start.66 = (f32[384,768]{1,0:T(8,128)}, f32[384,768]{1,0:T(8,128)}, u32[]{:S(2)}, u32[]{:S(2)}) collective-permute-start(f32[384,768]{1,0:T(8,128)} %bitcast.130), channel_id=1, source_target_pairs={{0,4},{1,5},{2,6},{3,7},{4,0},{5,1},{6,2},{7,3},{8,12},{9,13},{10,... | collective-permute-start | bytes 3538952 | tf_op jit(solution)/shard_map/ppermute | solution.py:911
  678.7 32.4 %collective-permute-start.62 = (f32[192,768]{1,0:T(8,128)}, f32[192,768]{1,0:T(8,128)S(1)}, u32[]{:S(2)}, u32[]{:S(2)}) collective-permute-start(f32[192,768]{1,0:T(8,128)} %pad_maximum_fusion.19), channel_id=1, source_target_pairs={{0,8},{1,9},{2,10},{3,11},{4,12},{5,13},{6,14},{7,15},{8,0},{9,1},... | collective-permute-start | bytes 1769480 | tf_op jit(solution)/shard_map/ppermute | solution.py:911
  705.2 42.1 %collective-permute-start.71 = (f32[1024,384]{1,0:T(8,128)}, f32[1024,384]{1,0:T(8,128)}, u32[]{:S(2)}, u32[]{:S(2)}) collective-permute-start(f32[1024,384]{1,0:T(8,128)} %get-tuple-element.473), channel_id=1, source_target_pairs={{0,8},{2,10},{4,12},{6,14},{8,0},{10,2},{12,4},{14,6},{17,25},{19,... | collective-permute-start | bytes 4718600 | tf_op jit(solution)/shard_map/ppermute | solution.py:911
  714.3 32.9 %collective-permute-start.68 = (f32[192,768]{1,0:T(8,128)S(1)}, f32[192,768]{1,0:T(8,128)S(1)}, u32[]{:S(2)}, u32[]{:S(2)}) collective-permute-start(f32[192,768]{1,0:T(8,128)S(1)} %get-tuple-element.560), channel_id=1, source_target_pairs={{0,4},{1,5},{2,6},{3,7},{4,0},{5,1},{6,2},{7,3},{8,12},{9,13},{10,... | collective-permute-start | bytes 1769480 | tf_op jit(solution)/shard_map/ppermute | solution.py:911
  719.9 39.8 %collective-permute-start.75 = (f32[192,768]{1,0:T(8,128)}, f32[192,768]{1,0:T(8,128)}, u32[]{:S(2)}, u32[]{:S(2)}) collective-permute-start(f32[192,768]{1,0:T(8,128)} %slice_select_fusion.8), channel_id=1, source_target_pairs={{0,16},{1,17},{2,18},{3,19},{4,20},{5,21},{6,22},{7,23},{8,24},{9,... | collective-permute-start | bytes 1769480 | tf_op jit(solution)/shard_map/ppermute | solution.py:911
  762.4 46.1 %collective-permute-start.77 = (f32[192,768]{1,0:T(8,128)}, f32[192,768]{1,0:T(8,128)}, u32[]{:S(2)}, u32[]{:S(2)}) collective-permute-start(f32[192,768]{1,0:T(8,128)} %slice_select_fusion.4), channel_id=1, source_target_pairs={{0,16},{1,17},{2,18},{3,19},{4,20},{5,21},{6,22},{7,23},{8,24},{9,... | collective-permute-start | bytes 1769480 | tf_op jit(solution)/shard_map/ppermute | solution.py:911
  778.0 48.9 %collective-permute-start.73 = (f32[1024,384]{1,0:T(8,128)}, f32[1024,384]{1,0:T(8,128)S(1)}, u32[]{:S(2)}, u32[]{:S(2)}) collective-permute-start(f32[1024,384]{1,0:T(8,128)} %pad_maximum_fusion.4), channel_id=1, source_target_pairs={{0,16},{2,18},{4,20},{6,22},{8,24},{10,26},{12,28},{14,30},{17,1},... | collective-permute-start | bytes 4718600 | tf_op jit(solution)/shard_map/ppermute | solution.py:911
  (129 other events, 2264.0 us)

commit v4 on v3

--- a/solution.py
+++ b/solution.py
@@ -1289,23 +1289,24 @@
     doh = after(doh, *down_0.after(out_bias_sum).advance())
     grads = ride(attn_heads_back, [feed_1], ph, pl_, doh, dol, oh, ol, lse)
     mixed = attn_1.merge(down_0)
-    grads[0] = after(grads[0], *mixed.after(grads[0]).advance())
+    *e, attn_vec = attn_back_two("e", 0, flags[0], grads, xh, xl, vec, wh, wl, do)
+    e = plan.added(*e)
+    grads[0] = after(grads[0], attn_vec, *mixed.after(attn_vec).advance())
     *pieces, pair_sum = ride(attn_back_two, [up_0], "w", 3, flags[0], grads, xh, xl, vec, wh, wl, do)
     attn_0 = Sum(plan, 3, pieces)
-    *e, attn_vec = attn_back_two("e", 0, flags[0], [after(grads[0], pair_sum), *grads[1:]], xh, xl, vec, wh, wl, do)
-    e = plan.added(*mixed.wait(*up_0.wait(*e)))
+    e = (*e[:2], after(e[2], pair_sum), after(e[3], pair_sum))
     small[0] = (attn_vec, pair_sum, out_bias_sum, ffn_vec, up_bias_sum, down_bias_sum)
 
     def cross(low, high):
         on = jnp.where(low_planes, high, low)
         return jnp.where(low_planes, low, high), on, plan.along_z(on, 2)
 
-    feed_1, mixed = feed_1.finish(), mixed.finish()
+    grad_near, grad_far, row_sum = finish(plane_flags, g, e, xh, xl, x_scale, mask)
+    feed_1, mixed = feed_1.finish(), mixed.after(grad_far).finish()
     down_mine, down_on, down_got = cross(mixed[count:], feed_1[:count])
-    g = after(g, down_on, *up_0.advance())
-    grad_near, grad_far, row_sum = finish(plane_flags, g, e, xh, xl, x_scale, mask)
+    up_0.after(grad_far).advance()
     out_rows = settle_rows(out_near, out_beside, out_beyond)
-    grad_beside = beside(after(grad_far, down_got))
+    grad_beside = beside(grad_far)
 
     up_mine, up_on, up_got = cross(up_0.after(grad_far).finish(), feed_1[count:])
     pack_flags = jnp.stack([z % 2, core, sequence]).astype(jnp.int32)

time: 840 us -> 842 us (level)
  transfers between devices with their start and end apart: 82 -> 82, of which waited for: 23 -> 22; matrix products, arithmetic and copies ran while one was open for 15% -> 14% of each run, Pallas kernels for 44% -> 44%
where the time goes in v4:
time: 842 us; the launch traced here: 832 us
  Pallas kernels  402 us (48%)
  waiting for transfers between devices  166 us (20%)
  starting transfers between devices  107 us (13%)
  local copies, waits for them, and re-layouts  82.3 us (10%)
  other arithmetic  69.1 us (8%)
    pallas_call x25, Pallas kernels, call(): pl.pallas_call(whole, grid=(grid,), in_specs=in_specs, out_specs=list(out...  402 us
    ppermute x82, waiting for transfers between devices, permute(): return lax.ppermute(value, AXES, pairs)  166 us
    ppermute x82, starting transfers between devices, permute(): return lax.ppermute(value, AXES, pairs)  107 us
    unnamed x164, local copies, waits for them, and re-layouts  29.6 us
  transfers between devices with their start and end apart: 82, of which 22 were waited for; matrix products, arithmetic and copies ran while one was open for 14% of the time, Pallas kernels for 44%

profile of v4, /device:TPU:0, one launch (start us, length us, event | category | flops | bytes accessed | tf_op | source)
XLA Modules:
  0.0 832.2 jit_solution(11154862382327525700)
XLA Ops:
  28.4 15.2 %collective-permute-done = f32[208,768]{1,0:T(8,128)} collective-permute-done((f32[208,768]{1,0:T(8,128)}, f32[208,768]{1,0:T(8,128)}, u32[]{:S(2)}, u32[]{:S(2)}) %collective-permute-start) | collective-permute-done | bytes 639008 | tf_op jit(solution)/shard_map/ppermute | solution.py:911
  61.9 10.4 %collective-permute-done.3 = f32[208,768]{1,0:T(8,128)} collective-permute-done((f32[208,768]{1,0:T(8,128)}, f32[208,768]{1,0:T(8,128)}, u32[]{:S(2)}, u32[]{:S(2)}) %collective-permute-start.3) | collective-permute-done | bytes 639008 | tf_op jit(solution)/shard_map/ppermute | solution.py:911
  110.8 11.1 %collective-permute-done.12 = f32[192,768]{1,0:T(8,128)S(1)} collective-permute-done((f32[192,768]{1,0:T(8,128)S(1)}, f32[192,768]{1,0:T(8,128)S(1)}, u32[]{:S(2)}, u32[]{:S(2)}) %collective-permute-start.12) | collective-permute-done | bytes 589856 | tf_op jit(solution)/shard_map/ppermute | solution.py:911
  129.5 13.5 %attn_in.2 = (bf16[1024,768]{1,0:T(8,128)(2,1)}, bf16[1024,768]{1,0:T(8,128)(2,1)}, f32[1024,1]{1,0:T(8,128)}, bf16[1152,1024]{1,0:T(8,128)(2,1)}, bf16[1152,102...) custom-call(s32[5]{0:T(128)} %get-tuple-element.601.refs_0_, ...), custom_call_target="tpu_custom_call" | custom-call | flops 1 | bytes 1 | tf_op jit(solution)/shard_map/attn_in/pallas_call | solution.py:194
  156.0 20.0 %attn_heads.2 = (bf16[384,1024]{1,0:T(8,128)(2,1)}, bf16[384,1024]{1,0:T(8,128)(2,1)}, f32[6,1,1024]{2,1,0:T(1,128)}, f32[512,768]{1,0:T(8,128)}, f32[512,768]{1,0:T(8,128)}) custom-call(bf16[1152,1024]{1,0:T(8,128)(2,1)} %get-tuple-element.276.refs_0_.refs_2_.refs_4_, bf16[1152,1024]{1,0:T(8,128)(2,1)} %get-tuple-element.277.refs_1_.refs_3_.refs_5_, ...), custom_call_target="tpu_custom_call" | custom-call | flops 1 | bytes 1 | tf_op jit(solution)/shard_map/attn_heads/pallas_call | solution.py:194
  179.7 12.2 %collective-permute-done.21.refs_6_ = f32[192,768]{1,0:T(8,128)S(1)} collective-permute-done((f32[192,768]{1,0:T(8,128)S(1)}, f32[192,768]{1,0:T(8,128)S(1)}, u32[]{:S(2)}, u32[]{:S(2)}) %collective-permute-start.21) | collective-permute-done | bytes 589856 | tf_op jit(solution)/shard_map/ppermute | solution.py:911
  202.7 19.3 %feed_up.2 = (f32[1024,768]{1,0:T(8,128)}, bf16[1024,768]{1,0:T(8,128)(2,1)}, bf16[1024,768]{1,0:T(8,128)(2,1)}, f32[1024,1]{1,0:T(8,128)}, bf16[1024,1536]{1,0:...) custom-call(s32[5]{0:T(128)} %get-tuple-element.601.refs_0_, ...), custom_call_target="tpu_custom_call" | custom-call | flops 1 | bytes 1 | tf_op jit(solution)/shard_map/feed_up/pallas_call | solution.py:194
  239.1 15.6 %feed_down.2 = (f32[512,768]{1,0:T(8,128)}, f32[512,768]{1,0:T(8,128)}, bf16[2,768,768]{2,1,0:T(8,128)(2,1)}, bf16[2,768,768]{2,1,0:T(8,128)(2,1)}) custom-call(s32[5]{0:T(128)} %get-tuple-element.601.refs_0_, bf16[1024,1536]{1,0:T(8,128)(2,1)} %get-tuple-element.292.refs_1_.refs_11_, bf16[1024,1536]{1,0:T(8,128)(2,1)} %get-tuple-element.293.refs_2_.refs_12_, ...), custom_call_target="tpu_custom_call" | custom-call | flops 1 | bytes 1 | tf_op jit(solution)/shard_map/feed_down/pallas_call | solution.py:194
  264.7 16.2 %attn_in.3 = (f32[1024,768]{1,0:T(8,128)}, bf16[1024,768]{1,0:T(8,128)(2,1)}, bf16[1024,768]{1,0:T(8,128)(2,1)}, f32[1024,1]{1,0:T(8,128)}, bf16[1152,1024]{1,0:...) custom-call(s32[5]{0:T(128)} %get-tuple-element.600.refs_0_, ...), custom_call_target="tpu_custom_call" | custom-call | flops 1 | bytes 1 | tf_op jit(solution)/shard_map/attn_in/pallas_call | solution.py:194
  280.9 20.0 %attn_heads.3 = (bf16[384,1024]{1,0:T(8,128)(2,1)}, bf16[384,1024]{1,0:T(8,128)(2,1)}, f32[6,1,1024]{2,1,0:T(1,128)}, f32[512,768]{1,0:T(8,128)}, f32[512,768]{1,0:T(8,128)}) custom-call(bf16[1152,1024]{1,0:T(8,128)(2,1)} %get-tuple-element.310.refs_0_.refs_2_.refs_4_, bf16[1152,1024]{1,0:T(8,128)(2,1)} %get-tuple-element.311.refs_1_.refs_3_.refs_5_, ...), custom_call_target="tpu_custom_call" | custom-call | flops 1 | bytes 1 | tf_op jit(solution)/shard_map/attn_heads/pallas_call | solution.py:194
  309.0 19.2 %feed_up.3 = (f32[1024,768]{1,0:T(8,128)}, bf16[1024,768]{1,0:T(8,128)(2,1)}, bf16[1024,768]{1,0:T(8,128)(2,1)}, f32[1024,1]{1,0:T(8,128)}, bf16[1024,1536]{1,0:...) custom-call(s32[5]{0:T(128)} %get-tuple-element.600.refs_0_, ...), custom_call_target="tpu_custom_call" | custom-call | flops 1 | bytes 1 | tf_op jit(solution)/shard_map/feed_up/pallas_call | solution.py:194
  328.2 15.9 %feed_down.3 = (f32[512,768]{1,0:T(8,128)}, f32[512,768]{1,0:T(8,128)}, bf16[2,768,768]{2,1,0:T(8,128)(2,1)}, bf16[2,768,768]{2,1,0:T(8,128)(2,1)}) custom-call(s32[5]{0:T(128)} %get-tuple-element.600.refs_0_, bf16[1024,1536]{1,0:T(8,128)(2,1)} %get-tuple-element.319.refs_1_.refs_4_, bf16[1024,1536]{1,0:T(8,128)(2,1)} %get-tuple-element.320.refs_2_.refs_5_, ...), custom_call_target="tpu_custom_call" | custom-call | flops 1 | bytes 1 | tf_op jit(solution)/shard_map/feed_down/pallas_call | solution.py:194
  349.3 23.6 %feed_back_one.2 = (f32[1024,768]{1,0:T(8,128)}, bf16[1024,1536]{1,0:T(8,128)(2,1)}, bf16[1024,1536]{1,0:T(8,128)(2,1)}, f32[2,2,192,768]{3,2,1,0:T(8,128)}, f32...) custom-call(s32[5]{0:T(128)} %get-tuple-element.600.refs_0_, ...), custom_call_target="tpu_custom_call" | custom-call | flops 1 | bytes 1 | tf_op jit(solution)/shard_map/feed_back_one/pallas_call | solution.py:194
  384.7 13.6 %feed_back_two_e.2 = (f32[512,768]{1,0:T(8,128)}, f32[512,768]{1,0:T(8,128)}, f32[4,768]{1,0:T(4,128)}) custom-call(s32[5]{0:T(128)} %get-tuple-element.600.refs_0_, bf16[1024,1536]{1,0:T(8,128)(2,1)} %get-tuple-element.343.refs_1_, bf16[1024,1536]{1,0:T(8,128)(2,1)} %get-tuple-element.335.refs_2_, bf16[1024,768]{1,0:T(8,128)(2,1)} %get-tuple-element.336.refs_3_.refs_5_, ...), custom_call_target="tpu_custom_call" | custom-call | flops 1 | bytes 1 | tf_op jit(solution)/shard_map/feed_back_two_e/pallas_call | solution.py:194
  398.9 13.2 %feed_back_two_w.2 = (f32[2,2,192,768]{3,2,1,0:T(8,128)}, f32[2,2,192,768]{3,2,1,0:T(8,128)}) custom-call(s32[5]{0:T(128)} %get-tuple-element.600.refs_0_, bf16[1024,1536]{1,0:T(8,128)(2,1)} %get-tuple-element.343.refs_1_, bf16[1024,1536]{1,0:T(8,128)(2,1)} %get-tuple-element.335.refs_2_, bf16[1024,768]{1,0:T(8,128)(2,1)} %get-tuple-element.336.refs_3_.refs_5_, ...), custom_call_target="tpu_custom_call" | custom-call | flops 1 | bytes 1 | tf_op jit(solution)/shard_map/feed_back_two_w/pallas_call | solution.py:194
  412.6 11.3 %attn_back_one.2 = (f32[1024,768]{1,0:T(8,128)}, bf16[384,1024]{1,0:T(8,128)(2,1)}, bf16[384,1024]{1,0:T(8,128)(2,1)}, f32[384,768]{1,0:T(8,128)}, f32[1,768]{1,0:T(1,128)}) custom-call(f32[1024,768]{1,0:T(8,128)} %get-tuple-element.346.refs_0_, f32[512,768]{1,0:T(8,128)} %get-tuple-element.340.refs_1_, f32[512,768]{1,0:T(8,128)} %get-tuple-element.341.refs_2_, ...), custom_call_target="tpu_custom_call" | custom-call | flops 1 | bytes 1 | tf_op jit(solution)/shard_map/attn_back_one/pallas_call | solution.py:194
  423.9 28.3 %attn_heads_back.2 = (bf16[384,1024]{1,0:T(8,128)(2,1)}, bf16[384,1024]{1,0:T(8,128)(2,1)}, bf16[384,1024]{1,0:T(8,128)(2,1)}, bf16[384,1024]{1,0:T(8,128)(2,1)}...) custom-call(bf16[1152,1024]{1,0:T(8,128)(2,1)} %get-tuple-element.310.refs_0_.refs_2_.refs_4_, ...), custom_call_target="tpu_custom_call" | custom-call | flops 1 | bytes 1 | tf_op jit(solution)/shard_map/attn_heads_back/pallas_call | solution.py:194
  453.7 14.7 %attn_back_two_e.2 = (f32[512,768]{1,0:T(8,128)}, f32[512,768]{1,0:T(8,128)}, f32[4,768]{1,0:T(4,128)}, f32[384,768]{1,0:T(8,128)}, f32[384,768]{1,0:T(8,128)}) custom-call(s32[5]{0:T(128)} %get-tuple-element.600.refs_0_, bf16[384,1024]{1,0:T(8,128)(2,1)} %get-tuple-element.356.refs_1_, bf16[384,1024]{1,0:T(8,128)(2,1)} %get-tuple-element.357.refs_2_, ...), custom_call_target="tpu_custom_call" | custom-call | flops 1 | bytes 1 | tf_op jit(solution)/shard_map/attn_back_two_e/pallas_call | solution.py:194
  473.6 10.7 %collective-permute-start.47 = (f32[1024,384]{1,0:T(8,128)}, f32[1024,384]{1,0:T(8,128)}, u32[]{:S(2)}, u32[]{:S(2)}) collective-permute-start(f32[1024,384]{1,0:T(8,128)} %pad_maximum_fusion.3), channel_id=1, source_target_pairs={{0,16},{2,18},{4,20},{6,22},{8,24},{10,26},{12,28},{14,30},{17,1},... | collective-permute-start | bytes 4718600 | tf_op jit(solution)/shard_map/ppermute | solution.py:911
  485.3 15.2 %attn_back_two_w.2 = (f32[2,2,192,768]{3,2,1,0:T(8,128)}, f32[2,2,192,768]{3,2,1,0:T(8,128)}, f32[2,8,576]{2,1,0:T(8,128)}, f32[384,768]{1,0:T(8,128)}, f32[384,768]{1,0:T(8,128)}) custom-call(s32[5]{0:T(128)} %get-tuple-element.600.refs_0_, bf16[384,1024]{1,0:T(8,128)(2,1)} %get-tuple-element.356.refs_1_, bf16[384,1024]{1,0:T(8,128)(2,1)} %get-tuple-element.357.refs_2_, ...), custom_call_target="tpu_custom_call" | custom-call | flops 1 | bytes 1 | tf_op jit(solution)/shard_map/attn_back_two_w/pallas_call | solution.py:194
  503.9 27.2 %feed_back_one.3 = (f32[1024,768]{1,0:T(8,128)}, bf16[1024,1536]{1,0:T(8,128)(2,1)}, bf16[1024,1536]{1,0:T(8,128)(2,1)}, f32[2,2,192,768]{3,2,1,0:T(8,128)}, f32...) custom-call(s32[5]{0:T(128)} %get-tuple-element.601.refs_0_, f32[1024,768]{1,0:T(8,128)} %get-tuple-element.373.refs_1_, ...), custom_call_target="tpu_custom_call" | custom-call | flops 1 | bytes 1 | tf_op jit(solution)/shard_map/feed_back_one/pallas_call | solution.py:194
  533.1 15.1 %feed_back_two_e.3 = (f32[512,768]{1,0:T(8,128)}, f32[512,768]{1,0:T(8,128)}, f32[4,768]{1,0:T(4,128)}, f32[384,768]{1,0:T(8,128)}, f32[384,768]{1,0:T(8,128)}) custom-call(s32[5]{0:T(128)} %get-tuple-element.601.refs_0_, bf16[1024,1536]{1,0:T(8,128)(2,1)} %get-tuple-element.396.refs_1_, bf16[1024,1536]{1,0:T(8,128)(2,1)} %get-tuple-element.384.refs_2_, ...), custom_call_target="tpu_custom_call" | custom-call | flops 1 | bytes 1 | tf_op jit(solution)/shard_map/feed_back_two_e/pallas_call | solution.py:194
  548.8 13.4 %feed_back_two_w.3 = (f32[2,2,96,768]{3,2,1,0:T(8,128)}, f32[2,2,96,768]{3,2,1,0:T(8,128)}, f32[2,2,96,768]{3,2,1,0:T(8,128)}, f32[2,2,96,768]{3,2,1,0:T(8,128)}) custom-call(s32[5]{0:T(128)} %get-tuple-element.601.refs_0_, bf16[1024,1536]{1,0:T(8,128)(2,1)} %get-tuple-element.396.refs_1_, bf16[1024,1536]{1,0:T(8,128)(2,1)} %get-tuple-element.384.refs_2_, ...), custom_call_target="tpu_custom_call" | custom-call | flops 1 | bytes 1 | tf_op jit(solution)/shard_map/feed_back_two_w/pallas_call | solution.py:194
  565.4 12.5 %attn_back_one.3 = (f32[1024,768]{1,0:T(8,128)}, bf16[384,1024]{1,0:T(8,128)(2,1)}, bf16[384,1024]{1,0:T(8,128)(2,1)}, f32[384,768]{1,0:T(8,128)}, f32[1,768]{1,...) custom-call(f32[1024,768]{1,0:T(8,128)} %get-tuple-element.398.refs_0_, f32[512,768]{1,0:T(8,128)} %get-tuple-element.393.refs_1_, ...), custom_call_target="tpu_custom_call" | custom-call | flops 1 | bytes 1 | tf_op jit(solution)/shard_map/attn_back_one/pallas_call | solution.py:194
  590.4 28.6 %attn_heads_back.3 = (bf16[384,1024]{1,0:T(8,128)(2,1)}, bf16[384,1024]{1,0:T(8,128)(2,1)}, bf16[384,1024]{1,0:T(8,128)(2,1)}, bf16[384,1024]{1,0:T(8,128)(2,1)}...) custom-call(bf16[1152,1024]{1,0:T(8,128)(2,1)} %get-tuple-element.276.refs_0_.refs_2_.refs_4_, ...), custom_call_target="tpu_custom_call" | custom-call | flops 1 | bytes 1 | tf_op jit(solution)/shard_map/attn_heads_back/pallas_call | solution.py:194
  619.0 13.5 %attn_back_two_e.3 = (f32[512,768]{1,0:T(8,128)}, f32[512,768]{1,0:T(8,128)}, f32[4,768]{1,0:T(4,128)}) custom-call(s32[5]{0:T(128)} %get-tuple-element.601.refs_0_, bf16[384,1024]{1,0:T(8,128)(2,1)} %get-tuple-element.429.refs_1_, bf16[384,1024]{1,0:T(8,128)(2,1)} %get-tuple-element.417.refs_2_, bf16[384,1024]{1,0:T(8,128)(2,1)} %get-tuple-element.418.refs_3_, ...), custom_call_target="tpu_custom_call" | custom-call | flops 1 | bytes 1 | tf_op jit(solution)/shard_map/attn_back_two_e/pallas_call | solution.py:194
  639.6 15.3 %attn_back_two_w.3 = (f32[2,2,96,768]{3,2,1,0:T(8,128)}, f32[2,2,96,768]{3,2,1,0:T(8,128)}, f32[2,2,96,768]{3,2,1,0:T(8,128)}, f32[2,2,96,768]{3,2,1,0:T(8,128)}...) custom-call(s32[5]{0:T(128)} %get-tuple-element.601.refs_0_, ...), custom_call_target="tpu_custom_call" | custom-call | flops 1 | bytes 1 | tf_op jit(solution)/shard_map/attn_back_two_w/pallas_call | solution.py:194
  661.8 8.4 %finish.1 = (f32[1024,384]{1,0:T(8,128)}, f32[1024,384]{1,0:T(8,128)}, f32[1,768]{1,0:T(1,128)}) custom-call(s32[2]{0:T(128)} %pad_add_fusion.2.refs_0_, f32[1024,768]{1,0:T(8,128)} %get-tuple-element.439.refs_1_, f32[512,768]{1,0:T(8,128)} %get-tuple-element.440.refs_2_, f32[512,768]{1,0:T(8,128)} %get-tuple-element.441.refs_3_, ...), custom_call_target="tpu_custom_call" | custom-call | flops 1 | bytes 1 | tf_op jit(solution)/shard_map/finish/pallas_call | solution.py:194
  684.4 13.9 %collective-permute-done.64 = f32[192,768]{1,0:T(8,128)S(1)} collective-permute-done((f32[192,768]{1,0:T(8,128)}, f32[192,768]{1,0:T(8,128)S(1)}, u32[]{:S(2)}, u32[]{:S(2)}) %collective-permute-start.64) | collective-permute-done | bytes 589856 | tf_op jit(solution)/shard_map/ppermute | solution.py:911
  710.8 18.3 %collective-permute-done.70 = f32[56,768]{1,0:T(8,128)S(1)} collective-permute-done((f32[56,768]{1,0:T(8,128)S(1)}, f32[56,768]{1,0:T(8,128)S(1)}, u32[]{:S(2)}, u32[]{:S(2)}) %collective-permute-start.70) | collective-permute-done | bytes 172064 | tf_op jit(solution)/shard_map/ppermute | solution.py:911
  734.0 19.0 %collective-permute-done.75 = f32[56,768]{1,0:T(8,128)} collective-permute-done((f32[56,768]{1,0:T(8,128)S(1)}, f32[56,768]{1,0:T(8,128)}, u32[]{:S(2)}, u32[]{:S(2)}) %collective-permute-start.75) | collective-permute-done | bytes 172064 | tf_op jit(solution)/shard_map/ppermute | solution.py:911
  776.0 32.9 %collective-permute-done.76 = f32[192,768]{1,0:T(8,128)} collective-permute-done((f32[192,768]{1,0:T(8,128)}, f32[192,768]{1,0:T(8,128)}, u32[]{:S(2)}, u32[]{:S(2)}) %collective-permute-start.76) | collective-permute-done | bytes 589856 | tf_op jit(solution)/shard_map/ppermute | solution.py:911
  (441 shorter events, 290.2 us)
Async XLA Ops:
  11.1 32.5 %collective-permute-start = (f32[208,768]{1,0:T(8,128)}, f32[208,768]{1,0:T(8,128)}, u32[]{:S(2)}, u32[]{:S(2)}) collective-permute-start(f32[208,768]{1,0:T(8,128)} %concatenate.106), channel_id=1, source_target_pairs={{0,16},{1,17},{2,18},{3,19},{4,20},{5,21},{6,22},{7,23},{8,24},{9,... | collective-permute-start | bytes 1916936 | tf_op jit(solution)/shard_map/ppermute | solution.py:911
  47.8 43.1 %collective-permute-start.8 = (f32[1024,768]{1,0:T(8,128)}, f32[1024,768]{1,0:T(8,128)}, u32[]{:S(2)}, u32[]{:S(2)}) collective-permute-start(f32[1024,768]{1,0:T(8,128)} %constant_dynamic-slice_fusion.8), channel_id=1, source_target_pairs={{0,1},{2,3},{4,5},{6,7},{8,9},{10,11},{12,13},{14,15},{17,16},{19,... | collective-permute-start | bytes 9437192 | tf_op jit(solution)/shard_map/ppermute | solution.py:911
  99.0 44.0 %collective-permute-start.9 = (f32[192,768]{1,0:T(8,128)S(1)}, f32[192,768]{1,0:T(8,128)S(1)}, u32[]{:S(2)}, u32[]{:S(2)}) collective-permute-start(f32[192,768]{1,0:T(8,128)S(1)} %collective-permute-done.5.refs_9_), channel_id=1, source_target_pairs={{0,2},{1,3},{2,0},{3,1},{4,6},{5,7},{6,4},{7,5},{8,10},{9,11},{10,... | collective-permute-start | bytes 1769480 | tf_op jit(solution)/shard_map/ppermute | solution.py:911
  99.5 43.4 %collective-permute-start.14 = (f32[192,768]{1,0:T(8,128)}, f32[192,768]{1,0:T(8,128)S(1)}, u32[]{:S(2)}, u32[]{:S(2)}) collective-permute-start(f32[192,768]{1,0:T(8,128)} %constant_dynamic-slice_fusion.9), channel_id=1, source_target_pairs={{0,16},{1,17},{2,18},{3,19},{4,20},{5,21},{6,22},{7,23},{8,24},{9,... | collective-permute-start | bytes 1769480 | tf_op jit(solution)/shard_map/ppermute | solution.py:911
  144.3 31.7 %collective-permute-start.18 = (f32[384,768]{1,0:T(8,128)}, f32[384,768]{1,0:T(8,128)}, u32[]{:S(2)}, u32[]{:S(2)}) collective-permute-start(f32[384,768]{1,0:T(8,128)} %pad_maximum_fusion.7), channel_id=1, source_target_pairs={{0,4},{1,5},{2,6},{3,7},{4,0},{5,1},{6,2},{7,3},{8,12},{9,13},{10,... | collective-permute-start | bytes 3538952 | tf_op jit(solution)/shard_map/ppermute | solution.py:911
  152.5 80.6 %collective-permute-start.25 = (f32[1024,768]{1,0:T(8,128)}, f32[1024,768]{1,0:T(8,128)}, u32[]{:S(2)}, u32[]{:S(2)}) collective-permute-start(f32[1024,768]{1,0:T(8,128)} %constant_dynamic-slice_fusion.5), channel_id=1, source_target_pairs={{0,1},{2,3},{4,5},{6,7},{8,9},{10,11},{12,13},{14,15},{17,16},{19,... | collective-permute-start | bytes 9437192 | tf_op jit(solution)/shard_map/ppermute | solution.py:911
  195.0 43.1 %collective-permute-start.26 = (f32[384,768]{1,0:T(8,128)}, f32[384,768]{1,0:T(8,128)S(1)}, u32[]{:S(2)}, u32[]{:S(2)}) collective-permute-start(f32[384,768]{1,0:T(8,128)} %pad_maximum_fusion.9), channel_id=1, source_target_pairs={{0,4},{1,5},{2,6},{3,7},{4,0},{5,1},{6,2},{7,3},{8,12},{9,13},{10,... | collective-permute-start | bytes 3538952 | tf_op jit(solution)/shard_map/ppermute | solution.py:911
  197.1 41.5 %collective-permute-start.27 = (f32[384,768]{1,0:T(8,128)}, f32[384,768]{1,0:T(8,128)}, u32[]{:S(2)}, u32[]{:S(2)}) collective-permute-start(f32[384,768]{1,0:T(8,128)} %pad_maximum_fusion.10), channel_id=1, source_target_pairs={{0,2},{1,3},{2,0},{3,1},{4,6},{5,7},{6,4},{7,5},{8,10},{9,11},{10,... | collective-permute-start | bytes 3538952 | tf_op jit(solution)/shard_map/ppermute | solution.py:911
  199.3 33.1 %collective-permute-start.17 = (f32[96,768]{1,0:T(8,128)S(1)}, f32[96,768]{1,0:T(8,128)}, u32[]{:S(2)}, u32[]{:S(2)}) collective-permute-start(f32[96,768]{1,0:T(8,128)S(1)} %get-tuple-element.581.refs_15_), channel_id=1, source_target_pairs={{0,4},{1,5},{2,6},{3,7},{4,0},{5,1},{6,2},{7,3},{8,12},{9,13},{10,... | collective-permute-start | bytes 884744 | tf_op jit(solution)/shard_map/ppermute | solution.py:911
  259.5 41.4 %collective-permute-start.34 = (f32[384,768]{1,0:T(8,128)}, f32[384,768]{1,0:T(8,128)S(1)}, u32[]{:S(2)}, u32[]{:S(2)}) collective-permute-start(f32[384,768]{1,0:T(8,128)} %pad_maximum_fusion.11), channel_id=1, source_target_pairs={{0,4},{1,5},{2,6},{3,7},{4,0},{5,1},{6,2},{7,3},{8,12},{9,13},{10,... | collective-permute-start | bytes 3538952 | tf_op jit(solution)/shard_map/ppermute | solution.py:911
  262.5 38.5 %collective-permute-start.35 = (f32[384,768]{1,0:T(8,128)}, f32[384,768]{1,0:T(8,128)S(1)}, u32[]{:S(2)}, u32[]{:S(2)}) collective-permute-start(f32[384,768]{1,0:T(8,128)} %pad_maximum_fusion.12), channel_id=1, source_target_pairs={{0,2},{1,3},{2,0},{3,1},{4,6},{5,7},{6,4},{7,5},{8,10},{9,11},{10,... | collective-permute-start | bytes 3538952 | tf_op jit(solution)/shard_map/ppermute | solution.py:911
  372.9 79.3 %collective-permute-start.43 = (f32[768,768]{1,0:T(8,128)}, f32[768,768]{1,0:T(8,128)S(1)}, u32[]{:S(2)}, u32[]{:S(2)}) collective-permute-start(f32[768,768]{1,0:T(8,128)} %bitcast.128), channel_id=1, source_target_pairs={{0,2},{1,3},{2,0},{3,1},{4,6},{5,7},{6,4},{7,5},{8,10},{9,11},{10,... | collective-permute-start | bytes 7077896 | tf_op jit(solution)/shard_map/ppermute | solution.py:911
  412.0 73.3 %collective-permute-start.46 = (f32[768,768]{1,0:T(8,128)}, f32[768,768]{1,0:T(8,128)}, u32[]{:S(2)}, u32[]{:S(2)}) collective-permute-start(f32[768,768]{1,0:T(8,128)} %bitcast.129), channel_id=1, source_target_pairs={{0,4},{1,5},{2,6},{3,7},{4,0},{5,1},{6,2},{7,3},{8,12},{9,13},{10,... | collective-permute-start | bytes 7077896 | tf_op jit(solution)/shard_map/ppermute | solution.py:911
  468.4 33.2 %collective-permute-start.44 = (f32[512,768]{1,0:T(8,128)}, f32[512,768]{1,0:T(8,128)S(1)}, u32[]{:S(2)}, u32[]{:S(2)}) collective-permute-start(f32[512,768]{1,0:T(8,128)} %get-tuple-element.366.refs_2_), channel_id=1, source_target_pairs={{0,1},{1,0},{2,3},{3,2},{4,5},{5,4},{6,7},{7,6},{8,9},{9,8},{10,11... | collective-permute-start | bytes 4718600 | tf_op jit(solution)/shard_map/ppermute | solution.py:911
  468.4 35.4 %collective-permute-start.45 = (f32[512,768]{1,0:T(8,128)}, f32[512,768]{1,0:T(8,128)}, u32[]{:S(2)}, u32[]{:S(2)}) collective-permute-start(f32[512,768]{1,0:T(8,128)} %get-tuple-element.367.refs_3_), channel_id=1, source_target_pairs={{0,1},{1,0},{2,3},{3,2},{4,5},{5,4},{6,7},{7,6},{8,9},{9,8},{10,11... | collective-permute-start | bytes 4718600 | tf_op jit(solution)/shard_map/ppermute | solution.py:911
  473.6 58.5 %collective-permute-start.47 = (f32[1024,384]{1,0:T(8,128)}, f32[1024,384]{1,0:T(8,128)}, u32[]{:S(2)}, u32[]{:S(2)}) collective-permute-start(f32[1024,384]{1,0:T(8,128)} %pad_maximum_fusion.3), channel_id=1, source_target_pairs={{0,16},{2,18},{4,20},{6,22},{8,24},{10,26},{12,28},{14,30},{17,1},... | collective-permute-start | bytes 4718600 | tf_op jit(solution)/shard_map/ppermute | solution.py:911
  484.3 47.8 %collective-permute-start.48 = (f32[384,768]{1,0:T(8,128)}, f32[384,768]{1,0:T(8,128)S(1)}, u32[]{:S(2)}, u32[]{:S(2)}) collective-permute-start(f32[384,768]{1,0:T(8,128)} %get-tuple-element.390), channel_id=1, source_target_pairs={{0,4},{1,5},{2,6},{3,7},{4,0},{5,1},{6,2},{7,3},{8,12},{9,13},{10,... | collective-permute-start | bytes 3538952 | tf_op jit(solution)/shard_map/ppermute | solution.py:911
  500.5 31.6 %collective-permute-start.49 = (f32[384,768]{1,0:T(8,128)}, f32[384,768]{1,0:T(8,128)}, u32[]{:S(2)}, u32[]{:S(2)}) collective-permute-start(f32[384,768]{1,0:T(8,128)} %get-tuple-element.392), channel_id=1, source_target_pairs={{0,2},{1,3},{2,0},{3,1},{4,6},{5,7},{6,4},{7,5},{8,10},{9,11},{10,... | collective-permute-start | bytes 3538952 | tf_op jit(solution)/shard_map/ppermute | solution.py:911
  502.8 61.1 %collective-permute-start.52 = (f32[768,768]{1,0:T(8,128)}, f32[768,768]{1,0:T(8,128)S(1)}, u32[]{:S(2)}, u32[]{:S(2)}) collective-permute-start(f32[768,768]{1,0:T(8,128)} %bitcast.126), channel_id=1, source_target_pairs={{0,4},{1,5},{2,6},{3,7},{4,0},{5,1},{6,2},{7,3},{8,12},{9,13},{10,... | collective-permute-start | bytes 7077896 | tf_op jit(solution)/shard_map/ppermute | solution.py:911
  531.0 49.8 %collective-permute-start.53 = (f32[768,768]{1,0:T(8,128)}, f32[768,768]{1,0:T(8,128)}, u32[]{:S(2)}, u32[]{:S(2)}) collective-permute-start(f32[768,768]{1,0:T(8,128)} %bitcast.127), channel_id=1, source_target_pairs={{0,2},{1,3},{2,0},{3,1},{4,6},{5,7},{6,4},{7,5},{8,10},{9,11},{10,... | collective-permute-start | bytes 7077896 | tf_op jit(solution)/shard_map/ppermute | solution.py:911
  577.9 54.7 %collective-permute-start.55 = (f32[384,768]{1,0:T(8,128)}, f32[384,768]{1,0:T(8,128)}, u32[]{:S(2)}, u32[]{:S(2)}) collective-permute-start(f32[384,768]{1,0:T(8,128)} %get-tuple-element.426), channel_id=1, source_target_pairs={{0,2},{1,3},{2,0},{3,1},{4,6},{5,7},{6,4},{7,5},{8,10},{9,11},{10,... | collective-permute-start | bytes 3538952 | tf_op jit(solution)/shard_map/ppermute | solution.py:911
  583.8 51.0 %collective-permute-start.56 = (f32[384,768]{1,0:T(8,128)}, f32[384,768]{1,0:T(8,128)}, u32[]{:S(2)}, u32[]{:S(2)}) collective-permute-start(f32[384,768]{1,0:T(8,128)} %get-tuple-element.536), channel_id=1, source_target_pairs={{0,4},{1,5},{2,6},{3,7},{4,0},{5,1},{6,2},{7,3},{8,12},{9,13},{10,... | collective-permute-start | bytes 3538952 | tf_op jit(solution)/shard_map/ppermute | solution.py:911
  584.8 53.4 %collective-permute-start.57 = (f32[384,768]{1,0:T(8,128)}, f32[384,768]{1,0:T(8,128)S(1)}, u32[]{:S(2)}, u32[]{:S(2)}) collective-permute-start(f32[384,768]{1,0:T(8,128)} %bitcast.34), channel_id=1, source_target_pairs={{0,2},{1,3},{2,0},{3,1},{4,6},{5,7},{6,4},{7,5},{8,10},{9,11},{10,... | collective-permute-start | bytes 3538952 | tf_op jit(solution)/shard_map/ppermute | solution.py:911
  585.8 52.4 %collective-permute-start.58 = (f32[384,768]{1,0:T(8,128)}, f32[384,768]{1,0:T(8,128)S(1)}, u32[]{:S(2)}, u32[]{:S(2)}) collective-permute-start(f32[384,768]{1,0:T(8,128)} %bitcast.36), channel_id=1, source_target_pairs={{0,4},{1,5},{2,6},{3,7},{4,0},{5,1},{6,2},{7,3},{8,12},{9,13},{10,... | collective-permute-start | bytes 3538952 | tf_op jit(solution)/shard_map/ppermute | solution.py:911
  658.0 40.2 %collective-permute-start.72 = (f32[384,768]{1,0:T(8,128)}, f32[384,768]{1,0:T(8,128)S(1)}, u32[]{:S(2)}, u32[]{:S(2)}) collective-permute-start(f32[384,768]{1,0:T(8,128)} %pad_maximum_fusion.14), channel_id=1, source_target_pairs={{0,8},{1,9},{2,10},{3,11},{4,12},{5,13},{6,14},{7,15},{8,0},{9,1},... | collective-permute-start | bytes 3538952 | tf_op jit(solution)/shard_map/ppermute | solution.py:911
  659.7 42.4 %collective-permute-start.59 = (f32[384,768]{1,0:T(8,128)}, f32[384,768]{1,0:T(8,128)}, u32[]{:S(2)}, u32[]{:S(2)}) collective-permute-start(f32[384,768]{1,0:T(8,128)} %bitcast.131), channel_id=1, source_target_pairs={{0,2},{1,3},{2,0},{3,1},{4,6},{5,7},{6,4},{7,5},{8,10},{9,11},{10,... | collective-permute-start | bytes 3538952 | tf_op jit(solution)/shard_map/ppermute | solution.py:911
  660.7 41.4 %collective-permute-start.65 = (f32[384,768]{1,0:T(8,128)}, f32[384,768]{1,0:T(8,128)}, u32[]{:S(2)}, u32[]{:S(2)}) collective-permute-start(f32[384,768]{1,0:T(8,128)} %bitcast.130), channel_id=1, source_target_pairs={{0,4},{1,5},{2,6},{3,7},{4,0},{5,1},{6,2},{7,3},{8,12},{9,13},{10,... | collective-permute-start | bytes 3538952 | tf_op jit(solution)/shard_map/ppermute | solution.py:911
  682.1 46.9 %collective-permute-start.69 = (f32[1024,384]{1,0:T(8,128)S(1)}, f32[1024,384]{1,0:T(8,128)S(1)}, u32[]{:S(2)}, u32[]{:S(2)}) collective-permute-start(f32[1024,384]{1,0:T(8,128)S(1)} %copy-done.78), channel_id=1, source_target_pairs={{0,8},{2,10},{4,12},{6,14},{8,0},{10,2},{12,4},{14,6},{17,25},{19,... | collective-permute-start | bytes 4718600 | tf_op jit(solution)/shard_map/ppermute | solution.py:911
  708.8 45.2 %collective-permute-start.74 = (f32[192,768]{1,0:T(8,128)}, f32[192,768]{1,0:T(8,128)}, u32[]{:S(2)}, u32[]{:S(2)}) collective-permute-start(f32[192,768]{1,0:T(8,128)} %get-tuple-element.546), channel_id=1, source_target_pairs={{0,16},{1,17},{2,18},{3,19},{4,20},{5,21},{6,22},{7,23},{8,24},{9,... | collective-permute-start | bytes 1769480 | tf_op jit(solution)/shard_map/ppermute | solution.py:911
  731.2 77.8 %collective-permute-start.79 = (f32[192,768]{1,0:T(8,128)}, f32[192,768]{1,0:T(8,128)}, u32[]{:S(2)}, u32[]{:S(2)}) collective-permute-start(f32[192,768]{1,0:T(8,128)} %get-tuple-element.545), channel_id=1, source_target_pairs={{0,16},{1,17},{2,18},{3,19},{4,20},{5,21},{6,22},{7,23},{8,24},{9,... | collective-permute-start | bytes 1769480 | tf_op jit(solution)/shard_map/ppermute | solution.py:911
  756.0 52.9 %collective-permute-start.76 = (f32[192,768]{1,0:T(8,128)}, f32[192,768]{1,0:T(8,128)}, u32[]{:S(2)}, u32[]{:S(2)}) collective-permute-start(f32[192,768]{1,0:T(8,128)} %slice_select_fusion.5), channel_id=1, source_target_pairs={{0,16},{1,17},{2,18},{3,19},{4,20},{5,21},{6,22},{7,23},{8,24},{9,... | collective-permute-start | bytes 1769480 | tf_op jit(solution)/shard_map/ppermute | solution.py:911
  772.1 56.2 %collective-permute-start.71 = (f32[1024,384]{1,0:T(8,128)}, f32[1024,384]{1,0:T(8,128)S(1)}, u32[]{:S(2)}, u32[]{:S(2)}) collective-permute-start(f32[1024,384]{1,0:T(8,128)} %pad_maximum_fusion.4), channel_id=1, source_target_pairs={{0,16},{2,18},{4,20},{6,22},{8,24},{10,26},{12,28},{14,30},{17,1},... | collective-permute-start | bytes 4718600 | tf_op jit(solution)/shard_map/ppermute | solution.py:911
  (129 other events, 2363.4 us)
